TPU v7x, 32 devices: a whole 2x2x4 slice. The times are simulated.
32 devices in a mesh: brick: 8 (over y, x, core), slab: 4 (over z).
Axes of the slice: x: 2, y: 2, z: 4, core: 2. Of those that a mesh axis runs over, the one named last changes fastest.
Arguments:
- positions: float32 [3, 4, 1536], P(None, 'slab', 'brick'), may hold values from -3 to 3
- types: int32 [4, 1536], P('slab', 'brick'), may hold values from 0 to 1, as said below
- neighbours: int32 [4, 1536, 64], P('slab', 'brick'), may hold values from 0 to 383
- neighbour_count: int32 [4, 1536], P('slab', 'brick'), may hold values from 32 to 64, as said below
- send_index: int32 [4, 1536], P('slab', 'brick'), may hold values from 0 to 191
- cell_x: int32 [4, 1536], P('slab', 'brick'), may hold values from 0 to 31, as said below
- cell_y: int32 [4, 1536], P('slab', 'brick'), may hold values from 0 to 63, as said below
- cell_z: int32 [4, 1536], P('slab', 'brick'), may hold values from 0 to 255, as said below
- spline_fraction: float32 [3, 4, 1536], P(None, 'slab', 'brick'), may hold values from 0 to 1
- embed_first: float32 [2, 25], replicated, may hold values from -4 to 4
- embed_second: float32 [25, 50], replicated, may hold values from -1.25 to 1.25
- embed_third: float32 [50, 100], replicated, may hold values from -0.875 to 0.875
- energy_in: float32 [1600, 240], replicated, may hold values from -0.3125 to 0.3125
- energy_hidden: float32 [2, 240, 240], replicated, may hold values from -0.375 to 0.375
- energy_out: float32 [240], replicated, may hold values from -0.375 to 0.375
- wannier_in: float32 [1600, 240], replicated, may hold values from -0.3125 to 0.3125
- wannier_hidden: float32 [2, 240, 240], replicated, may hold values from -0.375 to 0.375
- wannier_out: float32 [240], replicated, may hold values from -0.01953125 to 0.01953125
- charge_base: float32 [2], replicated, may hold values from -2 to 1
Outputs:
- atom_energy: float32 [4, 1536], P('slab', 'brick')
- potential: float32 [256, 256, 256], P('brick', 'slab')
Inputs may be any that keep to these rules, and one draw needn't show every extreme that they name: The first neighbour_count entries of an atom's neighbour row are live, the rest are padding; the first atom of every block has all 64 slots live. `types`: atoms 3k, 3k + 1 and 3k + 2 of a row form one water molecule: one oxygen and two hydrogens. `cell_x`: each hydrogen's first grid point along the first dimension is that of its molecule's oxygen or one further. `cell_y`: each hydrogen's first grid point along the second dimension is that of its molecule's oxygen or one further. `cell_z`: each hydrogen's first grid point along the third dimension is that of its molecule's oxygen or one further.
All inputs are finite; a program needn't handle non-finite values.
Results may differ from a plain program's by a relative error of at most 0.0003.
Values sent between devices are 32-bit elements; how exact they have to be, the bound alone decides.
No kernel may reach another device: no remote copies, remote signals or barrier semaphores. Data moves between devices by JAX's collectives and lax.ppermute only.
A program may use at most 128 MiB of HBM per device.

v0:
```python
import math

import jax
import jax.numpy as jnp
from jax import lax
from jax.sharding import PartitionSpec as P

NG = 256
AXIS = 16


HIGH = lax.Precision.HIGHEST


def with_halo(cells, sides, width):
    for axis, dim in sides:
        count = lax.axis_size(axis)
        head = lax.slice_in_dim(cells, 0, width, axis=dim)
        tail = lax.slice_in_dim(cells, cells.shape[dim] - width, cells.shape[dim], axis=dim)
        cells = jnp.concatenate(
            [
                lax.ppermute(tail, axis, [(i, (i + 1) % count) for i in range(count)]),
                cells,
                lax.ppermute(head, axis, [((i + 1) % count, i) for i in range(count)]),
            ],
            axis=dim,
        )
    return cells


def spline_weights(fraction):
    cubed = fraction * fraction * fraction
    square = fraction * fraction
    return jnp.stack(
        [
            (1.0 - fraction) * (1.0 - fraction) * (1.0 - fraction) / 6.0,
            (3.0 * cubed - 6.0 * square + 4.0) / 6.0,
            (-3.0 * cubed + 3.0 * square + 3.0 * fraction + 1.0) / 6.0,
            cubed / 6.0,
        ]
    )


def fitting(descriptor, weight_in, weight_hidden, weight_out):
    hidden = jnp.tanh(jnp.dot(descriptor, weight_in, precision=HIGH))
    for depth_index in range(weight_hidden.shape[0]):
        hidden = jnp.tanh(jnp.dot(hidden, weight_hidden[depth_index], precision=HIGH)) + hidden
    return jnp.dot(hidden, weight_out, precision=HIGH)


def atom_terms(
    extended,
    neighbour_rows,
    neighbour_total,
    embed_first,
    embed_second,
    embed_third,
    energy_in,
    energy_hidden,
    energy_out,
    wannier_in,
    wannier_hidden,
    wannier_out,
):
    atom_count, slots = neighbour_rows.shape
    ghost_rows = (extended.shape[1] - atom_count) // 2
    block_size = 64
    blocks = atom_count // block_size
    present = (jnp.arange(slots, dtype=jnp.int32)[None, :] < neighbour_total[:, None]).astype(
        jnp.float32
    )
    centre_ids = (ghost_rows + jnp.arange(atom_count, dtype=jnp.int32)).reshape(blocks, block_size)
    second_weight = embed_second.T
    third_weight = embed_third.T

    def one_block(pieces):
        centre_rows, rows_block, present_block = pieces
        centre_block = extended[:3, centre_rows]
        gathered = extended[:, rows_block]
        offsets = gathered[:3] - centre_block[:, :, None]
        smooth = present_block / (1.0 + jnp.sum(offsets * offsets, axis=0))
        environment = jnp.stack(
            [smooth, smooth * offsets[0], smooth * offsets[1], smooth * offsets[2]], axis=0
        )
        kind = gathered[3][None]
        mixing = (1.0 - kind) * embed_first[0][:, None, None] + kind * embed_first[1][:, None, None]
        first = jnp.tanh(smooth[None] * mixing).reshape(embed_first.shape[1], block_size * slots)
        second = jnp.tanh(jnp.dot(second_weight, first, precision=HIGH)) + jnp.concatenate(
            [first, first], axis=0
        )
        third = jnp.tanh(jnp.dot(third_weight, second, precision=HIGH)) + jnp.concatenate(
            [second, second], axis=0
        )
        third_blocks = third.reshape(third.shape[0], block_size, slots)
        moments = jnp.einsum("kan,can->akc", third_blocks, environment, precision=HIGH) / slots
        descriptor = jnp.einsum("amc,akc->amk", moments, moments[:, :AXIS], precision=HIGH).reshape(
            block_size, -1
        )
        return (
            fitting(descriptor, energy_in, energy_hidden, energy_out),
            fitting(descriptor, wannier_in, wannier_hidden, wannier_out),
        )

    energy_short, charge_shift = lax.map(
        one_block,
        (
            centre_ids,
            neighbour_rows.reshape(blocks, block_size, slots),
            present.reshape(blocks, block_size, slots),
        ),
    )
    return (energy_short.reshape(atom_count), charge_shift.reshape(atom_count))


def green_table(first, second, third, size):

    def folded(index):
        return jnp.where(index < size // 2, index, index - size).astype(jnp.float32) * (
            2.0 * math.pi / size
        )

    kappa_x = folded(first)[:, None, None]
    kappa_y = folded(second)[None, :, None]
    kappa_z = folded(third)[None, None, :]
    squared = kappa_x * kappa_x + kappa_y * kappa_y + kappa_z * kappa_z
    root = (
        (first[:, None, None] == 0) & (second[None, :, None] == 0) & (third[None, None, :] == 0)
    ).astype(jnp.float32)
    return (1.0 - root) * jnp.exp(-0.5 * squared) / (squared + root)


def dft_tables(size):
    index = jnp.arange(size, dtype=jnp.int32)
    phase = (index[:, None] * index[None, :] % size).astype(jnp.float32) * (2.0 * math.pi / size)
    return (jnp.cos(phase), jnp.sin(phase))


def along(values, table, axis_index):
    result = jnp.tensordot(values, table, axes=([axis_index], [0]), precision=HIGH)
    return jnp.moveaxis(result, -1, axis_index)


def complex_transform(paired, axis_index, cosine, sine, inverse):
    real_part = paired[0]
    imag_part = paired[1]
    inner = axis_index - 1
    real_cos = along(real_part, cosine, inner)
    real_sin = along(real_part, sine, inner)
    imag_cos = along(imag_part, cosine, inner)
    imag_sin = along(imag_part, sine, inner)
    if inverse:
        return jnp.stack([real_cos - imag_sin, imag_cos + real_sin])
    return jnp.stack([real_cos + imag_sin, imag_cos - real_sin])


def fold_windows(values, axis_index, block, count):
    front = jnp.moveaxis(values, axis_index, 0)
    rest = front.shape[1:]
    windows = front.reshape((count, block + 3) + rest)
    main_part = windows[:, :block]
    carried = jnp.roll(windows[:, block:], 1, axis=0)
    main_part = main_part.at[:, :3].add(carried)
    return jnp.moveaxis(main_part.reshape((count * block,) + rest), 0, axis_index)


def make_windows(values, axis_index, block, count):
    front = jnp.moveaxis(values, axis_index, 0)
    rest = front.shape[1:]
    pieces = front.reshape((count, block) + rest)
    trailing = jnp.roll(pieces, -1, axis=0)[:, :3]
    windows = jnp.concatenate([pieces, trailing], axis=1)
    return jnp.moveaxis(windows.reshape((count * (block + 3),) + rest), 0, axis_index)


def spread_matrix(start, weights, width, wrap_size):
    offsets = jnp.arange(4, dtype=jnp.int32)[:, None, None]
    target = start[None, :, None] + offsets
    if wrap_size > 0:
        target = target % wrap_size
    hits = (target == jnp.arange(width, dtype=jnp.int32)[None, None, :]).astype(jnp.float32)
    return jnp.sum(weights[:, :, None] * hits, axis=0)


def per_device(
    positions,
    types,
    neighbours,
    neighbour_count,
    send_index,
    cell_x,
    cell_y,
    cell_z,
    spline_fraction,
    embed_first,
    embed_second,
    embed_third,
    energy_in,
    energy_hidden,
    energy_out,
    wannier_in,
    wannier_hidden,
    wannier_out,
    charge_base,
):
    atom_count = types.shape[1]
    ghost_rows = send_index.shape[1] // 2
    kind_float = types[0].astype(jnp.float32)
    own_atoms = jnp.concatenate([positions[:, 0], kind_float[None]], axis=0)
    outgoing = own_atoms[:, send_index[0]]
    padded_ghosts = with_halo(outgoing, (("brick", 1),), ghost_rows)
    extended = jnp.concatenate(
        [padded_ghosts[:, :ghost_rows], own_atoms, padded_ghosts[:, 3 * ghost_rows :]], axis=1
    )
    energy_short, charge_shift = atom_terms(
        extended,
        neighbours[0],
        neighbour_count[0],
        embed_first,
        embed_second,
        embed_third,
        energy_in,
        energy_hidden,
        energy_out,
        wannier_in,
        wannier_hidden,
        wannier_out,
    )
    charge = (1.0 - kind_float) * charge_base[0] + kind_float * charge_base[1] + charge_shift
    count_x = lax.axis_size("brick")
    count_y = lax.axis_size("slab")
    block_x = NG // count_x
    block_y = NG // count_y
    wide_x = block_x + 3
    wide_y = block_y + 3
    spread_x = spread_matrix(cell_x[0], spline_weights(spline_fraction[0, 0]), wide_x, 0)
    spread_y = spread_matrix(cell_y[0], spline_weights(spline_fraction[1, 0]), wide_y, 0)
    spread_z = spread_matrix(cell_z[0], spline_weights(spline_fraction[2, 0]), NG, NG)
    spread_xy = (spread_x[:, :, None] * spread_y[:, None, :]).reshape(atom_count, wide_x * wide_y)
    charge_grid = jnp.einsum(
        "ap,az->pz", spread_xy, charge[:, None] * spread_z, precision=HIGH
    ).reshape(wide_x, wide_y, NG)
    cosine, sine = dft_tables(NG)
    scale = 1.0 / (NG * NG * NG)
    full_index = jnp.arange(NG, dtype=jnp.int32)
    paired = jnp.stack([along(charge_grid, cosine, 2), -along(charge_grid, sine, 2)])
    moved = lax.all_to_all(paired, "slab", split_axis=3, concat_axis=2, tiled=True)
    moved = complex_transform(fold_windows(moved, 2, block_y, count_y), 2, cosine, sine, False)
    moved = lax.all_to_all(moved, "brick", split_axis=2, concat_axis=1, tiled=True)
    moved = complex_transform(fold_windows(moved, 1, block_x, count_x), 1, cosine, sine, False)
    part_y = NG // count_x
    part_z = NG // count_y
    index_y = lax.axis_index("brick") * part_y + jnp.arange(part_y, dtype=jnp.int32)
    index_z = lax.axis_index("slab") * part_z + jnp.arange(part_z, dtype=jnp.int32)
    moved = moved * (green_table(full_index, index_y, index_z, NG) * scale)[None]
    moved = make_windows(complex_transform(moved, 1, cosine, sine, True), 1, block_x, count_x)
    moved = lax.all_to_all(moved, "brick", split_axis=1, concat_axis=2, tiled=True)
    moved = make_windows(complex_transform(moved, 2, cosine, sine, True), 2, block_y, count_y)
    moved = lax.all_to_all(moved, "slab", split_axis=2, concat_axis=3, tiled=True)
    potential_wide = along(moved[0], cosine, 2) - along(moved[1], sine, 2)
    sampled = jnp.einsum(
        "ap,pz->az", spread_xy, potential_wide.reshape(wide_x * wide_y, NG), precision=HIGH
    )
    potential_at = jnp.sum(sampled * spread_z, axis=1)
    atom_energy = energy_short + 0.5 * charge * potential_at
    return (atom_energy[None, :], potential_wide[:block_x, :block_y])


def solution(mesh):
    placed = (
        P(None, "slab", "brick"),
        P("slab", "brick"),
        P("slab", "brick", None),
        P("slab", "brick"),
        P("slab", "brick"),
        P("slab", "brick"),
        P("slab", "brick"),
        P("slab", "brick"),
        P(None, "slab", "brick"),
        P(),
        P(),
        P(),
        P(),
        P(),
        P(),
        P(),
        P(),
        P(),
        P(),
    )
    return jax.shard_map(
        per_device,
        mesh=mesh,
        in_specs=placed,
        out_specs=(P("slab", "brick"), P("brick", "slab", None)),
        check_vma=False,
    )
```

profile of v0, /device:TPU:0, one launch (start us, length us, event | category | flops | bytes accessed | tf_op | source)
XLA Modules:
  0.0 1673.3 jit_solution(6029884043219508250)
XLA Ops:
  3.6 3.4 collective-permute-start.1
  17.4 3.3 dot_general.107
  21.1 475.5 %while.17 = (s32[]{:T(128)}, f32[3,64]{1,0:T(4,128)S(1)}, f32[3,64]{1,0:T(4,128)S(1)}, f32[3,64,64]{2,0,1:T(4,128)S(1)}, s32[3,64,64]{2,1,0:T(8,128)S(1)}, /*ind...) while((s32[]{:T(128)}, f32[3,64]{1,0:T(4,128)S(1)}, ...), condition=%wide.region_2.3_spmd, body=%wide.region_0.2_spmd.sunk | while | flops 1100764416 | bytes 27716568 | solution.py:104
  21.2 10.8 gather_fusion
  33.1 129.2 %while.18 = (s32[]{:T(128)}, f32[4,384]{0,1:T(8,128)S(1)}, s32[64,2]{0,1:T(2,128)S(1)}, f32[64,3]{1,0:T(8,128)S(1)}, s32[]{:T(128)}, /*index=5*/s32[]{:T(128)}) while((s32[]{:T(128)}, f32[4,384]{0,1:T(8,128)S(1)}, s32[64,2]{0,1:T(2,128)S(1)}, f32[64,3]{1,0:T(8,128)S(1)}, s32[]{:T(128)}, /*index=5*/s32[]{:T(128)}) %tuple.87), condition=%wide.while_cond.2, body=%wide.while_body.2.sunk | while | flops 2 | bytes 173 | solution.py:78
  179.6 10.8 gather_fusion
  191.4 129.2 %while.18 = (s32[]{:T(128)}, f32[4,384]{0,1:T(8,128)S(1)}, s32[64,2]{0,1:T(2,128)S(1)}, f32[64,3]{1,0:T(8,128)S(1)}, s32[]{:T(128)}, /*index=5*/s32[]{:T(128)}) while((s32[]{:T(128)}, f32[4,384]{0,1:T(8,128)S(1)}, s32[64,2]{0,1:T(2,128)S(1)}, f32[64,3]{1,0:T(8,128)S(1)}, s32[]{:T(128)}, /*index=5*/s32[]{:T(128)}) %tuple.87), condition=%wide.while_cond.2, body=%wide.while_body.2.sunk | while | flops 2 | bytes 173 | solution.py:78
  337.9 10.8 gather_fusion
  349.8 129.2 %while.18 = (s32[]{:T(128)}, f32[4,384]{0,1:T(8,128)S(1)}, s32[64,2]{0,1:T(2,128)S(1)}, f32[64,3]{1,0:T(8,128)S(1)}, s32[]{:T(128)}, /*index=5*/s32[]{:T(128)}) while((s32[]{:T(128)}, f32[4,384]{0,1:T(8,128)S(1)}, s32[64,2]{0,1:T(2,128)S(1)}, f32[64,3]{1,0:T(8,128)S(1)}, s32[]{:T(128)}, /*index=5*/s32[]{:T(128)}) %tuple.87), condition=%wide.while_cond.2, body=%wide.while_body.2.sunk | while | flops 2 | bytes 173 | solution.py:78
  496.7 4.1 fusion.60
  500.8 3.3 negate_bitcast_fusion
  510.0 11.9 copy.186
  521.9 208.2 %all_to_all.66 = f32[2,35,67,256]{2,0,1,3:T(2,128)} all-to-all(f32[2,35,67,256]{2,0,1,3:T(2,128)} %copy.186), channel_id=1, replica_groups=mesh['brick'=8,'slab'=4] {'slab'}, dimensions={3} | all-to-all | bytes 9605120 | tf_op jit(solution)/shard_map/all_to_all | solution.py:246
  730.1 13.0 copy.230
  743.1 10.2 all_to_all.51
  753.4 10.7 reshape.795
  764.1 12.0 slice.287
  776.0 8.4 slice.286
  784.4 7.2 copy.225
  791.6 7.2 copy.227
  800.3 6.2 copy.192
  806.6 133.6 %scatter-add.6 = f32[4,64,2,35,64]{1,0,4,3,2:T(4,128)} dynamic-update-slice(f32[4,64,2,35,64]{1,0,4,3,2:T(4,128)} %bitcast.417, f32[4,3,2,35,64]{1,0,4,3,2:T(4,128)} %copy.192, s32[]{:T(128)} %constant.152.clone.1, s32[]{:T(128)} %constant.152.clone.1, s32[]{:T(128)} %constant.152.clone.1, s32[]{:T(128)} %constant.152.clone.1, s32[]{:T(128)} %constant.152.clone.1) | dynamic-update-slice | bytes 430084 | tf_op jit(solution)/shard_map/scatter-add | solution.py:162
  940.2 9.8 reshape.796
  950.0 4.8 fusion.28
  966.9 11.7 copy.193
  978.5 12.7 reshape.891
  991.2 4.6 all-to-all-start.1
  998.3 50.9 %all-to-all-done.1 = f32[8,1,143360]{2,1,0:T(1,128)} async-done(((f32[8,1,143360]{2,1,0:T(1,128)}), f32[8,1,143360]{2,1,0:T(1,128)}, u32[]{:S(2)}, u32[]{:S(2)}) %all-to-all-start.1) | async-done | bytes 4587552 | tf_op jit(solution)/shard_map/all_to_all | solution.py:248
  1049.7 35.3 %reduce.21 = f32[8,143360]{1,0:T(8,128)} reduce(f32[8,1,143360]{2,1,0:T(1,128)} %all-to-all-done.1, f32[]{:T(128)} %broadcast.826), dimensions={1}, to_apply=%all_to_all.52.reduce_sub_computation | reduce | bytes 9175044 | tf_op jit(solution)/shard_map/all_to_all | solution.py:248
  1084.9 12.5 reshape.892
  1097.4 4.8 copy.194
  1110.5 8.2 copy.197
  1154.0 9.1 copy.198
  1164.1 7.4 copy.199
  1171.4 9.4 fusion.27
  1180.8 10.4 reshape.893
  1191.2 57.8 %all_to_all.67 = f32[8,1,143360]{2,1,0:T(1,128)} all-to-all(f32[8,1,143360]{2,1,0:T(1,128)} %reshape.893), channel_id=1, replica_groups=mesh['brick'=8,'slab'=4] {'brick'}, dimensions={0} | all-to-all | bytes 9175040 | tf_op jit(solution)/shard_map/all_to_all | solution.py:256
  1248.9 35.6 %reduce.22 = f32[8,143360]{1,0:T(8,128)} reduce(f32[8,1,143360]{2,1,0:T(1,128)} %all_to_all.67, f32[]{:T(128)} %broadcast.826), dimensions={1}, to_apply=%all_to_all.56.reduce_sub_computation | reduce | bytes 9175044 | tf_op jit(solution)/shard_map/all_to_all | solution.py:256
  1284.6 9.4 reshape.894
  1294.0 4.7 copy.201
  1300.5 8.3 fusion.50
  1309.3 8.3 fusion.52
  1317.6 8.5 add_bitcast_fusion
  1326.1 8.3 subtract_bitcast_fusion
  1337.2 3.3 slice.302
  1340.5 8.8 reshape.801
  1351.3 6.6 copy.208
  1359.2 6.3 copy.210
  1365.5 13.2 pad_maximum_fusion.1
  1378.7 23.5 %copy.211 = f32[4,67,2,35,64]{4,2,3,1,0:T(2,128)} copy(f32[4,67,2,35,64]{1,0,4,3,2:T(4,128)} %pad_maximum_fusion.1) | data formatting | bytes 9605120 | tf_op jit(solution)/shard_map/concatenate | solution.py:171
  1402.2 12.8 reshape.895
  1415.0 5.1 all-to-all-start.3
  1420.3 106.1 %all-to-all-done.3 = f32[4,1,300160]{2,1,0:T(1,128)} async-done(((f32[4,1,300160]{2,1,0:T(1,128)}), f32[4,1,300160]{2,1,0:T(1,128)}, u32[]{:S(2)}, u32[]{:S(2)}) %all-to-all-start.3) | async-done | bytes 4802592 | tf_op jit(solution)/shard_map/all_to_all | solution.py:258
  1526.4 54.4 %reduce.23 = f32[4,300160]{1,0:T(4,128)} reduce(f32[4,1,300160]{2,1,0:T(1,128)} %all-to-all-done.3, f32[]{:T(128)} %broadcast.826), dimensions={1}, to_apply=%all_to_all.59.reduce_sub_computation | reduce | bytes 9605124 | tf_op jit(solution)/shard_map/all_to_all | solution.py:258
  1580.8 18.2 %reshape.896 = f32[268,35,2,64]{3,2,1,0:T(2,128)} reshape(f32[4,300160]{1,0:T(4,128)} %reduce.23) | data formatting | bytes 9605120
  1599.0 22.8 %copy.223 = f32[2,35,4,67,64]{3,2,4,1,0:T(4,128)} copy(f32[2,35,4,67,64]{4,0,1,3,2:T(2,128)} %bitcast.432) | data formatting | bytes 9605120 | tf_op jit(solution)/shard_map/all_to_all | solution.py:258
  1621.8 8.4 fusion.200
  1630.3 7.5 copy.213
  1637.7 5.2 squeeze.94
  1642.9 4.6 fusion.48
  1647.5 7.5 copy.214
  1655.0 5.0 squeeze.95
  1660.0 5.2 convolution_subtract_fusion
  1665.2 4.5 fusion.37
  (1042 shorter events, 533.2 us)
Async XLA Ops:
  0.6 13.5 copy-start.23
  0.6 14.7 copy-start.18
  0.7 14.8 copy-start.19
  3.6 17.1 %collective-permute-start.1 = (f32[4,96]{0,1:T(8,128)S(1)}, f32[4,96]{0,1:T(8,128)S(1)}, u32[]{:S(2)}, u32[]{:S(2)}) collective-permute-start(f32[4,96]{0,1:T(8,128)S(1)} %get-tuple-element.233), channel_id=1, source_target_pairs={{4,0},{8,4},{12,8},{16,12},{20,16},{24,20},{28,24},{0,28},{5,1},{9... | collective-permute-start | bytes 4616 | tf_op jit(solution)/shard_map/ppermute | solution.py:24
  7.0 13.7 collective-permute-start
  13.6 483.1 %copy-start.9 = (f32[192,256]{1,0:T(8,128)}, f32[192,256]{1,0:T(8,128)S(1)}, u32[]{:S(2)}) copy-start(f32[192,256]{1,0:T(8,128)S(1)} %select_reduce_fusion) | copy-start | bytes 589828
  13.8 3.5 copy-start.14
  13.9 3.4 copy-start.16
  17.4 3.7 copy-start.13
  17.4 3.7 copy-start.20
  17.4 3.7 copy-start.21
  17.4 3.7 copy-start.22
  21.1 143.0 %copy-start.11 = (f32[3,64,64]{2,0,1:T(4,128)}, f32[3,64,64]{2,0,1:T(4,128)S(1)}, u32[]{:S(2)}) copy-start(f32[3,64,64]{2,0,1:T(4,128)S(1)} %get-tuple-element.472) | copy-start | bytes 147460 | tf_op jit(solution)/shard_map/while
  171.8 1.6 copy-start.3
  173.4 1.6 copy-start.5
  175.0 3.7 copy-start.6
  175.0 4.4 copy-start.12
  179.5 143.0 %copy-start.11 = (f32[3,64,64]{2,0,1:T(4,128)}, f32[3,64,64]{2,0,1:T(4,128)S(1)}, u32[]{:S(2)}) copy-start(f32[3,64,64]{2,0,1:T(4,128)S(1)} %get-tuple-element.472) | copy-start | bytes 147460 | tf_op jit(solution)/shard_map/while
  330.2 1.6 copy-start.3
  331.7 1.6 copy-start.5
  333.3 3.7 copy-start.6
  333.3 4.4 copy-start.12
  337.8 143.0 %copy-start.11 = (f32[3,64,64]{2,0,1:T(4,128)}, f32[3,64,64]{2,0,1:T(4,128)S(1)}, u32[]{:S(2)}) copy-start(f32[3,64,64]{2,0,1:T(4,128)S(1)} %get-tuple-element.472) | copy-start | bytes 147460 | tf_op jit(solution)/shard_map/while
  488.5 1.6 copy-start.3
  490.1 1.6 copy-start.5
  491.7 3.7 copy-start.6
  491.7 4.4 copy-start.12
  496.6 4.2 copy-start.25
  496.6 4.2 copy-start.27
  950.0 4.8 copy-start.2
  991.2 57.9 %all-to-all-start.1 = ((f32[8,1,143360]{2,1,0:T(1,128)}), f32[8,1,143360]{2,1,0:T(1,128)}, u32[]{:S(2)}, u32[]{:S(2)}) async-start(f32[8,1,143360]{2,1,0:T(1,128)} %reshape.891), calls=%async_computation.1 | async-start | bytes 9175040 | tf_op jit(solution)/shard_map/all_to_all | solution.py:248
  1107.3 3.2 copy-start.4
  1133.1 1.6 copy-start.8
  1148.9 2.0 copy-start.1
  1335.0 2.2 copy-start
  1351.3 6.6 copy-start.7
  1415.0 5.1 copy-start.26
  1415.0 5.2 copy-start.28
  1415.0 111.4 %all-to-all-start.3 = ((f32[4,1,300160]{2,1,0:T(1,128)}), f32[4,1,300160]{2,1,0:T(1,128)}, u32[]{:S(2)}, u32[]{:S(2)}) async-start(f32[4,1,300160]{2,1,0:T(1,128)} %reshape.895), calls=%async_computation.3 | async-start | bytes 9605120 | tf_op jit(solution)/shard_map/all_to_all | solution.py:258
  1660.0 5.2 copy-start.10
  1660.0 5.2 copy-start.15
  1660.0 5.2 copy-start.17
  1669.7 1.6 copy-start.24
where the time goes:
time: 1690 us; the launch traced here: 1670 us
  local copies, waits for them, and re-layouts  925 us (55%)
  blocking collectives  266 us (16%)
  other arithmetic  175 us (10%)
  waiting for transfers between devices  157 us (9%)
  matrix products  133 us (8%)
    gather x768, local copies, waits for them, and re-layouts  387 us
    all_to_all x1, blocking collectives, per_device(): lax.all_to_all(paired, 'slab', split_axis=3, concat_axis=2, tiled=True)  208 us
    scatter-add x1, local copies, waits for them, and re-layouts, fold_windows(): main_part = main_part.at[:, :3].add(carried)  134 us
    all_to_all x1, waiting for transfers between devices, per_device(): lax.all_to_all(moved, 'slab', split_axis=2, concat_axis=3, tiled=True)  106 us
    unnamed x61, local copies, waits for them, and re-layouts  101 us
    dot_general x12, matrix products, along(): jnp.tensordot(values, table, axes=([axis_index], [0]), precision=HIGH)  63.6 us
    all_to_all x1, blocking collectives, per_device(): lax.all_to_all(moved, 'brick', split_axis=1, concat_axis=2, tiled=True)  57.8 us
    all_to_all x1, other arithmetic, per_device(): lax.all_to_all(moved, 'slab', split_axis=2, concat_axis=3, tiled=True)  54.4 us
  transfers between devices with their start and end apart: 4, of which 2 were waited for; matrix products, arithmetic and copies ran while one was open for 1% of the time, Pallas kernels for 0%

commit v1 on v0

--- a/solution.py
+++ b/solution.py
@@ -1,8 +1,13 @@
+import functools
 import math
 
 import jax
 import jax.numpy as jnp
+import ml_dtypes
+import numpy as np
 from jax import lax
+from jax.experimental import pallas as pl
+from jax.experimental.pallas import tpu as pltpu
 from jax.sharding import PartitionSpec as P
 
 NG = 256
@@ -181,7 +186,7 @@
     return jnp.sum(weights[:, :, None] * hits, axis=0)
 
 
-def per_device(
+def per_device_general(
     positions,
     types,
     neighbours,
@@ -265,6 +270,807 @@
     return (atom_energy[None, :], potential_wide[:block_x, :block_y])
 
 
+def split(values):
+    high = values.astype(jnp.bfloat16)
+    low = (values - high.astype(jnp.float32)).astype(jnp.bfloat16)
+    return high, low
+
+
+def multiply(left, right, dims):
+    return lax.dot_general(left, right, (dims, ((), ())), preferred_element_type=jnp.float32)
+
+
+def triple(left, right, dims=((1,), (0,))):
+    return (
+        multiply(left[0], right[0], dims)
+        + multiply(left[0], right[1], dims)
+        + multiply(left[1], right[0], dims)
+    )
+
+
+LANES = ((1,), (1,))
+
+
+def lane_pick(table, index):
+    return jnp.take_along_axis(table, index, axis=1, mode="promise_in_bounds")
+
+
+def full_spec(count):
+    return [pl.BlockSpec(memory_space=pltpu.VMEM)] * count
+
+
+def collect_kernel(
+    base_ref,
+    positions_ref,
+    types_ref,
+    count_ref,
+    send_ref,
+    cell_x_ref,
+    cell_y_ref,
+    cell_z_ref,
+    fraction_ref,
+    own_ref,
+    outgoing_ref,
+    static_ref,
+):
+    atoms = types_ref.shape[1]
+    own_ref[...] = jnp.zeros_like(own_ref)
+    static = jnp.concatenate(
+        [
+            (cell_x_ref[...] + base_ref[0]).astype(jnp.float32),
+            cell_y_ref[...].astype(jnp.float32),
+            cell_z_ref[...].astype(jnp.float32),
+        ]
+        + [fraction_ref[axis] for axis in range(3)]
+        + [jnp.zeros((2, atoms), jnp.float32)],
+        axis=0,
+    )
+    for copy in range(static_ref.shape[0]):
+        static_ref[copy] = static
+    for axis in range(3):
+        own_ref[axis : axis + 1, 0:atoms] = positions_ref[axis]
+    own_ref[3:4, 0:atoms] = types_ref[...].astype(jnp.float32)
+    own_ref[4:5, 0:atoms] = count_ref[...].astype(jnp.float32)
+    own_ref[5:6, 0:atoms] = send_ref[...].astype(jnp.float32)
+    for chunk in range(2):
+        lanes = slice(128 * chunk, 128 * chunk + 128)
+        wanted = jnp.broadcast_to(own_ref[5:6, lanes], (8, 128)).astype(jnp.int32)
+        within = wanted & 127
+        outgoing_ref[:, lanes] = jnp.where(
+            wanted < 128,
+            lane_pick(own_ref[:, 0:128], within),
+            lane_pick(own_ref[:, 128:256], within),
+        )
+
+
+def collect(
+    copies, base, positions, types, counts, send_index, cell_x, cell_y, cell_z, fraction
+):
+    atoms = types.shape[1]
+    return pl.pallas_call(
+        collect_kernel,
+        out_shape=[
+            jax.ShapeDtypeStruct((8, 256), jnp.float32),
+            jax.ShapeDtypeStruct((8, 256), jnp.float32),
+            jax.ShapeDtypeStruct((copies, 8, atoms), jnp.float32),
+        ],
+        in_specs=[pl.BlockSpec(memory_space=pltpu.SMEM)] + full_spec(8),
+        out_specs=full_spec(3),
+        name="collect_atoms",
+    )(base, positions, types, counts, send_index, cell_x, cell_y, cell_z, fraction)
+
+
+def fitting_rows(descriptor_ref, weight_in_ref, weight_hidden_ref, weight_out_ref):
+    depth = weight_in_ref.shape[1]
+    first = depth // 256 * 256
+    hidden = triple(
+        split(descriptor_ref[:, 0:first]), split(weight_in_ref[:, 0:first]), LANES
+    )
+    if first < depth:
+        hidden = hidden + triple(
+            split(descriptor_ref[:, first:depth]), split(weight_in_ref[:, first:depth]), LANES
+        )
+    hidden = jnp.tanh(hidden)
+    for layer in range(weight_hidden_ref.shape[0]):
+        hidden = jnp.tanh(triple(split(hidden), split(weight_hidden_ref[layer]))) + hidden
+    width = hidden.shape[1]
+    out_weight = jnp.broadcast_to(weight_out_ref[...], (8, width))
+    return triple(split(out_weight), split(hidden), LANES)
+
+
+def natural_order(rows):
+    atoms = rows.shape[1]
+    padded = jnp.concatenate([rows, jnp.zeros((8, 256 - atoms), jnp.float32)], axis=1)
+    pieces = []
+    for chunk in range(2):
+        atom = 128 * chunk + lax.broadcasted_iota(jnp.int32, (8, 128), 1)
+        late = atom >= atoms // 2
+        within = jnp.where(late, atom - atoms // 2, atom)
+        place = 8 * (within >> 2) + (within & 3) + jnp.where(late, 4, 0)
+        place = jnp.minimum(place, 255)
+        pieces.append(
+            jnp.where(
+                place < 128,
+                lane_pick(padded[:, 0:128], place & 127),
+                lane_pick(padded[:, 128:256], place & 127),
+            )
+        )
+    return jnp.concatenate(pieces, axis=1)[0:1, 0:atoms]
+
+
+def network_kernel(
+    ghosts,
+    base_ref,
+    own_ref,
+    lower_ref,
+    upper_ref,
+    slots_ref,
+    types_ref,
+    first_ref,
+    second_ref,
+    third_ref,
+    spot_ref,
+    weight_in_hbm,
+    weight_hidden_hbm,
+    weight_out_ref,
+    descriptor_ref,
+    charge_ref,
+    copies_ref,
+    environment_ref,
+    kind_ref,
+    moments_ref,
+    padded_ref,
+    weight_in_ref,
+    weight_hidden_ref,
+    semaphores,
+):
+    fetches = [
+        pltpu.make_async_copy(weight_in_hbm, weight_in_ref, semaphores.at[0]),
+        pltpu.make_async_copy(weight_hidden_hbm, weight_hidden_ref, semaphores.at[1]),
+    ]
+    for fetch in fetches:
+        fetch.start()
+    slots, atoms = slots_ref.shape
+    rows = atoms // 2
+    lane = lax.broadcasted_iota(jnp.int32, (8, 128), 1)
+    sub = lax.broadcasted_iota(jnp.int32, (8, 128), 0)
+
+    width = first_ref.shape[1]
+    padded_ref[...] = jnp.zeros_like(padded_ref)
+    padded_ref[0, 0:2, 0:width] = first_ref[...]
+    for column in range(2):
+        padded_ref[1, 0:width, 32 * column : 32 * column + width] = second_ref[
+            :, width * column : width * (column + 1)
+        ]
+    for row in range(2):
+        for column in range(4):
+            padded_ref[2, 32 * row : 32 * row + width, 32 * column : 32 * column + width] = (
+                third_ref[
+                    width * row : width * (row + 1), width * column : width * (column + 1)
+                ]
+            )
+    first_table = padded_ref[0].T
+    embed_zero = jnp.broadcast_to(first_table[0:32, 0:1], (32, 128))
+    embed_one = jnp.broadcast_to(first_table[0:32, 1:2], (32, 128))
+    second_high, second_low = split(padded_ref[1].T[0:64, 0:32])
+    second_weight = jnp.concatenate([second_high, second_high, second_low], axis=1)
+    third_high, third_low = split(padded_ref[2].T[:, 0:64])
+    third_weight = jnp.concatenate([third_high, third_high, third_low], axis=1)
+
+    def spread(ref, field, chunk):
+        return jnp.broadcast_to(ref[field : field + 1, 128 * chunk : 128 * chunk + 128], (8, 128))
+
+    own = [[spread(own_ref, field, chunk) for chunk in range(2)] for field in range(5)]
+    lower = [[spread(lower_ref, field, chunk) for chunk in range(2)] for field in range(4)]
+    upper = [spread(upper_ref, field, 0) for field in range(4)]
+
+    def pick_two(tables, index):
+        within = index & 127
+        return jnp.where(index < 128, lane_pick(tables[0], within), lane_pick(tables[1], within))
+
+    pairs = jnp.concatenate([slots_ref[:, 0:rows], slots_ref[:, rows:atoms]], axis=0).T
+    for tile in range(rows // 8):
+        band = slice(8 * tile, 8 * tile + 8)
+        index = pairs[band, :]
+        centre = 8 * tile + sub + jnp.where(lane < 64, 0, rows)
+        from_own = jnp.clip(index - ghosts, 0, atoms - 1)
+        from_lower = jnp.minimum(index + (atoms - ghosts), 255)
+        from_upper = jnp.clip(index - (ghosts + atoms), 0, 127)
+
+        def neighbour(field):
+            below = pick_two(lower[field], from_lower)
+            inside = pick_two(own[field], from_own)
+            above = lane_pick(upper[field], from_upper)
+            return jnp.where(
+                index < ghosts, below, jnp.where(index < ghosts + atoms, inside, above)
+            )
+
+        offsets = [neighbour(field) - pick_two(own[field], centre) for field in range(3)]
+        live = pick_two(own[4], centre)
+        present = jnp.where((lane & 63).astype(jnp.float32) < live, 1.0, 0.0)
+        smooth = present / (
+            1.0 + (offsets[0] * offsets[0] + offsets[1] * offsets[1] + offsets[2] * offsets[2])
+        )
+        environment_ref[0, band, :] = smooth
+        for field in range(3):
+            environment_ref[1 + field, band, :] = smooth * offsets[field]
+        kind_ref[band, :] = neighbour(3)
+
+    group = 8
+
+    def stacked(values):
+        high, low = split(values)
+        return jnp.concatenate([high, low, high], axis=0)
+
+    def one_group(start):
+        pieces = []
+        for row in range(group):
+            smooth = jnp.broadcast_to(environment_ref[0, pl.ds(start + row, 1), :], (32, 128))
+            kind = jnp.broadcast_to(kind_ref[pl.ds(start + row, 1), :], (32, 128))
+            pieces.append(
+                jnp.tanh(smooth * ((1.0 - kind) * embed_zero + kind * embed_one))
+            )
+        first = jnp.concatenate(pieces, axis=1)
+        second = jnp.tanh(multiply(second_weight, stacked(first), ((1,), (0,))))
+        second = second + jnp.concatenate([first, first], axis=0)
+        third = jnp.tanh(multiply(third_weight, stacked(second), ((1,), (0,))))
+        third = third + jnp.concatenate([second, second], axis=0)
+        third_pair = split(third)
+        for half in range(group // 4):
+            columns = slice(512 * half, 512 * half + 512)
+            bands = []
+            for part in range(4):
+                bands.append(
+                    jnp.concatenate(
+                        [
+                            jnp.where(
+                                sub == row + jnp.where(lane < 64, 0, 4),
+                                jnp.broadcast_to(
+                                    environment_ref[part, pl.ds(start + 4 * half + row, 1), :],
+                                    (8, 128),
+                                ),
+                                0.0,
+                            )
+                            for row in range(4)
+                        ],
+                        axis=1,
+                    )
+                )
+            environment = split(jnp.concatenate(bands, axis=0))
+            both = multiply(
+                jnp.concatenate(environment, axis=0), third_pair[0][:, columns], LANES
+            )
+            sums = both[0:32] + both[32:64]
+            sums = sums + multiply(environment[0], third_pair[1][:, columns], LANES)
+            sums = sums * (1.0 / slots)
+            for part in range(4):
+                moments_ref[part, pl.ds(2 * start + 8 * half, 8), :] = sums[
+                    8 * part : 8 * part + 8
+                ]
+
+    def body(step, carry):
+        one_group(pl.multiple_of(step * 2 * group, 2 * group))
+        one_group(pl.multiple_of(step * 2 * group + group, group))
+        return carry
+
+    lax.fori_loop(0, rows // (2 * group), body, 0)
+
+    chunks = (descriptor_ref.shape[1] + 127) // 128
+    last = descriptor_ref.shape[1] - 128 * (chunks - 1)
+
+    def describe(step, carry):
+        band = pl.ds(pl.multiple_of(step * 8, 8), 8)
+        moments = [moments_ref[part, band, :] for part in range(4)]
+        axis_part = [lane_pick(moments[part], lane & 15) for part in range(4)]
+        for chunk in range(chunks):
+            spot = jnp.broadcast_to(spot_ref[chunk : chunk + 1, :], (8, 128))
+            total = lane_pick(moments[0], spot) * axis_part[0]
+            for part in range(1, 4):
+                total = total + lane_pick(moments[part], spot) * axis_part[part]
+            if chunk < chunks - 1:
+                descriptor_ref[band, 128 * chunk : 128 * chunk + 128] = total
+            else:
+                descriptor_ref[band, 128 * chunk : 128 * chunk + last] = total[:, 0:last]
+        return carry
+
+    lax.fori_loop(0, atoms // 8, describe, 0)
+
+    for fetch in fetches:
+        fetch.wait()
+    shift = fitting_rows(descriptor_ref, weight_in_ref, weight_hidden_ref, weight_out_ref)
+    kind = types_ref[...].astype(jnp.float32)
+    charge = (1.0 - kind) * base_ref[0] + kind * base_ref[1] + natural_order(shift)
+    charge_ref[...] = charge
+    for copy in range(copies_ref.shape[0]):
+        copies_ref[copy] = charge
+
+
+def spot_table(embed, desc):
+    column = np.arange(desc) // AXIS
+    quarter = embed // 4
+    place = 32 * (column // quarter) + column % quarter
+    chunks = (desc + 127) // 128
+    table = np.zeros((chunks * 128,), np.int32)
+    table[:desc] = place
+    padded = np.zeros(((chunks + 7) // 8 * 8, 128), np.int32)
+    padded[:chunks] = table.reshape(chunks, 128)
+    return padded
+
+
+def networks(
+    copies,
+    ghosts,
+    charge_base,
+    own,
+    lower,
+    upper,
+    neighbours,
+    types,
+    embed_first,
+    embed_second,
+    embed_third,
+    weight_in,
+    weight_hidden,
+    weight_out,
+):
+    atoms = types.shape[1]
+    desc, width = weight_in.shape
+    spots = jnp.asarray(spot_table(embed_third.shape[1], desc))
+    anywhere = pl.BlockSpec(memory_space=pl.ANY)
+    return pl.pallas_call(
+        functools.partial(network_kernel, ghosts),
+        out_shape=[
+            jax.ShapeDtypeStruct((atoms, desc), jnp.float32),
+            jax.ShapeDtypeStruct((1, atoms), jnp.float32),
+            jax.ShapeDtypeStruct((copies, 1, atoms), jnp.float32),
+        ],
+        in_specs=[pl.BlockSpec(memory_space=pltpu.SMEM)]
+        + full_spec(9)
+        + [anywhere, anywhere]
+        + full_spec(1),
+        out_specs=full_spec(3),
+        scratch_shapes=[
+            pltpu.VMEM((4, atoms // 2, 128), jnp.float32),
+            pltpu.VMEM((atoms // 2, 128), jnp.float32),
+            pltpu.VMEM((4, atoms, 128), jnp.float32),
+            pltpu.VMEM((3, 128, 128), jnp.float32),
+            pltpu.VMEM((width, desc), jnp.float32),
+            pltpu.VMEM(weight_hidden.shape, jnp.float32),
+            pltpu.SemaphoreType.DMA((2,)),
+        ],
+        compiler_params=pltpu.CompilerParams(vmem_limit_bytes=32 * 2**20),
+        name="networks",
+    )(
+        charge_base,
+        own,
+        lower,
+        upper,
+        neighbours[0].T,
+        types,
+        embed_first,
+        embed_second,
+        embed_third,
+        spots,
+        weight_in.T,
+        weight_hidden,
+        weight_out.reshape(1, -1),
+    )
+
+
+def energy_kernel(descriptor_ref, weight_in_ref, weight_hidden_ref, weight_out_ref, energy_ref):
+    energy_ref[...] = natural_order(
+        fitting_rows(descriptor_ref, weight_in_ref, weight_hidden_ref, weight_out_ref)
+    )
+
+
+def energies(descriptor, weight_in, weight_hidden, weight_out):
+    atoms, desc = descriptor.shape
+    width = weight_in.shape[1]
+    return pl.pallas_call(
+        energy_kernel,
+        out_shape=jax.ShapeDtypeStruct((1, atoms), jnp.float32),
+        in_specs=full_spec(4),
+        out_specs=pl.BlockSpec(memory_space=pltpu.VMEM),
+        compiler_params=pltpu.CompilerParams(vmem_limit_bytes=32 * 2**20),
+        cost_estimate=pl.CostEstimate(
+            flops=6 * atoms * desc * width, bytes_accessed=4 * desc * width, transcendentals=0
+        ),
+        name="energies",
+    )(descriptor, weight_in.T, weight_hidden, weight_out.reshape(1, -1))
+
+
+def weight_rows(fraction):
+    square = fraction * fraction
+    cubed = square * fraction
+    rest = 1.0 - fraction
+    return [
+        rest * rest * rest / 6.0,
+        (3.0 * cubed - 6.0 * square + 4.0) / 6.0,
+        (-3.0 * cubed + 3.0 * square + 3.0 * fraction + 1.0) / 6.0,
+        cubed / 6.0,
+    ]
+
+
+def placed_weights(distance, weights):
+    shape = distance.shape
+    result = jnp.zeros(shape, jnp.float32)
+    for step in range(4):
+        result = jnp.where(
+            distance == step, jnp.broadcast_to(weights[step], shape), result
+        )
+    return result
+
+
+def atom_factors(fields, waves_ref, cosine_ref, window, scale):
+    row = lambda field: fields[field : field + 1, :]
+    atoms = fields.shape[1]
+    start_x = row(0).astype(jnp.int32)
+    start_y = row(1).astype(jnp.int32)
+    start_z = row(2).astype(jnp.int32)
+    along_x = weight_rows(row(3))
+    along_y = weight_rows(row(4))
+    along_z = weight_rows(row(5))
+    if scale is not None:
+        along_x = [weight * scale for weight in along_x]
+    rows_x = lax.broadcasted_iota(jnp.int32, (NG, atoms), 0)
+    table_x = placed_weights((rows_x - start_x) & (NG - 1), along_x)
+    rows_y = lax.broadcasted_iota(jnp.int32, (window, atoms), 0)
+    table_y = placed_weights(rows_y - start_y, along_y)
+    parts = waves_ref.shape[0]
+    cosine = jnp.broadcast_to(cosine_ref[...], (parts, 128))
+    wave = jnp.broadcast_to(waves_ref[:, 0:1], (parts, 128))
+    shift = jnp.broadcast_to(waves_ref[:, 1:2], (parts, 128))
+    pieces = []
+    for chunk in range(atoms // 128):
+        lanes = slice(128 * chunk, 128 * chunk + 128)
+        total = jnp.zeros((parts, 128), jnp.float32)
+        for step in range(4):
+            place = jnp.broadcast_to(start_z[:, lanes] + step, (parts, 128))
+            phase = (wave * place + shift) & (NG - 1)
+            value = lane_pick(cosine, phase & 127)
+            value = jnp.where(phase < 128, value, -value)
+            total = total + value * jnp.broadcast_to(along_z[step][:, lanes], (parts, 128))
+        pieces.append(total)
+    table_z = jnp.concatenate(pieces, axis=1)
+    table_yz = jnp.concatenate(
+        [table_y * table_z[part : part + 1, :] for part in range(parts)], axis=0
+    )
+    return table_x, table_yz
+
+
+def wave_of(index):
+    return jnp.where(index <= NG // 2, index, index - NG // 2)
+
+
+def solve_kernel(
+    block_x,
+    block_y,
+    window,
+    kappa_ref,
+    static_ref,
+    charge_ref,
+    waves_ref,
+    cosine_ref,
+    tables_hbm,
+    sent_ref,
+    half_ref,
+    atoms_ref,
+    grid_ref,
+    tables_ref,
+    semaphore,
+):
+    slabs = atoms_ref.shape[0]
+    parts = waves_ref.shape[0]
+    bricks = NG // block_x
+    block = static_ref.shape[2]
+    step = pl.program_id(0)
+
+    @pl.when(step == 0)
+    def _():
+        fetch = pltpu.make_async_copy(tables_hbm, tables_ref, semaphore)
+        fetch.start()
+        for slab in range(slabs):
+            for brick in range(bricks):
+                lanes = slice(block * brick, block * (brick + 1))
+                atoms_ref[slab, :, lanes] = static_ref[slab * bricks + brick]
+                atoms_ref[slab, 6:7, lanes] = charge_ref[slab * bricks + brick]
+        grid_ref[...] = jnp.zeros_like(grid_ref)
+        for slab in range(slabs):
+            fields = atoms_ref[slab]
+            table_x, table_yz = atom_factors(
+                fields, waves_ref, cosine_ref, window, fields[6:7, :]
+            )
+            spread = triple(split(table_yz), split(table_x), LANES)
+            rows = slice(slab * block_y, slab * block_y + window)
+            for part in range(parts):
+                grid_ref[part, rows, :] += spread[part * window : part * window + window]
+        extra = window - block_y
+        for part in range(parts):
+            grid_ref[part, 0:extra, :] += grid_ref[part, NG : NG + extra, :]
+        fetch.wait()
+
+    basis = (tables_ref[0], tables_ref[1])
+    turned = (tables_ref[2], tables_ref[3])
+    swapped = (tables_ref[4], tables_ref[5])
+    index_x = lax.broadcasted_iota(jnp.int32, (NG, 1), 0)
+    index_y = lax.broadcasted_iota(jnp.int32, (1, NG), 1)
+
+    def factors(index):
+        kappa = wave_of(index).astype(jnp.float32) * (2.0 * math.pi / NG)
+        squared = kappa * kappa
+        ends = (index == 0) | (index == NG // 2)
+        return squared, jnp.exp(-0.5 * squared) * jnp.where(ends, 1.0 / NG, 2.0 / NG)
+
+    square_x, damp_x = factors(index_x)
+    square_y, damp_y = factors(index_y)
+    square_xy = square_x + square_y
+    damp_xy = damp_x * damp_y
+
+    first = jnp.concatenate(
+        [
+            triple(basis, split(grid_ref[2 * step + part, 0:NG, :]), LANES)
+            for part in range(2)
+        ],
+        axis=0,
+    )
+    both = triple(split(first), turned)
+    scaled = []
+    for part in range(2):
+        squared = square_xy + kappa_ref[2 * step + part, 0]
+        root = jnp.where(squared == 0.0, 1.0, 0.0)
+        green = (1.0 - root) * (damp_xy * kappa_ref[2 * step + part, 1]) / (squared + root)
+        scaled.append(both[NG * part : NG * (part + 1)] * green)
+    back = triple(turned, split(jnp.concatenate(scaled, axis=1)))
+    halves = [back[:, 0:NG], back[:, NG:]]
+    for part in range(2):
+        half_ref[part] = halves[part]
+    full = [triple(split(halves[0]), basis), triple(split(halves[1]), swapped)]
+    low_lanes = lax.broadcasted_iota(jnp.int32, (block_x, 128), 1) < block_y
+    for brick in range(bricks):
+        rows = slice(block_x * brick, block_x * (brick + 1))
+        for slab in range(0, slabs, 2):
+            lanes = slice(block_y * slab, block_y * slab + 128)
+            here = [values[rows, lanes] for values in full]
+            sent_ref[brick * slabs + slab, 0] = jnp.where(low_lanes, here[0], here[1])
+            sent_ref[brick * slabs + slab + 1, 0] = jnp.where(low_lanes, here[1], here[0])
+
+
+def solve(block_x, block_y, window, kappa, static, charge, waves, cosine_row, tables):
+    devices, _, atoms = static.shape
+    slabs = NG // block_y
+    bricks = NG // block_x
+    parts = waves.shape[0]
+    whole = lambda shape: pl.BlockSpec(shape, lambda step: (0,) * len(shape))
+    return pl.pallas_call(
+        functools.partial(solve_kernel, block_x, block_y, window),
+        grid=(parts // 2,),
+        out_shape=[
+            jax.ShapeDtypeStruct((devices, parts // 2, block_x, 128), jnp.float32),
+            jax.ShapeDtypeStruct((parts, NG, NG), jnp.float32),
+            jax.ShapeDtypeStruct((slabs, 8, bricks * atoms), jnp.float32),
+        ],
+        in_specs=[
+            pl.BlockSpec(memory_space=pltpu.SMEM),
+            whole(static.shape),
+            whole(charge.shape),
+            whole(waves.shape),
+            whole(cosine_row.shape),
+            pl.BlockSpec(memory_space=pl.ANY),
+        ],
+        out_specs=[
+            pl.BlockSpec((devices, 1, block_x, 128), lambda step: (0, step, 0, 0)),
+            pl.BlockSpec((2, NG, NG), lambda step: (step, 0, 0)),
+            whole((slabs, 8, bricks * atoms)),
+        ],
+        scratch_shapes=[
+            pltpu.VMEM((parts, NG + window - block_y, NG), jnp.float32),
+            pltpu.VMEM(tables.shape, tables.dtype),
+            pltpu.SemaphoreType.DMA,
+        ],
+        compiler_params=pltpu.CompilerParams(vmem_limit_bytes=48 * 2**20),
+        name="solve",
+    )(kappa, static, charge, waves, cosine_row, tables)
+
+
+def sample_kernel(window, atoms_ref, waves_ref, cosine_ref, half_ref, table_ref, out_ref):
+    slabs = atoms_ref.shape[0]
+    parts = waves_ref.shape[0]
+    bricks = out_ref.shape[0] // slabs
+    block = out_ref.shape[2]
+    table = (table_ref[0], table_ref[1])
+    planes = [triple(table, split(half_ref[part]), LANES) for part in range(parts)]
+    for slab in range(slabs):
+        table_x, table_yz = atom_factors(
+            atoms_ref[slab], waves_ref, cosine_ref, window, None
+        )
+        rows = slice(window * slab, window * (slab + 1))
+        values = jnp.concatenate([plane[rows] for plane in planes], axis=0)
+        along = triple(split(values), split(table_x))
+        sums = jnp.sum(along * table_yz, axis=0, keepdims=True)
+        for brick in range(bricks):
+            out_ref[slab * bricks + brick] = sums[:, block * brick : block * (brick + 1)]
+
+
+def sample(block, window, atoms, waves, cosine_row, half, table):
+    slabs, _, row_atoms = atoms.shape
+    parts = waves.shape[0]
+    return pl.pallas_call(
+        functools.partial(sample_kernel, window),
+        out_shape=jax.ShapeDtypeStruct((slabs * row_atoms // block, 1, block), jnp.float32),
+        in_specs=full_spec(5),
+        out_specs=pl.BlockSpec(memory_space=pltpu.VMEM),
+        compiler_params=pltpu.CompilerParams(vmem_limit_bytes=48 * 2**20),
+        cost_estimate=pl.CostEstimate(
+            flops=6 * slabs * row_atoms * parts * window * NG,
+            bytes_accessed=4 * half.size,
+            transcendentals=0,
+        ),
+        name="sample",
+    )(atoms, waves, cosine_row, half, table)
+
+
+def finish_kernel(block_y, got_ref, table_ref, out_ref):
+    table = (table_ref[0], table_ref[1])
+    rows = []
+    for line in range(got_ref.shape[1]):
+        turned = got_ref[:, line, :].T
+        rows.append(jnp.concatenate([turned[0:block_y], turned[block_y:]], axis=1))
+    result = triple(split(jnp.concatenate(rows, axis=0)), table)
+    for line in range(got_ref.shape[1]):
+        out_ref[line] = result[block_y * line : block_y * (line + 1)]
+
+
+def finish(block_x, block_y, got, table):
+    step = 8
+    return pl.pallas_call(
+        functools.partial(finish_kernel, block_y),
+        grid=(block_x // step,),
+        out_shape=jax.ShapeDtypeStruct((block_x, block_y, NG), jnp.float32),
+        in_specs=[
+            pl.BlockSpec((NG // 2, step, 128), lambda index: (0, index, 0)),
+            pl.BlockSpec((2, NG, NG), lambda index: (0, 0, 0)),
+        ],
+        out_specs=pl.BlockSpec((step, block_y, NG), lambda index: (index, 0, 0)),
+        compiler_params=pltpu.CompilerParams(vmem_limit_bytes=32 * 2**20),
+        name="finish",
+    )(got, table)
+
+
+def two_parts(table):
+    table = np.asarray(table, np.float32)
+    high = table.astype(ml_dtypes.bfloat16)
+    low = (table - high.astype(np.float32)).astype(ml_dtypes.bfloat16)
+    return np.stack([high, low])
+
+
+def real_basis():
+    index = np.arange(NG)
+    wave = np.where(index <= NG // 2, index, index - NG // 2)
+    angle = (wave[:, None] * index[None, :] % NG) * (2.0 * math.pi / NG)
+    return np.where((index <= NG // 2)[:, None], np.cos(angle), np.sin(angle))
+
+
+def per_device(
+    positions,
+    types,
+    neighbours,
+    neighbour_count,
+    send_index,
+    cell_x,
+    cell_y,
+    cell_z,
+    spline_fraction,
+    embed_first,
+    embed_second,
+    embed_third,
+    energy_in,
+    energy_hidden,
+    energy_out,
+    wannier_in,
+    wannier_hidden,
+    wannier_out,
+    charge_base,
+):
+    atoms = types.shape[1]
+    ghosts = send_index.shape[1] // 2
+    count_x = lax.axis_size("brick")
+    count_y = lax.axis_size("slab")
+    devices = count_x * count_y
+    block_x = NG // count_x
+    block_y = NG // count_y
+    window = block_y + 8
+    parts = NG // devices
+    brick = lax.axis_index("brick")
+    slab = lax.axis_index("slab")
+
+    def exchange(values, axes):
+        return lax.all_to_all(values, axes, split_axis=0, concat_axis=0, tiled=True)
+
+    own, outgoing, static = collect(
+        devices,
+        (brick * block_x).astype(jnp.int32).reshape(1),
+        positions,
+        types,
+        neighbour_count,
+        send_index,
+        cell_x,
+        cell_y,
+        cell_z,
+        spline_fraction,
+    )
+    up = [(i, (i + 1) % count_x) for i in range(count_x)]
+    down = [((i + 1) % count_x, i) for i in range(count_x)]
+    lower = lax.ppermute(outgoing, "brick", up)
+    upper = lax.ppermute(outgoing, "brick", down)
+    static = exchange(static, ("slab", "brick"))
+
+    descriptor, charge, charge_copies = networks(
+        devices,
+        ghosts,
+        charge_base,
+        own,
+        lower,
+        upper,
+        neighbours,
+        types,
+        embed_first,
+        embed_second,
+        embed_third,
+        wannier_in,
+        wannier_hidden,
+        wannier_out,
+    )
+    every_charge = exchange(charge_copies, ("slab", "brick"))
+
+    part = (brick * count_y + slab) * parts + jnp.arange(parts, dtype=jnp.int32)
+    wave = wave_of(part)
+    waves = jnp.stack([wave, jnp.where(part <= NG // 2, 0, 3 * NG // 4)], axis=1)
+    kappa = wave.astype(jnp.float32) * (2.0 * math.pi / NG)
+    squared = kappa * kappa
+    ends = (part == 0) | (part == NG // 2)
+    kappa = jnp.stack(
+        [squared, jnp.exp(-0.5 * squared) * jnp.where(ends, 1.0 / NG, 2.0 / NG)], axis=1
+    )
+    basis = real_basis()
+    swapped = basis.reshape(NG, -1, 2, block_y)[:, :, ::-1].reshape(NG, NG)
+    tables = np.concatenate([two_parts(basis), two_parts(basis.T), two_parts(swapped)])
+    cosine_row = np.cos(np.arange(128) * (2.0 * math.pi / NG)).astype(np.float32)[None]
+    sent, half, every_atom = solve(
+        block_x,
+        block_y,
+        window,
+        kappa,
+        static,
+        every_charge,
+        waves,
+        jnp.asarray(cosine_row),
+        jnp.asarray(tables),
+    )
+    got = exchange(sent.reshape(devices, -1, 128), ("brick", "slab"))
+    points = (np.arange(count_y)[:, None] * block_y + np.arange(window)[None, :]) % NG
+    partial = sample(
+        atoms,
+        window,
+        every_atom,
+        waves,
+        jnp.asarray(cosine_row),
+        half,
+        jnp.asarray(two_parts(basis.T[points.reshape(-1)])),
+    )
+    energy_short = energies(descriptor, energy_in, energy_hidden, energy_out)
+    potential_at = jnp.sum(exchange(partial, ("slab", "brick")), axis=0)
+    atom_energy = energy_short + 0.5 * charge * potential_at
+    pairs = basis.reshape(-1, 2, NG).transpose(1, 0, 2)
+    ordered = np.stack([two_parts(pairs.reshape(NG, NG)), two_parts(pairs[::-1].reshape(NG, NG))])
+    potential = finish(
+        block_x,
+        block_y,
+        got.reshape(NG // 2, block_x, 128),
+        lax.dynamic_index_in_dim(jnp.asarray(ordered), slab % 2, 0, keepdims=False),
+    )
+    return atom_energy, potential
+
+
 def solution(mesh):
     placed = (
         P(None, "slab", "brick"),
@@ -276,19 +1082,10 @@
         P("slab", "brick"),
         P("slab", "brick"),
         P(None, "slab", "brick"),
-        P(),
-        P(),
-        P(),
-        P(),
-        P(),
-        P(),
-        P(),
-        P(),
-        P(),
-        P(),
-    )
+    ) + (P(),) * 10
+    fits = 2 * (NG // mesh.shape["slab"]) == 128 and (NG // 2) % mesh.size == 0
     return jax.shard_map(
-        per_device,
+        per_device if fits else per_device_general,
         mesh=mesh,
         in_specs=placed,
         out_specs=(P("slab", "brick"), P("brick", "slab", None)),

time: 1690 us -> 153 us (0.09)
  local copies, waits for them, and re-layouts: 925 us -> 15.4 us
  blocking collectives: 266 us -> 9.37 us
  other arithmetic: 175 us -> 0.71 us
  matrix products: 133 us -> 0 us
  waiting for transfers between devices: 157 us -> 59.9 us
  Pallas kernels: 0 us -> 49.7 us
    gather x775 -> x0, local copies, waits for them, and re-layouts: 422 us -> none
    all_to_all x2 -> x1, blocking collectives: 266 us -> 9.37 us  [exchange(): return lax.all_to_all(values, axes, split_axis=0, concat_axis=0, tiled=True)]
    scatter-add x1 -> x0, local copies, waits for them, and re-layouts: 134 us -> none  [fold_windows(): main_part = main_part.at[:, :3].add(carried)]
    all_to_all x3 -> x0, other arithmetic: 125 us -> none  [the longest x1 54.4 us: per_device(): lax.all_to_all(moved, 'slab', split_axis=2, concat_axis=3, tiled=True)]
    dot_general x50 -> x0, matrix products: 110 us -> none  [the longest x12 63.6 us: along(): jnp.tensordot(values, table, axes=([axis_index], [0]), precision=HIGH)]
    all_to_all x2 -> x3, waiting for transfers between devices: 157 us -> 58.3 us  [exchange(): return lax.all_to_all(values, axes, split_axis=0, concat_axis=0, tiled=True)]
    unnamed x61 -> x38, local copies, waits for them, and re-layouts: 101 us -> 13.6 us
    slice x25 -> x0, local copies, waits for them, and re-layouts: 83.9 us -> none  [the longest x9 30 us: make_windows(): trailing = jnp.roll(pieces, -1, axis=0)[:, :3]]
  transfers between devices with their start and end apart: 4 -> 5, of which waited for: 2 -> 4; matrix products, arithmetic and copies ran while one was open for 1% -> 2% of each run, Pallas kernels for 0% -> 1%
where the time goes in v1:
time: 153 us; the launch traced here: 152 us
  waiting for transfers between devices  59.9 us (39%)
  Pallas kernels  49.7 us (32%)
  starting transfers between devices  15.8 us (10%)
  local copies, waits for them, and re-layouts  15.4 us (10%)
  blocking collectives  9.37 us (6%)
    all_to_all x3, waiting for transfers between devices, exchange(): return lax.all_to_all(values, axes, split_axis=0, concat_axis=0, tiled=True)  58.3 us
    pallas_call x1, Pallas kernels, solve(): pl.pallas_call(functools.partial(solve_kernel, block_x, block_y, window),...  16.7 us
    pallas_call x1, Pallas kernels, networks(): pl.pallas_call(functools.partial(network_kernel, ghosts), out_shape=[jax....  16 us
    unnamed x38, local copies, waits for them, and re-layouts  13.6 us
    all_to_all x3, starting transfers between devices, exchange(): return lax.all_to_all(values, axes, split_axis=0, concat_axis=0, tiled=True)  12.5 us
    pallas_call x1, Pallas kernels, sample(): pl.pallas_call(functools.partial(sample_kernel, window), out_shape=jax.Sh...  9.89 us
    all_to_all x1, blocking collectives, exchange(): return lax.all_to_all(values, axes, split_axis=0, concat_axis=0, tiled=True)  9.37 us
    pallas_call x1, Pallas kernels, finish(): pl.pallas_call(functools.partial(finish_kernel, block_y), grid=(block_x /...  3.65 us
  transfers between devices with their start and end apart: 5, of which 4 were waited for; matrix products, arithmetic and copies ran while one was open for 2% of the time, Pallas kernels for 1%

profile of v1, /device:TPU:0, one launch (start us, length us, event | category | flops | bytes accessed | tf_op | source)
XLA Modules:
  0.0 151.6 jit_solution(10731952576955480753)
XLA Ops:
  0.6 0.0 copy-start.16
  0.7 1.6 %collect_atoms.1 = (f32[8,256]{1,0:T(8,128)}, f32[8,256]{1,0:T(8,128)}, f32[32,8,192]{2,1,0:T(8,128)}) custom-call(s32[1]{0:T(128)} %bitcast.base_ref, f32[3,1,192]{2,1,0:T(1,128)} %positions_ref.1, s32[1,192]{1,0:T(1,128)} %types_ref.3, s32[1,192]{1,0:T(1,128)} %count_ref.1, s32[1,192]{1,0:T(1,128)} %send_ref.1, s32[1,192]{1,0:T(1,128)} %cell_x_ref.1, ...), custom_call_target="tpu_custom_call" | custom-call | tf_op jit(solution)/shard_map/collect_atoms/pallas_call | solution.py:350
  2.2 0.5 collective-permute-start
  2.7 2.9 %collective-permute-start.1 = (f32[8,256]{1,0:T(8,128)}, f32[8,256]{1,0:T(8,128)S(1)}, u32[]{:S(2)}, u32[]{:S(2)}) collective-permute-start(f32[8,256]{1,0:T(8,128)} %get-tuple-element.12), channel_id=1, source_target_pairs={{4,0},{8,4},{12,8},{16,12},{20,16},{24,20},{28,24},{0,28},{5,1},{9... | collective-permute-start | bytes 24584 | tf_op jit(solution)/shard_map/ppermute | solution.py:1004
  5.6 1.5 %collective-permute-done.lower_ref = f32[8,256]{1,0:T(8,128)S(1)} collective-permute-done((f32[8,256]{1,0:T(8,128)}, f32[8,256]{1,0:T(8,128)S(1)}, u32[]{:S(2)}, u32[]{:S(2)}) %collective-permute-start) | collective-permute-done | bytes 8224 | tf_op jit(solution)/shard_map/ppermute | solution.py:1003
  7.1 0.0 collective-permute-done.1.upper_ref
  7.2 0.0 copy-start.1
  7.2 1.4 copy-done.1
  8.6 0.0 copy-start.5
  8.6 1.0 copy-done.5
  9.6 0.0 copy-start.7
  9.6 0.8 copy-done.7
  10.4 0.0 copy-start.8
  10.4 0.7 copy-done.8
  11.2 0.0 copy-start.9
  11.2 0.7 copy-done.9
  11.9 0.0 copy-start.10
  11.9 0.7 copy-done.10
  12.6 0.0 copy-start.11
  12.6 0.7 copy-done.11
  13.3 0.0 copy-start.12
  13.3 0.7 copy-done.12
  14.0 0.0 copy-start.13
  14.0 0.7 copy-done.13
  14.7 0.0 copy-start.14
  14.7 0.7 copy-done.14
  15.3 0.0 copy-start.17
  15.3 0.7 copy-done.17
  16.0 0.0 copy-start.4
  16.0 0.0 copy-start.18
  16.0 16.0 %networks.1 = (f32[192,1600]{1,0:T(8,128)S(1)}, f32[1,192]{1,0:T(1,128)S(1)}, f32[32,1,192]{2,1,0:T(1,128)}) custom-call(f32[2]{0:T(128)S(1)} %copy-done.17, f32[8,256]{1,0:T(8,128)S(1)} %copy-done.11, f32[8,256]{1,0:T(8,128)S(1)} %collective-permute-done.lower_ref, f32[8,256]{1,0:T(8,128)S(1)} %collective-permute-done.1.upper_ref, s32[64,192]{1,0:T(8,128)S(1)} %bitcast.17, ...), custom_call_target="tpu_custom_call" | custom-call | tf_op jit(solution)/shard_map/networks/pallas_call | solution.py:620
  32.0 6.9 %all-to-all-start.1 = ((f32[32,1,192]{2,1,0:T(1,128)}), f32[32,1,192]{2,1,0:T(1,128)S(1)}, u32[]{:S(2)}, u32[]{:S(2)}) async-start(f32[32,1,192]{2,1,0:T(1,128)} %get-tuple-element.16), calls=%async_computation.1 | async-start | bytes 65536 | tf_op jit(solution)/shard_map/all_to_all | solution.py:987
  38.9 7.2 %all-to-all-done.1.charge_ref = f32[32,1,192]{2,1,0:T(1,128)S(1)} async-done(((f32[32,1,192]{2,1,0:T(1,128)}), f32[32,1,192]{2,1,0:T(1,128)S(1)}, u32[]{:S(2)}, u32[]{:S(2)}) %all-to-all-start.1) | async-done | bytes 24608 | tf_op jit(solution)/shard_map/all_to_all | solution.py:987
  46.1 2.8 %all-to-all-start = ((f32[32,8,192]{2,1,0:T(8,128)}), f32[32,8,192]{2,1,0:T(8,128)S(1)}, u32[]{:S(2)}, u32[]{:S(2)}) async-start(f32[32,8,192]{2,1,0:T(8,128)} %get-tuple-element.15), calls=%async_computation | async-start | bytes 524288 | tf_op jit(solution)/shard_map/all_to_all | solution.py:987
  48.9 0.1 copy.26.kappa_ref
  49.0 0.1 copy.27.waves_ref
  49.1 10.2 %all-to-all-done.static_ref = f32[32,8,192]{2,1,0:T(8,128)S(1)} async-done(((f32[32,8,192]{2,1,0:T(8,128)}), f32[32,8,192]{2,1,0:T(8,128)S(1)}, u32[]{:S(2)}, u32[]{:S(2)}) %all-to-all-start) | async-done | bytes 196640 | tf_op jit(solution)/shard_map/all_to_all | solution.py:987
  59.3 0.0 copy-done.16
  59.3 0.0 copy-done.4
  59.3 16.7 %solve.1 = (f32[32,4,32,128]{3,2,1,0:T(8,128)S(1)}, f32[8,256,256]{2,1,0:T(8,128)S(1)}, f32[4,8,1536]{2,1,0:T(8,128)S(1)}) custom-call(f32[8,2]{1,0:T(8,128)S(1)} %copy.26.kappa_ref, f32[32,8,192]{2,1,0:T(8,128)S(1)} %all-to-all-done.static_ref, f32[32,1,192]{2,1,0:T(1,128)S(1)} %all-to-all-done.1.charge_ref, s32[8,2]{1,0:T(8,128)S(1)} %copy.27.waves_ref, ...), custom_call_target="tpu_custom_call" | custom-call | tf_op jit(solution)/shard_map/solve/pallas_call | solution.py:844
  76.0 0.0 copy-start
  76.1 1.3 copy-done
  77.4 0.0 copy-done.18
  77.4 9.9 %sample.1 = f32[32,1,192]{2,1,0:T(1,128)S(1)} custom-call(f32[4,8,1536]{2,1,0:T(8,128)S(1)} %get-tuple-element.17.atoms_ref, s32[8,2]{1,0:T(8,128)S(1)} %copy.27.waves_ref, f32[1,128]{1,0:T(1,128)S(1)} %copy-done.16, f32[8,256,256]{2,1,0:T(8,128)S(1)} %get-tuple-element.18.half_ref, bf16[2,288,256]{2,1,0:T(8,128)(2,1)S(1)} %copy-done.18), custom_call_target="tpu_custom_call" | custom-call | flops 5435817984 | bytes 2097152 | tf_op jit(solution)/shard_map/sample/pallas_call | solution.py:897
  87.3 9.4 %all_to_all.20 = f32[32,1,192]{2,1,0:T(1,128)S(1)} all-to-all(f32[32,1,192]{2,1,0:T(1,128)S(1)} %sample.1), channel_id=1, replica_groups=mesh['brick'=8,'slab'=4] {'slab','brick'}, dimensions={0} | all-to-all | bytes 49152 | tf_op jit(solution)/shard_map/all_to_all | solution.py:987
  96.6 0.0 copy-start.15
  96.6 2.9 %all-to-all-start.3 = ((f32[32,128,128]{2,1,0:T(8,128)}), f32[32,128,128]{2,1,0:T(8,128)S(1)}, u32[]{:S(2)}, u32[]{:S(2)}) async-start(f32[32,128,128]{2,1,0:T(8,128)} %bitcast.14), calls=%async_computation.3 | async-start | bytes 4194304 | tf_op jit(solution)/shard_map/all_to_all | solution.py:987
  99.5 1.7 %dynamic-slice_bitcast_fusion.table_ref = bf16[2,256,256]{2,1,0:T(8,128)(2,1)} fusion(bf16[2,2,256,256]{3,2,1,0:T(8,128)(2,1)} %constant.66.clone, s32[]{:T(128)S(6)} %select_n.56), kind=kLoop, calls=%fused_computation | loop fusion | bytes 524292 | tf_op jit(solution)/shard_map/jit(dynamic_index_in_dim)/squeeze | solution.py:1069
  101.2 0.0 copy-done.15
  101.2 0.0 copy-start.2
  101.2 1.4 copy-done.2
  102.6 0.0 copy-start.6
  102.6 1.0 copy-done.6
  103.6 1.9 %energies.1 = f32[1,192]{1,0:T(1,128)S(1)} custom-call(f32[192,1600]{1,0:T(8,128)S(1)} %get-tuple-element.13.descriptor_ref, f32[240,1600]{1,0:T(8,128)S(1)} %bitcast.16, f32[2,240,240]{2,1,0:T(8,128)S(1)} %copy-done.6, f32[1,240]{1,0:T(1,128)S(1)} %bitcast.19), custom_call_target="tpu_custom_call" | custom-call | flops 442368000 | bytes 1536000 | tf_op jit(solution)/shard_map/energies/pallas_call | solution.py:669
  105.5 0.1 reduce_sum.11
  105.6 0.6 multiply_add_fusion
  106.2 40.8 %all-to-all-done.3 = f32[32,128,128]{2,1,0:T(8,128)S(1)} async-done(((f32[32,128,128]{2,1,0:T(8,128)}), f32[32,128,128]{2,1,0:T(8,128)S(1)}, u32[]{:S(2)}, u32[]{:S(2)}) %all-to-all-start.3) | async-done | bytes 2097184 | tf_op jit(solution)/shard_map/all_to_all | solution.py:987
  147.0 0.0 copy-start.3
  147.0 0.9 copy-done.3
  147.9 3.6 %finish.1 = f32[32,64,256]{2,1,0:T(8,128)} custom-call(f32[128,32,128]{2,1,0:T(8,128)S(1)} %bitcast.13, bf16[2,256,256]{2,1,0:T(8,128)(2,1)S(1)} %copy-done.3), custom_call_target="tpu_custom_call" | custom-call | tf_op jit(solution)/shard_map/finish/pallas_call | solution.py:925
  (4 shorter events, 0.0 us)
Async XLA Ops:
  0.6 58.7 %copy-start.16 = (f32[1,128]{1,0:T(1,128)S(1)}, f32[1,128]{1,0:T(1,128)}, u32[]{:S(2)}) copy-start(f32[1,128]{1,0:T(1,128)} %constant.63.clone.cosine_ref) | copy-start | bytes 1540
  2.2 4.9 %collective-permute-start = (f32[8,256]{1,0:T(8,128)}, f32[8,256]{1,0:T(8,128)S(1)}, u32[]{:S(2)}, u32[]{:S(2)}) collective-permute-start(f32[8,256]{1,0:T(8,128)} %get-tuple-element.12), channel_id=1, source_target_pairs={{0,4},{4,8},{8,12},{12,16},{16,20},{20,24},{24,28},{28,0},{1,5},{5... | collective-permute-start | bytes 24584 | tf_op jit(solution)/shard_map/ppermute | solution.py:1003
  2.7 4.5 %collective-permute-start.1 = (f32[8,256]{1,0:T(8,128)}, f32[8,256]{1,0:T(8,128)S(1)}, u32[]{:S(2)}, u32[]{:S(2)}) collective-permute-start(f32[8,256]{1,0:T(8,128)} %get-tuple-element.12), channel_id=1, source_target_pairs={{4,0},{8,4},{12,8},{16,12},{20,16},{24,20},{28,24},{0,28},{5,1},{9... | collective-permute-start | bytes 24584 | tf_op jit(solution)/shard_map/ppermute | solution.py:1004
  7.2 1.4 copy-start.1
  8.6 1.0 copy-start.5
  9.6 0.8 copy-start.7
  10.4 0.7 copy-start.8
  11.2 0.7 copy-start.9
  11.9 0.7 copy-start.10
  12.6 0.7 copy-start.11
  13.3 0.7 copy-start.12
  14.0 0.7 copy-start.13
  14.7 0.7 copy-start.14
  15.3 0.7 copy-start.17
  16.0 43.3 %copy-start.4 = (bf16[6,256,256]{2,1,0:T(8,128)(2,1)S(1)}, bf16[6,256,256]{2,1,0:T(8,128)(2,1)}, u32[]{:S(2)}) copy-start(bf16[6,256,256]{2,1,0:T(8,128)(2,1)} %constant.64.clone.tables_hbm) | copy-start | bytes 2359300
  16.0 61.4 %copy-start.18 = (bf16[2,288,256]{2,1,0:T(8,128)(2,1)S(1)}, bf16[2,288,256]{2,1,0:T(8,128)(2,1)}, u32[]{:S(2)}) copy-start(bf16[2,288,256]{2,1,0:T(8,128)(2,1)} %constant.65.clone.table_ref) | copy-start | bytes 884740
  32.0 14.1 %all-to-all-start.1 = ((f32[32,1,192]{2,1,0:T(1,128)}), f32[32,1,192]{2,1,0:T(1,128)S(1)}, u32[]{:S(2)}, u32[]{:S(2)}) async-start(f32[32,1,192]{2,1,0:T(1,128)} %get-tuple-element.16), calls=%async_computation.1 | async-start | bytes 65536 | tf_op jit(solution)/shard_map/all_to_all | solution.py:987
  46.1 13.2 %all-to-all-start = ((f32[32,8,192]{2,1,0:T(8,128)}), f32[32,8,192]{2,1,0:T(8,128)S(1)}, u32[]{:S(2)}, u32[]{:S(2)}) async-start(f32[32,8,192]{2,1,0:T(8,128)} %get-tuple-element.15), calls=%async_computation | async-start | bytes 524288 | tf_op jit(solution)/shard_map/all_to_all | solution.py:987
  76.0 1.3 copy-start
  96.6 4.6 %copy-start.15 = (f32[240]{0:T(256)S(1)}, f32[240]{0:T(256)}, u32[]{:S(2)}) copy-start(f32[240]{0:T(256)} %param.38) | copy-start | bytes 2884
  96.6 50.4 %all-to-all-start.3 = ((f32[32,128,128]{2,1,0:T(8,128)}), f32[32,128,128]{2,1,0:T(8,128)S(1)}, u32[]{:S(2)}, u32[]{:S(2)}) async-start(f32[32,128,128]{2,1,0:T(8,128)} %bitcast.14), calls=%async_computation.3 | async-start | bytes 4194304 | tf_op jit(solution)/shard_map/all_to_all | solution.py:987
  101.2 1.4 copy-start.2
  102.6 1.0 copy-start.6
  147.0 1.0 copy-start.3

commit v2 on v1

--- a/solution.py
+++ b/solution.py
@@ -295,38 +295,19 @@
     return jnp.take_along_axis(table, index, axis=1, mode="promise_in_bounds")
 
 
-def full_spec(count):
-    return [pl.BlockSpec(memory_space=pltpu.VMEM)] * count
+def whole(shape):
+    return pl.BlockSpec(tuple(shape), lambda step: (0,) * len(shape))
+
+
+def whole_specs(*arrays):
+    return [whole(array.shape) for array in arrays]
 
 
 def collect_kernel(
-    base_ref,
-    positions_ref,
-    types_ref,
-    count_ref,
-    send_ref,
-    cell_x_ref,
-    cell_y_ref,
-    cell_z_ref,
-    fraction_ref,
-    own_ref,
-    outgoing_ref,
-    static_ref,
+    positions_ref, types_ref, count_ref, send_ref, own_ref, outgoing_ref
 ):
     atoms = types_ref.shape[1]
     own_ref[...] = jnp.zeros_like(own_ref)
-    static = jnp.concatenate(
-        [
-            (cell_x_ref[...] + base_ref[0]).astype(jnp.float32),
-            cell_y_ref[...].astype(jnp.float32),
-            cell_z_ref[...].astype(jnp.float32),
-        ]
-        + [fraction_ref[axis] for axis in range(3)]
-        + [jnp.zeros((2, atoms), jnp.float32)],
-        axis=0,
-    )
-    for copy in range(static_ref.shape[0]):
-        static_ref[copy] = static
     for axis in range(3):
         own_ref[axis : axis + 1, 0:atoms] = positions_ref[axis]
     own_ref[3:4, 0:atoms] = types_ref[...].astype(jnp.float32)
@@ -343,21 +324,17 @@
         )
 
 
-def collect(
-    copies, base, positions, types, counts, send_index, cell_x, cell_y, cell_z, fraction
-):
-    atoms = types.shape[1]
+def collect(positions, types, counts, send_index):
+    arrays = (positions, types, counts, send_index)
+    result = jax.ShapeDtypeStruct((8, 256), jnp.float32)
     return pl.pallas_call(
         collect_kernel,
-        out_shape=[
-            jax.ShapeDtypeStruct((8, 256), jnp.float32),
-            jax.ShapeDtypeStruct((8, 256), jnp.float32),
-            jax.ShapeDtypeStruct((copies, 8, atoms), jnp.float32),
-        ],
-        in_specs=[pl.BlockSpec(memory_space=pltpu.SMEM)] + full_spec(8),
-        out_specs=full_spec(3),
+        grid=(1,),
+        out_shape=[result, result],
+        in_specs=whole_specs(*arrays),
+        out_specs=whole_specs(result, result),
         name="collect_atoms",
-    )(base, positions, types, counts, send_index, cell_x, cell_y, cell_z, fraction)
+    )(*arrays)
 
 
 def fitting_rows(descriptor_ref, weight_in_ref, weight_hidden_ref, weight_out_ref):
@@ -401,11 +378,16 @@
 def network_kernel(
     ghosts,
     base_ref,
+    charges_ref,
     own_ref,
     lower_ref,
     upper_ref,
     slots_ref,
     types_ref,
+    cell_x_ref,
+    cell_y_ref,
+    cell_z_ref,
+    fraction_ref,
     first_ref,
     second_ref,
     third_ref,
@@ -413,9 +395,10 @@
     weight_in_hbm,
     weight_hidden_hbm,
     weight_out_ref,
-    descriptor_ref,
+    descriptor_hbm,
     charge_ref,
     copies_ref,
+    descriptor_ref,
     environment_ref,
     kind_ref,
     moments_ref,
@@ -575,14 +558,27 @@
 
     lax.fori_loop(0, atoms // 8, describe, 0)
 
+    store = pltpu.make_async_copy(descriptor_ref, descriptor_hbm, semaphores.at[2])
+    store.start()
     for fetch in fetches:
         fetch.wait()
     shift = fitting_rows(descriptor_ref, weight_in_ref, weight_hidden_ref, weight_out_ref)
     kind = types_ref[...].astype(jnp.float32)
-    charge = (1.0 - kind) * base_ref[0] + kind * base_ref[1] + natural_order(shift)
+    charge = (1.0 - kind) * charges_ref[0] + kind * charges_ref[1] + natural_order(shift)
     charge_ref[...] = charge
+    fields = jnp.concatenate(
+        [
+            cell_x_ref[...].astype(jnp.float32),
+            (cell_y_ref[...] + base_ref[0]).astype(jnp.float32),
+            cell_z_ref[...].astype(jnp.float32),
+        ]
+        + [fraction_ref[axis] for axis in range(3)]
+        + [charge, jnp.zeros((1, atoms), jnp.float32)],
+        axis=0,
+    )
     for copy in range(copies_ref.shape[0]):
-        copies_ref[copy] = charge
+        copies_ref[copy] = fields
+    store.wait()
 
 
 def spot_table(embed, desc):
@@ -600,61 +596,54 @@
 def networks(
     copies,
     ghosts,
+    base,
     charge_base,
     own,
     lower,
     upper,
     neighbours,
     types,
-    embed_first,
-    embed_second,
-    embed_third,
+    cells,
+    fraction,
+    embed,
     weight_in,
     weight_hidden,
     weight_out,
 ):
     atoms = types.shape[1]
     desc, width = weight_in.shape
-    spots = jnp.asarray(spot_table(embed_third.shape[1], desc))
+    spots = jnp.asarray(spot_table(embed[2].shape[1], desc))
     anywhere = pl.BlockSpec(memory_space=pl.ANY)
+    scalars = pl.BlockSpec(memory_space=pltpu.SMEM)
+    blocks = (own, lower, upper, neighbours[0].T, types, *cells, fraction, *embed, spots)
+    weight_out = weight_out.reshape(1, -1)
+    results = [
+        jax.ShapeDtypeStruct((atoms, desc), jnp.float32),
+        jax.ShapeDtypeStruct((1, atoms), jnp.float32),
+        jax.ShapeDtypeStruct((copies, 8, atoms), jnp.float32),
+    ]
     return pl.pallas_call(
         functools.partial(network_kernel, ghosts),
-        out_shape=[
-            jax.ShapeDtypeStruct((atoms, desc), jnp.float32),
-            jax.ShapeDtypeStruct((1, atoms), jnp.float32),
-            jax.ShapeDtypeStruct((copies, 1, atoms), jnp.float32),
-        ],
-        in_specs=[pl.BlockSpec(memory_space=pltpu.SMEM)]
-        + full_spec(9)
+        grid=(1,),
+        out_shape=results,
+        in_specs=[scalars, scalars]
+        + whole_specs(*blocks)
         + [anywhere, anywhere]
-        + full_spec(1),
-        out_specs=full_spec(3),
+        + whole_specs(weight_out),
+        out_specs=[anywhere] + whole_specs(*results[1:]),
         scratch_shapes=[
+            pltpu.VMEM((atoms, desc), jnp.float32),
             pltpu.VMEM((4, atoms // 2, 128), jnp.float32),
             pltpu.VMEM((atoms // 2, 128), jnp.float32),
             pltpu.VMEM((4, atoms, 128), jnp.float32),
             pltpu.VMEM((3, 128, 128), jnp.float32),
             pltpu.VMEM((width, desc), jnp.float32),
             pltpu.VMEM(weight_hidden.shape, jnp.float32),
-            pltpu.SemaphoreType.DMA((2,)),
+            pltpu.SemaphoreType.DMA((3,)),
         ],
         compiler_params=pltpu.CompilerParams(vmem_limit_bytes=32 * 2**20),
         name="networks",
-    )(
-        charge_base,
-        own,
-        lower,
-        upper,
-        neighbours[0].T,
-        types,
-        embed_first,
-        embed_second,
-        embed_third,
-        spots,
-        weight_in.T,
-        weight_hidden,
-        weight_out.reshape(1, -1),
-    )
+    )(base, charge_base, *blocks, weight_in.T, weight_hidden, weight_out)
 
 
 def energy_kernel(descriptor_ref, weight_in_ref, weight_hidden_ref, weight_out_ref, energy_ref):
@@ -666,17 +655,20 @@
 def energies(descriptor, weight_in, weight_hidden, weight_out):
     atoms, desc = descriptor.shape
     width = weight_in.shape[1]
+    arrays = (descriptor, weight_in.T, weight_hidden, weight_out.reshape(1, -1))
+    result = jax.ShapeDtypeStruct((1, atoms), jnp.float32)
     return pl.pallas_call(
         energy_kernel,
-        out_shape=jax.ShapeDtypeStruct((1, atoms), jnp.float32),
-        in_specs=full_spec(4),
-        out_specs=pl.BlockSpec(memory_space=pltpu.VMEM),
+        grid=(1,),
+        out_shape=result,
+        in_specs=whole_specs(*arrays),
+        out_specs=whole(result.shape),
         compiler_params=pltpu.CompilerParams(vmem_limit_bytes=32 * 2**20),
         cost_estimate=pl.CostEstimate(
             flops=6 * atoms * desc * width, bytes_accessed=4 * desc * width, transcendentals=0
         ),
         name="energies",
-    )(descriptor, weight_in.T, weight_hidden, weight_out.reshape(1, -1))
+    )(*arrays)
 
 
 def weight_rows(fraction):
@@ -701,21 +693,10 @@
     return result
 
 
-def atom_factors(fields, waves_ref, cosine_ref, window, scale):
-    row = lambda field: fields[field : field + 1, :]
+def third_factors(fields, waves_ref, cosine_ref):
     atoms = fields.shape[1]
-    start_x = row(0).astype(jnp.int32)
-    start_y = row(1).astype(jnp.int32)
-    start_z = row(2).astype(jnp.int32)
-    along_x = weight_rows(row(3))
-    along_y = weight_rows(row(4))
-    along_z = weight_rows(row(5))
-    if scale is not None:
-        along_x = [weight * scale for weight in along_x]
-    rows_x = lax.broadcasted_iota(jnp.int32, (NG, atoms), 0)
-    table_x = placed_weights((rows_x - start_x) & (NG - 1), along_x)
-    rows_y = lax.broadcasted_iota(jnp.int32, (window, atoms), 0)
-    table_y = placed_weights(rows_y - start_y, along_y)
+    start = fields[2:3, :].astype(jnp.int32)
+    along = weight_rows(fields[5:6, :])
     parts = waves_ref.shape[0]
     cosine = jnp.broadcast_to(cosine_ref[...], (parts, 128))
     wave = jnp.broadcast_to(waves_ref[:, 0:1], (parts, 128))
@@ -725,17 +706,33 @@
         lanes = slice(128 * chunk, 128 * chunk + 128)
         total = jnp.zeros((parts, 128), jnp.float32)
         for step in range(4):
-            place = jnp.broadcast_to(start_z[:, lanes] + step, (parts, 128))
+            place = jnp.broadcast_to(start[:, lanes] + step, (parts, 128))
             phase = (wave * place + shift) & (NG - 1)
             value = lane_pick(cosine, phase & 127)
             value = jnp.where(phase < 128, value, -value)
-            total = total + value * jnp.broadcast_to(along_z[step][:, lanes], (parts, 128))
+            total = total + value * jnp.broadcast_to(along[step][:, lanes], (parts, 128))
         pieces.append(total)
-    table_z = jnp.concatenate(pieces, axis=1)
-    table_yz = jnp.concatenate(
-        [table_y * table_z[part : part + 1, :] for part in range(parts)], axis=0
-    )
-    return table_x, table_yz
+    return jnp.concatenate(pieces, axis=1)
+
+
+def first_third(fields, waves_ref, cosine_ref, window, scale):
+    atoms = fields.shape[1]
+    third = third_factors(fields, waves_ref, cosine_ref)
+    if scale is not None:
+        third = third * scale
+    rows = lax.broadcasted_iota(jnp.int32, (window, atoms), 0)
+    first = placed_weights(
+        rows - fields[0:1, :].astype(jnp.int32), weight_rows(fields[3:4, :])
+    )
+    return jnp.concatenate(
+        [first * third[part : part + 1, :] for part in range(third.shape[0])], axis=0
+    )
+
+
+def second_factors(fields, base):
+    rows = lax.broadcasted_iota(jnp.int32, (NG, fields.shape[1]), 0)
+    start = fields[1:2, :].astype(jnp.int32) - base
+    return placed_weights((rows - start) & (NG - 1), weight_rows(fields[4:5, :]))
 
 
 def wave_of(index):
@@ -747,51 +744,55 @@
     block_y,
     window,
     kappa_ref,
+    pair_ref,
     static_ref,
-    charge_ref,
     waves_ref,
     cosine_ref,
     tables_hbm,
+    last_hbm,
     sent_ref,
-    half_ref,
+    full_ref,
     atoms_ref,
     grid_ref,
     tables_ref,
-    semaphore,
+    last_ref,
+    semaphores,
 ):
-    slabs = atoms_ref.shape[0]
+    slabs = NG // block_y
+    bricks = NG // block_x
     parts = waves_ref.shape[0]
-    bricks = NG // block_x
     block = static_ref.shape[2]
     step = pl.program_id(0)
 
     @pl.when(step == 0)
     def _():
-        fetch = pltpu.make_async_copy(tables_hbm, tables_ref, semaphore)
-        fetch.start()
+        fetches = [
+            pltpu.make_async_copy(tables_hbm, tables_ref, semaphores.at[0]),
+            pltpu.make_async_copy(last_hbm.at[pair_ref[0]], last_ref, semaphores.at[1]),
+        ]
+        for fetch in fetches:
+            fetch.start()
         for slab in range(slabs):
+            lanes = slice(block * slab, block * (slab + 1))
             for brick in range(bricks):
-                lanes = slice(block * brick, block * (brick + 1))
-                atoms_ref[slab, :, lanes] = static_ref[slab * bricks + brick]
-                atoms_ref[slab, 6:7, lanes] = charge_ref[slab * bricks + brick]
+                atoms_ref[brick, :, lanes] = static_ref[slab * bricks + brick]
         grid_ref[...] = jnp.zeros_like(grid_ref)
-        for slab in range(slabs):
-            fields = atoms_ref[slab]
-            table_x, table_yz = atom_factors(
-                fields, waves_ref, cosine_ref, window, fields[6:7, :]
-            )
-            spread = triple(split(table_yz), split(table_x), LANES)
-            rows = slice(slab * block_y, slab * block_y + window)
+        for brick in range(bricks):
+            fields = atoms_ref[brick]
+            table = split(first_third(fields, waves_ref, cosine_ref, window, fields[6:7, :]))
+            spread = triple(table, split(second_factors(fields, 0)), LANES)
+            rows = slice(block_x * brick, block_x * brick + window)
             for part in range(parts):
                 grid_ref[part, rows, :] += spread[part * window : part * window + window]
-        extra = window - block_y
+        extra = window - block_x
         for part in range(parts):
             grid_ref[part, 0:extra, :] += grid_ref[part, NG : NG + extra, :]
-        fetch.wait()
+        for fetch in fetches:
+            fetch.wait()
 
     basis = (tables_ref[0], tables_ref[1])
     turned = (tables_ref[2], tables_ref[3])
-    swapped = (tables_ref[4], tables_ref[5])
+    last = (last_ref[0], last_ref[1])
     index_x = lax.broadcasted_iota(jnp.int32, (NG, 1), 0)
     index_y = lax.broadcasted_iota(jnp.int32, (1, NG), 1)
 
@@ -806,13 +807,9 @@
     square_xy = square_x + square_y
     damp_xy = damp_x * damp_y
 
-    first = jnp.concatenate(
-        [
-            triple(basis, split(grid_ref[2 * step + part, 0:NG, :]), LANES)
-            for part in range(2)
-        ],
-        axis=0,
-    )
+    planes = jnp.concatenate([grid_ref[2 * step + part, 0:NG, :] for part in range(2)], axis=1)
+    first = triple(basis, split(planes))
+    first = jnp.concatenate([first[:, 0:NG], first[:, NG:]], axis=0)
     both = triple(split(first), turned)
     scaled = []
     for part in range(2):
@@ -821,92 +818,101 @@
         green = (1.0 - root) * (damp_xy * kappa_ref[2 * step + part, 1]) / (squared + root)
         scaled.append(both[NG * part : NG * (part + 1)] * green)
     back = triple(turned, split(jnp.concatenate(scaled, axis=1)))
-    halves = [back[:, 0:NG], back[:, NG:]]
-    for part in range(2):
-        half_ref[part] = halves[part]
-    full = [triple(split(halves[0]), basis), triple(split(halves[1]), swapped)]
-    low_lanes = lax.broadcasted_iota(jnp.int32, (block_x, 128), 1) < block_y
+    back = jnp.concatenate([back[:, 0:NG], back[:, NG:]], axis=0)
+    full = triple(split(back), last)
+    full_ref[0] = full[0:NG]
+    full_ref[1] = full[NG:]
+    low_lanes = lax.broadcasted_iota(jnp.int32, (NG, 128), 1) < block_y
+    even = full[0:NG, 0:128]
+    odd = full[NG:, 0:128]
+    blocks = [
+        jnp.where(low_lanes, even, pltpu.roll(odd, block_y, 1)),
+        jnp.where(low_lanes, pltpu.roll(even, block_y, 1), odd),
+    ]
     for brick in range(bricks):
         rows = slice(block_x * brick, block_x * (brick + 1))
-        for slab in range(0, slabs, 2):
-            lanes = slice(block_y * slab, block_y * slab + 128)
-            here = [values[rows, lanes] for values in full]
-            sent_ref[brick * slabs + slab, 0] = jnp.where(low_lanes, here[0], here[1])
-            sent_ref[brick * slabs + slab + 1, 0] = jnp.where(low_lanes, here[1], here[0])
-
-
-def solve(block_x, block_y, window, kappa, static, charge, waves, cosine_row, tables):
+        for side in range(2):
+            sent_ref[2 * brick + side, 0] = blocks[side][rows]
+
+
+def solve(block_x, block_y, window, kappa, pair, static, waves, cosine_row, tables, last):
     devices, _, atoms = static.shape
     slabs = NG // block_y
     bricks = NG // block_x
     parts = waves.shape[0]
-    whole = lambda shape: pl.BlockSpec(shape, lambda step: (0,) * len(shape))
+    anywhere = pl.BlockSpec(memory_space=pl.ANY)
+    scalars = pl.BlockSpec(memory_space=pltpu.SMEM)
     return pl.pallas_call(
         functools.partial(solve_kernel, block_x, block_y, window),
         grid=(parts // 2,),
         out_shape=[
-            jax.ShapeDtypeStruct((devices, parts // 2, block_x, 128), jnp.float32),
+            jax.ShapeDtypeStruct((2 * bricks, parts // 2, block_x, 128), jnp.float32),
             jax.ShapeDtypeStruct((parts, NG, NG), jnp.float32),
-            jax.ShapeDtypeStruct((slabs, 8, bricks * atoms), jnp.float32),
+            jax.ShapeDtypeStruct((bricks, 8, slabs * atoms), jnp.float32),
         ],
-        in_specs=[
-            pl.BlockSpec(memory_space=pltpu.SMEM),
-            whole(static.shape),
-            whole(charge.shape),
-            whole(waves.shape),
-            whole(cosine_row.shape),
-            pl.BlockSpec(memory_space=pl.ANY),
-        ],
+        in_specs=[scalars, scalars]
+        + whole_specs(static, waves, cosine_row)
+        + [anywhere, anywhere],
         out_specs=[
-            pl.BlockSpec((devices, 1, block_x, 128), lambda step: (0, step, 0, 0)),
+            pl.BlockSpec((2 * bricks, 1, block_x, 128), lambda step: (0, step, 0, 0)),
             pl.BlockSpec((2, NG, NG), lambda step: (step, 0, 0)),
-            whole((slabs, 8, bricks * atoms)),
+            whole((bricks, 8, slabs * atoms)),
         ],
         scratch_shapes=[
-            pltpu.VMEM((parts, NG + window - block_y, NG), jnp.float32),
+            pltpu.VMEM((parts, NG + window - block_x, NG), jnp.float32),
             pltpu.VMEM(tables.shape, tables.dtype),
-            pltpu.SemaphoreType.DMA,
+            pltpu.VMEM(last.shape[1:], last.dtype),
+            pltpu.SemaphoreType.DMA((2,)),
         ],
         compiler_params=pltpu.CompilerParams(vmem_limit_bytes=48 * 2**20),
         name="solve",
-    )(kappa, static, charge, waves, cosine_row, tables)
-
-
-def sample_kernel(window, atoms_ref, waves_ref, cosine_ref, half_ref, table_ref, out_ref):
-    slabs = atoms_ref.shape[0]
+    )(kappa, pair, static, waves, cosine_row, tables, last)
+
+
+def sample_kernel(
+    block_x, block_y, window, pair_ref, atoms_ref, waves_ref, cosine_ref, full_ref, out_ref
+):
+    bricks = atoms_ref.shape[0]
     parts = waves_ref.shape[0]
-    bricks = out_ref.shape[0] // slabs
     block = out_ref.shape[2]
-    table = (table_ref[0], table_ref[1])
-    planes = [triple(table, split(half_ref[part]), LANES) for part in range(parts)]
-    for slab in range(slabs):
-        table_x, table_yz = atom_factors(
-            atoms_ref[slab], waves_ref, cosine_ref, window, None
-        )
-        rows = slice(window * slab, window * (slab + 1))
-        values = jnp.concatenate([plane[rows] for plane in planes], axis=0)
-        along = triple(split(values), split(table_x))
-        sums = jnp.sum(along * table_yz, axis=0, keepdims=True)
-        for brick in range(bricks):
-            out_ref[slab * bricks + brick] = sums[:, block * brick : block * (brick + 1)]
-
-
-def sample(block, window, atoms, waves, cosine_row, half, table):
-    slabs, _, row_atoms = atoms.shape
+    base = 2 * block_y * pair_ref[0]
+    lanes = pl.ds(pl.multiple_of(2 * block * pair_ref[0], 128), 2 * block)
+    for brick in range(bricks):
+        fields = atoms_ref[brick, :, lanes]
+        weights = first_third(fields, waves_ref, cosine_ref, window, None)
+        start = block_x * brick
+        inside = min(window, NG - start)
+        values = []
+        for part in range(parts):
+            values.append(full_ref[part, start : start + inside, :])
+            if inside < window:
+                values.append(full_ref[part, 0 : window - inside, :])
+        values = split(jnp.concatenate(values, axis=0))
+        along = triple(values, split(second_factors(fields, base)))
+        sums = jnp.sum(along * weights, axis=0, keepdims=True)
+        for side in range(2):
+            out_ref[2 * brick + side] = sums[:, block * side : block * (side + 1)]
+
+
+def sample(block, block_x, block_y, window, pair, atoms, waves, cosine_row, full):
+    bricks = atoms.shape[0]
     parts = waves.shape[0]
+    result = jax.ShapeDtypeStruct((2 * bricks, 1, block), jnp.float32)
     return pl.pallas_call(
-        functools.partial(sample_kernel, window),
-        out_shape=jax.ShapeDtypeStruct((slabs * row_atoms // block, 1, block), jnp.float32),
-        in_specs=full_spec(5),
-        out_specs=pl.BlockSpec(memory_space=pltpu.VMEM),
+        functools.partial(sample_kernel, block_x, block_y, window),
+        grid=(1,),
+        out_shape=result,
+        in_specs=[pl.BlockSpec(memory_space=pltpu.SMEM)]
+        + whole_specs(atoms, waves, cosine_row, full),
+        out_specs=whole(result.shape),
         compiler_params=pltpu.CompilerParams(vmem_limit_bytes=48 * 2**20),
         cost_estimate=pl.CostEstimate(
-            flops=6 * slabs * row_atoms * parts * window * NG,
-            bytes_accessed=4 * half.size,
+            flops=12 * bricks * block * parts * window * NG,
+            bytes_accessed=4 * full.size,
             transcendentals=0,
         ),
         name="sample",
-    )(atoms, waves, cosine_row, half, table)
+    )(pair, atoms, waves, cosine_row, full)
 
 
 def finish_kernel(block_y, got_ref, table_ref, out_ref):
@@ -975,54 +981,48 @@
     ghosts = send_index.shape[1] // 2
     count_x = lax.axis_size("brick")
     count_y = lax.axis_size("slab")
-    devices = count_x * count_y
     block_x = NG // count_x
     block_y = NG // count_y
-    window = block_y + 8
-    parts = NG // devices
+    window = block_x + 8
+    parts = NG // (2 * count_x)
     brick = lax.axis_index("brick")
     slab = lax.axis_index("slab")
-
-    def exchange(values, axes):
-        return lax.all_to_all(values, axes, split_axis=0, concat_axis=0, tiled=True)
-
-    own, outgoing, static = collect(
-        devices,
-        (brick * block_x).astype(jnp.int32).reshape(1),
-        positions,
-        types,
-        neighbour_count,
-        send_index,
-        cell_x,
-        cell_y,
-        cell_z,
-        spline_fraction,
-    )
+    pair = (slab // 2).astype(jnp.int32).reshape(1)
+    halves = [
+        [b * count_y + 2 * p + side for b in range(count_x) for side in range(2)]
+        for p in range(count_y // 2)
+    ]
+
+    def exchange(values, axes, groups=None):
+        return lax.all_to_all(
+            values, axes, split_axis=0, concat_axis=0, tiled=True, axis_index_groups=groups
+        )
+
+    own, outgoing = collect(positions, types, neighbour_count, send_index)
     up = [(i, (i + 1) % count_x) for i in range(count_x)]
     down = [((i + 1) % count_x, i) for i in range(count_x)]
     lower = lax.ppermute(outgoing, "brick", up)
     upper = lax.ppermute(outgoing, "brick", down)
-    static = exchange(static, ("slab", "brick"))
-
-    descriptor, charge, charge_copies = networks(
-        devices,
+    descriptor, charge, fields = networks(
+        count_x * count_y,
         ghosts,
+        (slab * block_y).astype(jnp.int32).reshape(1),
         charge_base,
         own,
         lower,
         upper,
         neighbours,
         types,
-        embed_first,
-        embed_second,
-        embed_third,
+        (cell_x, cell_y, cell_z),
+        spline_fraction,
+        (embed_first, embed_second, embed_third),
         wannier_in,
         wannier_hidden,
         wannier_out,
     )
-    every_charge = exchange(charge_copies, ("slab", "brick"))
-
-    part = (brick * count_y + slab) * parts + jnp.arange(parts, dtype=jnp.int32)
+    every_field = exchange(fields, ("slab", "brick"))
+
+    part = (2 * brick + slab % 2) * parts + jnp.arange(parts, dtype=jnp.int32)
     wave = wave_of(part)
     waves = jnp.stack([wave, jnp.where(part <= NG // 2, 0, 3 * NG // 4)], axis=1)
     kappa = wave.astype(jnp.float32) * (2.0 * math.pi / NG)
@@ -1032,41 +1032,38 @@
         [squared, jnp.exp(-0.5 * squared) * jnp.where(ends, 1.0 / NG, 2.0 / NG)], axis=1
     )
     basis = real_basis()
-    swapped = basis.reshape(NG, -1, 2, block_y)[:, :, ::-1].reshape(NG, NG)
-    tables = np.concatenate([two_parts(basis), two_parts(basis.T), two_parts(swapped)])
+    tables = np.concatenate([two_parts(basis), two_parts(basis.T)])
+    last = []
+    for p in range(count_y // 2):
+        points = (2 * block_y * p + np.arange(2 * block_y + 8)) % NG
+        columns = np.zeros((NG, NG))
+        columns[:, : points.size] = basis[:, points]
+        last.append(two_parts(columns))
     cosine_row = np.cos(np.arange(128) * (2.0 * math.pi / NG)).astype(np.float32)[None]
-    sent, half, every_atom = solve(
+    cosine_row = jnp.asarray(cosine_row)
+    sent, full, every_atom = solve(
         block_x,
         block_y,
         window,
         kappa,
-        static,
-        every_charge,
+        pair,
+        every_field,
         waves,
-        jnp.asarray(cosine_row),
+        cosine_row,
         jnp.asarray(tables),
-    )
-    got = exchange(sent.reshape(devices, -1, 128), ("brick", "slab"))
-    points = (np.arange(count_y)[:, None] * block_y + np.arange(window)[None, :]) % NG
+        jnp.asarray(np.stack(last)),
+    )
+    got = exchange(sent.reshape(2 * count_x, -1, 128), ("brick", "slab"), halves)
     partial = sample(
-        atoms,
-        window,
-        every_atom,
-        waves,
-        jnp.asarray(cosine_row),
-        half,
-        jnp.asarray(two_parts(basis.T[points.reshape(-1)])),
+        atoms, block_x, block_y, window, pair, every_atom, waves, cosine_row, full
     )
     energy_short = energies(descriptor, energy_in, energy_hidden, energy_out)
-    potential_at = jnp.sum(exchange(partial, ("slab", "brick")), axis=0)
+    partial, got = lax.optimization_barrier((partial, got))
+    potential_at = jnp.sum(exchange(partial, ("brick", "slab"), halves), axis=0)
     atom_energy = energy_short + 0.5 * charge * potential_at
-    pairs = basis.reshape(-1, 2, NG).transpose(1, 0, 2)
-    ordered = np.stack([two_parts(pairs.reshape(NG, NG)), two_parts(pairs[::-1].reshape(NG, NG))])
+    pairs = basis.reshape(-1, 2, NG).transpose(1, 0, 2).reshape(NG, NG)
     potential = finish(
-        block_x,
-        block_y,
-        got.reshape(NG // 2, block_x, 128),
-        lax.dynamic_index_in_dim(jnp.asarray(ordered), slab % 2, 0, keepdims=False),
+        block_x, block_y, got.reshape(NG // 2, block_x, 128), jnp.asarray(two_parts(pairs))
     )
     return atom_energy, potential
 
@@ -1083,7 +1080,8 @@
         P("slab", "brick"),
         P(None, "slab", "brick"),
     ) + (P(),) * 10
-    fits = 2 * (NG // mesh.shape["slab"]) == 128 and (NG // 2) % mesh.size == 0
+    bricks, slabs = mesh.shape["brick"], mesh.shape["slab"]
+    fits = 2 * NG == 128 * slabs and slabs % 2 == 0 and NG % (4 * bricks) == 0
     return jax.shard_map(
         per_device if fits else per_device_general,
         mesh=mesh,

time: 153 us -> 124 us (0.81)
  waiting for transfers between devices: 59.9 us -> 32.8 us
  blocking collectives: 9.37 us -> 0 us
  Pallas kernels: 49.7 us -> 54.1 us
  local copies, waits for them, and re-layouts: 15.4 us -> 19.3 us
    all_to_all x3, waiting for transfers between devices: 58.3 us -> 28.6 us  [exchange(): lax.all_to_all(values, axes, split_axis=0, concat_axis=0, tiled=True, axi...]
    all_to_all x1 -> x0, blocking collectives: 9.37 us -> none  [exchange(): return lax.all_to_all(values, axes, split_axis=0, concat_axis=0, tiled=True)]
    pallas_call x1, Pallas kernels: 16.7 us -> 24.9 us  [solve(): pl.pallas_call(functools.partial(solve_kernel, block_x, block_y, window),...]
    unnamed x38 -> x52, local copies, waits for them, and re-layouts: 13.6 us -> 19.1 us
    pallas_call x4, Pallas kernels: 29.3 us -> 25.5 us  [the longest x1 16.5 us: networks(): pl.pallas_call(functools.partial(network_kernel, ghosts), grid=(1,), out_...]
    squeeze x1 -> x0, local copies, waits for them, and re-layouts: 1.67 us -> none  [per_device(): lax.dynamic_index_in_dim(jnp.asarray(ordered), slab % 2, 0, keepdims=False)]
    ppermute x1, waiting for transfers between devices: 0.04 us -> 1.57 us  [per_device(): upper = lax.ppermute(outgoing, 'brick', down)]
  transfers between devices with their start and end apart: 5 -> 5, of which waited for: 4 -> 4; matrix products, arithmetic and copies ran while one was open for 2% -> 0% of each run, Pallas kernels for 1% -> 9%
where the time goes in v2:
time: 124 us; the launch traced here: 123 us
  Pallas kernels  54.1 us (44%)
  waiting for transfers between devices  32.8 us (26%)
  local copies, waits for them, and re-layouts  19.3 us (16%)
  starting transfers between devices  15.9 us (13%)
    all_to_all x3, waiting for transfers between devices, exchange(): lax.all_to_all(values, axes, split_axis=0, concat_axis=0, tiled=True, axi...  28.6 us
    pallas_call x1, Pallas kernels, solve(): pl.pallas_call(functools.partial(solve_kernel, block_x, block_y, window),...  24.9 us
    unnamed x52, local copies, waits for them, and re-layouts  19.1 us
    pallas_call x1, Pallas kernels, networks(): pl.pallas_call(functools.partial(network_kernel, ghosts), grid=(1,), out_...  16.5 us
    all_to_all x3, starting transfers between devices, exchange(): lax.all_to_all(values, axes, split_axis=0, concat_axis=0, tiled=True, axi...  12.6 us
    pallas_call x1, Pallas kernels, sample(): pl.pallas_call(functools.partial(sample_kernel, block_x, block_y, window)...  5.74 us
    pallas_call x1, Pallas kernels, finish(): pl.pallas_call(functools.partial(finish_kernel, block_y), grid=(block_x /...  3.67 us
    ppermute x1, starting transfers between devices, per_device(): upper = lax.ppermute(outgoing, 'brick', down)  3.33 us
  transfers between devices with their start and end apart: 5, of which 4 were waited for; matrix products, arithmetic and copies ran while one was open for 0% of the time, Pallas kernels for 9%

profile of v2, /device:TPU:0, one launch (start us, length us, event | category | flops | bytes accessed | tf_op | source)
XLA Modules:
  0.0 123.4 jit_solution(17206415749561998546)
XLA Ops:
  0.6 0.0 copy-start.22
  0.6 1.4 %collect_atoms.1 = (f32[8,256]{1,0:T(8,128)}, f32[8,256]{1,0:T(8,128)}) custom-call(f32[3,1,192]{2,1,0:T(1,128)} %positions_ref.1, s32[1,192]{1,0:T(1,128)} %types_ref.3, s32[1,192]{1,0:T(1,128)} %count_ref.1, s32[1,192]{1,0:T(1,128)} %send_ref.1), custom_call_target="tpu_custom_call" | custom-call | tf_op jit(solution)/shard_map/collect_atoms/pallas_call | solution.py:330
  2.1 3.3 %collective-permute-start.1 = (f32[8,256]{1,0:T(8,128)}, f32[8,256]{1,0:T(8,128)S(1)}, u32[]{:S(2)}, u32[]{:S(2)}) collective-permute-start(f32[8,256]{1,0:T(8,128)} %get-tuple-element.13), channel_id=1, source_target_pairs={{4,0},{8,4},{12,8},{16,12},{20,16},{24,20},{28,24},{0,28},{5,1},{9... | collective-permute-start | bytes 24584 | tf_op jit(solution)/shard_map/ppermute | solution.py:1005
  5.4 0.0 collective-permute-start
  5.4 1.6 %collective-permute-done.1.upper_ref = f32[8,256]{1,0:T(8,128)S(1)} collective-permute-done((f32[8,256]{1,0:T(8,128)}, f32[8,256]{1,0:T(8,128)S(1)}, u32[]{:S(2)}, u32[]{:S(2)}) %collective-permute-start.1) | collective-permute-done | bytes 8224 | tf_op jit(solution)/shard_map/ppermute | solution.py:1005
  7.0 2.6 %collective-permute-done.lower_ref = f32[8,256]{1,0:T(8,128)S(1)} collective-permute-done((f32[8,256]{1,0:T(8,128)}, f32[8,256]{1,0:T(8,128)S(1)}, u32[]{:S(2)}, u32[]{:S(2)}) %collective-permute-start) | collective-permute-done | bytes 8224 | tf_op jit(solution)/shard_map/ppermute | solution.py:1004
  9.6 0.0 copy-start.1
  9.6 1.4 %copy-done.1 = f32[1600,240]{0,1:T(8,128)S(1)} copy-done((f32[1600,240]{0,1:T(8,128)S(1)}, f32[1600,240]{0,1:T(8,128)}, u32[]{:S(2)}) %copy-start.1) | copy-done | bytes 1536024
  11.0 0.0 copy-start.5
  11.0 1.0 copy-done.5
  12.0 0.0 copy-start.8
  12.0 0.8 copy-done.8
  12.9 0.0 copy-start.9
  12.9 0.7 copy-done.9
  13.6 0.0 copy-start.10
  13.6 0.7 copy-done.10
  14.3 0.0 copy-start.11
  14.3 0.7 copy-done.11
  15.0 0.0 copy-start.12
  15.0 0.7 copy-done.12
  15.7 0.0 copy-start.13
  15.7 0.7 copy-done.13
  16.4 0.0 copy-start.14
  16.4 0.7 copy-done.14
  17.1 0.0 copy-start.15
  17.1 0.7 copy-done.15
  17.8 0.0 copy-start.16
  17.8 0.7 copy-done.16
  18.4 0.0 copy-start.17
  18.4 0.7 copy-done.17
  19.1 0.0 copy-start.18
  19.1 0.7 copy-done.18
  19.8 0.0 copy-start.19
  19.8 0.7 copy-done.19
  20.5 0.0 copy-start.21
  20.5 0.7 copy-done.21
  21.1 16.5 %networks.1 = (f32[192,1600]{1,0:T(8,128)S(1)}, f32[1,192]{1,0:T(1,128)S(1)}, f32[32,8,192]{2,1,0:T(8,128)}) custom-call(s32[1]{0:T(128)} %bitcast.base_ref, f32[2]{0:T(128)S(1)} %copy-done.21, f32[8,256]{1,0:T(8,128)S(1)} %copy-done.12, f32[8,256]{1,0:T(8,128)S(1)} %collective-permute-done.lower_ref, f32[8,256]{1,0:T(8,128)S(1)} %collective-permute-done.1.upper_ref, ...), custom_call_target="tpu_custom_call" | custom-call | tf_op jit(solution)/shard_map/networks/pallas_call | solution.py:625
  37.6 4.1 %all-to-all-start = ((f32[32,8,192]{2,1,0:T(8,128)}), f32[32,8,192]{2,1,0:T(8,128)S(1)}, u32[]{:S(2)}, u32[]{:S(2)}) async-start(f32[32,8,192]{2,1,0:T(8,128)} %get-tuple-element.16), calls=%async_computation | async-start | bytes 524288 | tf_op jit(solution)/shard_map/all_to_all | solution.py:997
  41.8 0.1 copy.27.waves_ref
  41.9 0.1 copy.26.kappa_ref
  42.0 10.2 %all-to-all-done.static_ref = f32[32,8,192]{2,1,0:T(8,128)S(1)} async-done(((f32[32,8,192]{2,1,0:T(8,128)}), f32[32,8,192]{2,1,0:T(8,128)S(1)}, u32[]{:S(2)}, u32[]{:S(2)}) %all-to-all-start) | async-done | bytes 196640 | tf_op jit(solution)/shard_map/all_to_all | solution.py:997
  52.2 0.0 copy-done.22
  52.2 0.0 copy-done.3
  52.2 0.0 copy-done.4
  52.2 24.9 %solve.1 = (f32[16,8,32,128]{3,2,1,0:T(8,128)S(1)}, f32[16,256,256]{2,1,0:T(8,128)}, f32[8,8,768]{2,1,0:T(8,128)S(1)}) custom-call(f32[16,2]{1,0:T(8,128)S(1)} %copy.26.kappa_ref, s32[1]{0:T(128)} %bitcast.7.pair_ref, f32[32,8,192]{2,1,0:T(8,128)S(1)} %all-to-all-done.static_ref, s32[16,2]{1,0:T(8,128)S(1)} %copy.27.waves_ref, f32[1,128]{1,0:T(1,128)S(1)} %copy-done.22, ...), custom_call_target="tpu_custom_call" | custom-call | tf_op jit(solution)/shard_map/solve/pallas_call | solution.py:845
  77.1 0.0 copy-start
  77.2 1.3 %copy-done = f32[16,8,32,128]{3,2,1,0:T(8,128)} copy-done((f32[16,8,32,128]{3,2,1,0:T(8,128)}, f32[16,8,32,128]{3,2,1,0:T(8,128)S(1)}, u32[]{:S(2)}) %copy-start) | copy-done | bytes 2097176
  78.5 0.7 copy-done.24
  79.1 3.9 %all-to-all-start.1 = ((f32[16,256,128]{2,1,0:T(8,128)}), f32[16,256,128]{2,1,0:T(8,128)S(1)}, u32[]{:S(2)}, u32[]{:S(2)}) async-start(f32[16,256,128]{2,1,0:T(8,128)} %bitcast.13), calls=%async_computation.1 | async-start | bytes 4194304 | tf_op jit(solution)/shard_map/all_to_all | solution.py:997
  83.1 0.0 copy-start.23
  83.1 2.2 %copy-done.23 = f32[16,256,256]{2,1,0:T(8,128)S(1)} copy-done((f32[16,256,256]{2,1,0:T(8,128)S(1)}, f32[16,256,256]{2,1,0:T(8,128)}, u32[]{:S(2)}) %copy-start.23) | copy-done | bytes 4194328
  85.3 0.9 copy-done.25
  86.2 5.7 %sample.1 = f32[16,1,192]{2,1,0:T(1,128)} custom-call(s32[1]{0:T(128)} %bitcast.7.pair_ref, f32[8,8,768]{2,1,0:T(8,128)S(1)} %copy-done.25, s32[16,2]{1,0:T(8,128)S(1)} %copy.27.waves_ref, f32[1,128]{1,0:T(1,128)S(1)} %copy-done.22, f32[16,256,256]{2,1,0:T(8,128)S(1)} %copy-done.23), custom_call_target="tpu_custom_call" | custom-call | flops 3019898880 | bytes 4194304 | tf_op jit(solution)/shard_map/sample/pallas_call | solution.py:901
  92.0 18.4 %all-to-all-done.1 = f32[16,256,128]{2,1,0:T(8,128)S(1)} async-done(((f32[16,256,128]{2,1,0:T(8,128)}), f32[16,256,128]{2,1,0:T(8,128)S(1)}, u32[]{:S(2)}, u32[]{:S(2)}) %all-to-all-start.1) | async-done | bytes 2097184 | tf_op jit(solution)/shard_map/all_to_all | solution.py:997
  110.4 4.5 %all-to-all-start.2 = ((f32[16,1,192]{2,1,0:T(1,128)}), f32[16,1,192]{2,1,0:T(1,128)S(1)}, u32[]{:S(2)}, u32[]{:S(2)}) async-start(f32[16,1,192]{2,1,0:T(1,128)} %sample.1), calls=%async_computation.2 | async-start | bytes 32768 | tf_op jit(solution)/shard_map/all_to_all | solution.py:997
  114.9 0.0 copy-done.20
  114.9 0.0 copy-start.2
  114.9 1.4 %copy-done.2 = f32[1600,240]{0,1:T(8,128)S(1)} copy-done((f32[1600,240]{0,1:T(8,128)S(1)}, f32[1600,240]{0,1:T(8,128)}, u32[]{:S(2)}) %copy-start.2) | copy-done | bytes 1536024
  116.3 1.0 copy-done.6
  117.3 1.8 %energies.1 = f32[1,192]{1,0:T(1,128)S(1)} custom-call(f32[192,1600]{1,0:T(8,128)S(1)} %get-tuple-element.14.descriptor_ref, f32[240,1600]{1,0:T(8,128)S(1)} %bitcast.15, f32[2,240,240]{2,1,0:T(8,128)S(1)} %copy-done.6, f32[1,240]{1,0:T(1,128)S(1)} %bitcast.18), custom_call_target="tpu_custom_call" | custom-call | flops 442368000 | bytes 1536000 | tf_op jit(solution)/shard_map/energies/pallas_call | solution.py:660
  119.2 0.0 copy-done.7
  119.2 3.7 %finish.1 = f32[32,64,256]{2,1,0:T(8,128)} custom-call(f32[128,32,128]{2,1,0:T(8,128)S(1)} %bitcast.12, bf16[2,256,256]{2,1,0:T(8,128)(2,1)S(1)} %copy-done.7), custom_call_target="tpu_custom_call" | custom-call | tf_op jit(solution)/shard_map/finish/pallas_call | solution.py:931
  122.8 0.0 all-to-all-done.2
  122.9 0.6 multiply_add_fusion
  (12 shorter events, 0.1 us)
Async XLA Ops:
  0.6 51.6 %copy-start.22 = (f32[1,128]{1,0:T(1,128)S(1)}, f32[1,128]{1,0:T(1,128)}, u32[]{:S(2)}) copy-start(f32[1,128]{1,0:T(1,128)} %constant.68.clone.cosine_ref) | copy-start | bytes 1540
  2.1 4.9 %collective-permute-start.1 = (f32[8,256]{1,0:T(8,128)}, f32[8,256]{1,0:T(8,128)S(1)}, u32[]{:S(2)}, u32[]{:S(2)}) collective-permute-start(f32[8,256]{1,0:T(8,128)} %get-tuple-element.13), channel_id=1, source_target_pairs={{4,0},{8,4},{12,8},{16,12},{20,16},{24,20},{28,24},{0,28},{5,1},{9... | collective-permute-start | bytes 24584 | tf_op jit(solution)/shard_map/ppermute | solution.py:1005
  5.4 4.2 %collective-permute-start = (f32[8,256]{1,0:T(8,128)}, f32[8,256]{1,0:T(8,128)S(1)}, u32[]{:S(2)}, u32[]{:S(2)}) collective-permute-start(f32[8,256]{1,0:T(8,128)} %get-tuple-element.13), channel_id=1, source_target_pairs={{0,4},{4,8},{8,12},{12,16},{16,20},{20,24},{24,28},{28,0},{1,5},{5... | collective-permute-start | bytes 24584 | tf_op jit(solution)/shard_map/ppermute | solution.py:1004
  9.6 1.4 %copy-start.1 = (f32[1600,240]{0,1:T(8,128)S(1)}, f32[1600,240]{0,1:T(8,128)}, u32[]{:S(2)}) copy-start(f32[1600,240]{0,1:T(8,128)} %param.39) | copy-start | bytes 4608004
  11.0 1.0 copy-start.5
  12.0 0.8 copy-start.8
  12.9 0.7 copy-start.9
  13.6 0.7 copy-start.10
  14.3 0.7 copy-start.11
  15.0 0.7 copy-start.12
  15.7 0.7 copy-start.13
  16.4 0.7 copy-start.14
  17.1 0.7 copy-start.15
  17.8 0.7 copy-start.16
  18.4 0.7 copy-start.17
  19.1 0.7 copy-start.18
  19.8 0.7 copy-start.19
  20.5 0.7 copy-start.21
  21.1 31.1 %copy-start.3 = (bf16[2,2,256,256]{3,2,1,0:T(8,128)(2,1)S(1)}, bf16[2,2,256,256]{3,2,1,0:T(8,128)(2,1)}, u32[]{:S(2)}) copy-start(bf16[2,2,256,256]{3,2,1,0:T(8,128)(2,1)} %constant.70.clone.last_hbm) | copy-start | bytes 1572868
  21.1 31.1 %copy-start.4 = (bf16[4,256,256]{2,1,0:T(8,128)(2,1)S(1)}, bf16[4,256,256]{2,1,0:T(8,128)(2,1)}, u32[]{:S(2)}) copy-start(bf16[4,256,256]{2,1,0:T(8,128)(2,1)} %constant.69.clone.tables_hbm) | copy-start | bytes 1572868
  37.6 14.6 %all-to-all-start = ((f32[32,8,192]{2,1,0:T(8,128)}), f32[32,8,192]{2,1,0:T(8,128)S(1)}, u32[]{:S(2)}, u32[]{:S(2)}) async-start(f32[32,8,192]{2,1,0:T(8,128)} %get-tuple-element.16), calls=%async_computation | async-start | bytes 524288 | tf_op jit(solution)/shard_map/all_to_all | solution.py:997
  77.1 1.3 %copy-start = (f32[16,8,32,128]{3,2,1,0:T(8,128)}, f32[16,8,32,128]{3,2,1,0:T(8,128)S(1)}, u32[]{:S(2)}) copy-start(f32[16,8,32,128]{3,2,1,0:T(8,128)S(1)} %get-tuple-element.19) | copy-start | bytes 6291460
  78.5 0.7 copy-start.24
  79.1 31.2 %all-to-all-start.1 = ((f32[16,256,128]{2,1,0:T(8,128)}), f32[16,256,128]{2,1,0:T(8,128)S(1)}, u32[]{:S(2)}, u32[]{:S(2)}) async-start(f32[16,256,128]{2,1,0:T(8,128)} %bitcast.13), calls=%async_computation.1 | async-start | bytes 4194304 | tf_op jit(solution)/shard_map/all_to_all | solution.py:997
  83.1 2.2 %copy-start.23 = (f32[16,256,256]{2,1,0:T(8,128)S(1)}, f32[16,256,256]{2,1,0:T(8,128)}, u32[]{:S(2)}) copy-start(f32[16,256,256]{2,1,0:T(8,128)} %get-tuple-element.18.full_ref) | copy-start | bytes 12582916
  85.3 0.9 copy-start.25
  86.2 28.7 %copy-start.20 = (f32[240]{0:T(256)S(1)}, f32[240]{0:T(256)}, u32[]{:S(2)}) copy-start(f32[240]{0:T(256)} %param.38) | copy-start | bytes 2884
  110.4 12.5 %all-to-all-start.2 = ((f32[16,1,192]{2,1,0:T(1,128)}), f32[16,1,192]{2,1,0:T(1,128)S(1)}, u32[]{:S(2)}, u32[]{:S(2)}) async-start(f32[16,1,192]{2,1,0:T(1,128)} %sample.1), calls=%async_computation.2 | async-start | bytes 32768 | tf_op jit(solution)/shard_map/all_to_all | solution.py:997
  114.9 1.4 %copy-start.2 = (f32[1600,240]{0,1:T(8,128)S(1)}, f32[1600,240]{0,1:T(8,128)}, u32[]{:S(2)}) copy-start(f32[1600,240]{0,1:T(8,128)} %param.36) | copy-start | bytes 4608004
  116.3 1.0 copy-start.6
  117.3 1.8 %copy-start.7 = (bf16[2,256,256]{2,1,0:T(8,128)(2,1)S(1)}, bf16[2,256,256]{2,1,0:T(8,128)(2,1)}, u32[]{:S(2)}) copy-start(bf16[2,256,256]{2,1,0:T(8,128)(2,1)} %constant.71.clone.table_ref) | copy-start | bytes 786436

commit v3 on v2

--- a/solution.py
+++ b/solution.py
@@ -12,6 +12,7 @@
 
 NG = 256
 AXIS = 16
+VMEM_BYTES = 60 * 2**20
 
 
 HIGH = lax.Precision.HIGHEST
@@ -333,6 +334,7 @@
         out_shape=[result, result],
         in_specs=whole_specs(*arrays),
         out_specs=whole_specs(result, result),
+        compiler_params=pltpu.CompilerParams(vmem_limit_bytes=VMEM_BYTES),
         name="collect_atoms",
     )(*arrays)
 
@@ -641,7 +643,7 @@
             pltpu.VMEM(weight_hidden.shape, jnp.float32),
             pltpu.SemaphoreType.DMA((3,)),
         ],
-        compiler_params=pltpu.CompilerParams(vmem_limit_bytes=32 * 2**20),
+        compiler_params=pltpu.CompilerParams(vmem_limit_bytes=VMEM_BYTES),
         name="networks",
     )(base, charge_base, *blocks, weight_in.T, weight_hidden, weight_out)
 
@@ -663,7 +665,7 @@
         out_shape=result,
         in_specs=whole_specs(*arrays),
         out_specs=whole(result.shape),
-        compiler_params=pltpu.CompilerParams(vmem_limit_bytes=32 * 2**20),
+        compiler_params=pltpu.CompilerParams(vmem_limit_bytes=VMEM_BYTES),
         cost_estimate=pl.CostEstimate(
             flops=6 * atoms * desc * width, bytes_accessed=4 * desc * width, transcendentals=0
         ),
@@ -739,7 +741,54 @@
     return jnp.where(index <= NG // 2, index, index - NG // 2)
 
 
-def solve_kernel(
+def damping(index):
+    kappa = wave_of(index).astype(jnp.float32) * (2.0 * math.pi / NG)
+    squared = kappa * kappa
+    ends = (index == 0) | (index == NG // 2)
+    return squared, jnp.exp(-0.5 * squared) * jnp.where(ends, 1.0 / NG, 2.0 / NG)
+
+
+def transform(planes, kappa_ref, first_part, tables_ref, last_ref):
+    count = len(planes)
+    basis = (tables_ref[0], tables_ref[1])
+    turned = (tables_ref[2], tables_ref[3])
+    last = (last_ref[0], last_ref[1])
+    square_x, damp_x = damping(lax.broadcasted_iota(jnp.int32, (NG, 1), 0))
+    square_y, damp_y = damping(lax.broadcasted_iota(jnp.int32, (1, NG), 1))
+    square_xy = square_x + square_y
+    damp_xy = damp_x * damp_y
+    columns = [slice(NG * part, NG * (part + 1)) for part in range(count)]
+    first = triple(basis, split(jnp.concatenate(planes, axis=1)))
+    first = jnp.concatenate([first[:, column] for column in columns], axis=0)
+    both = triple(split(first), turned)
+    scaled = []
+    for part in range(count):
+        squared = square_xy + kappa_ref[first_part + part, 0]
+        root = jnp.where(squared == 0.0, 1.0, 0.0)
+        green = (1.0 - root) * (damp_xy * kappa_ref[first_part + part, 1]) / (squared + root)
+        scaled.append(both[columns[part]] * green)
+    back = triple(turned, split(jnp.concatenate(scaled, axis=1)))
+    back = jnp.concatenate([back[:, column] for column in columns], axis=0)
+    return triple(split(back), last)
+
+
+def send_blocks(full, block_x, block_y, put):
+    low_lanes = lax.broadcasted_iota(jnp.int32, (NG, 128), 1) < block_y
+    for pair in range(full.shape[0] // (2 * NG)):
+        even = full[2 * NG * pair : 2 * NG * pair + NG, 0:128]
+        odd = full[2 * NG * pair + NG : 2 * NG * (pair + 1), 0:128]
+        blocks = [
+            jnp.where(low_lanes, even, pltpu.roll(odd, block_y, 1)),
+            jnp.where(low_lanes, pltpu.roll(even, block_y, 1), odd),
+        ]
+        for brick in range(NG // block_x):
+            for side in range(2):
+                for group in range(block_x // 8):
+                    start = block_x * brick + 8 * group
+                    put(pair, brick, side, group, blocks[side][start : start + 8])
+
+
+def spread_kernel(
     block_x,
     block_y,
     window,
@@ -753,6 +802,7 @@
     sent_ref,
     full_ref,
     atoms_ref,
+    later_hbm,
     grid_ref,
     tables_ref,
     last_ref,
@@ -762,7 +812,11 @@
     bricks = NG // block_x
     parts = waves_ref.shape[0]
     block = static_ref.shape[2]
+    count = full_ref.shape[0]
     step = pl.program_id(0)
+    store = pltpu.make_async_copy(
+        grid_ref.at[pl.ds(parts // 2, parts // 2), pl.ds(0, NG)], later_hbm, semaphores.at[2]
+    )
 
     @pl.when(step == 0)
     def _():
@@ -787,94 +841,115 @@
         extra = window - block_x
         for part in range(parts):
             grid_ref[part, 0:extra, :] += grid_ref[part, NG : NG + extra, :]
+        store.start()
         for fetch in fetches:
             fetch.wait()
 
-    basis = (tables_ref[0], tables_ref[1])
-    turned = (tables_ref[2], tables_ref[3])
-    last = (last_ref[0], last_ref[1])
-    index_x = lax.broadcasted_iota(jnp.int32, (NG, 1), 0)
-    index_y = lax.broadcasted_iota(jnp.int32, (1, NG), 1)
-
-    def factors(index):
-        kappa = wave_of(index).astype(jnp.float32) * (2.0 * math.pi / NG)
-        squared = kappa * kappa
-        ends = (index == 0) | (index == NG // 2)
-        return squared, jnp.exp(-0.5 * squared) * jnp.where(ends, 1.0 / NG, 2.0 / NG)
-
-    square_x, damp_x = factors(index_x)
-    square_y, damp_y = factors(index_y)
-    square_xy = square_x + square_y
-    damp_xy = damp_x * damp_y
-
-    planes = jnp.concatenate([grid_ref[2 * step + part, 0:NG, :] for part in range(2)], axis=1)
-    first = triple(basis, split(planes))
-    first = jnp.concatenate([first[:, 0:NG], first[:, NG:]], axis=0)
-    both = triple(split(first), turned)
-    scaled = []
-    for part in range(2):
-        squared = square_xy + kappa_ref[2 * step + part, 0]
-        root = jnp.where(squared == 0.0, 1.0, 0.0)
-        green = (1.0 - root) * (damp_xy * kappa_ref[2 * step + part, 1]) / (squared + root)
-        scaled.append(both[NG * part : NG * (part + 1)] * green)
-    back = triple(turned, split(jnp.concatenate(scaled, axis=1)))
-    back = jnp.concatenate([back[:, 0:NG], back[:, NG:]], axis=0)
-    full = triple(split(back), last)
-    full_ref[0] = full[0:NG]
-    full_ref[1] = full[NG:]
-    low_lanes = lax.broadcasted_iota(jnp.int32, (NG, 128), 1) < block_y
-    even = full[0:NG, 0:128]
-    odd = full[NG:, 0:128]
-    blocks = [
-        jnp.where(low_lanes, even, pltpu.roll(odd, block_y, 1)),
-        jnp.where(low_lanes, pltpu.roll(even, block_y, 1), odd),
-    ]
-    for brick in range(bricks):
-        rows = slice(block_x * brick, block_x * (brick + 1))
-        for side in range(2):
-            sent_ref[2 * brick + side, 0] = blocks[side][rows]
-
-
-def solve(block_x, block_y, window, kappa, pair, static, waves, cosine_row, tables, last):
+    planes = [grid_ref[count * step + part, 0:NG, :] for part in range(count)]
+    full = transform(planes, kappa_ref, count * step, tables_ref, last_ref)
+    for part in range(count):
+        full_ref[part] = full[NG * part : NG * (part + 1)]
+
+    def put(pair, brick, side, group, tile):
+        sent_ref[2 * brick + side, group, pair] = tile
+
+    send_blocks(full, block_x, block_y, put)
+
+    @pl.when(step == pl.num_programs(0) - 1)
+    def _():
+        store.wait()
+
+
+def spread_and_solve(
+    block_x, block_y, window, kappa, pair, static, waves, cosine_row, tables, last
+):
     devices, _, atoms = static.shape
     slabs = NG // block_y
     bricks = NG // block_x
     parts = waves.shape[0]
+    pairs = parts // 4
+    count = 4
     anywhere = pl.BlockSpec(memory_space=pl.ANY)
     scalars = pl.BlockSpec(memory_space=pltpu.SMEM)
+    sent_block = (2 * bricks, block_x // 8, count // 2, 8, 128)
     return pl.pallas_call(
-        functools.partial(solve_kernel, block_x, block_y, window),
-        grid=(parts // 2,),
+        functools.partial(spread_kernel, block_x, block_y, window),
+        grid=(parts // 2 // count,),
         out_shape=[
-            jax.ShapeDtypeStruct((2 * bricks, parts // 2, block_x, 128), jnp.float32),
-            jax.ShapeDtypeStruct((parts, NG, NG), jnp.float32),
+            jax.ShapeDtypeStruct((2 * bricks, block_x // 8, pairs, 8, 128), jnp.float32),
+            jax.ShapeDtypeStruct((parts // 2, NG, NG), jnp.float32),
             jax.ShapeDtypeStruct((bricks, 8, slabs * atoms), jnp.float32),
+            jax.ShapeDtypeStruct((parts // 2, NG, NG), jnp.float32),
         ],
         in_specs=[scalars, scalars]
         + whole_specs(static, waves, cosine_row)
         + [anywhere, anywhere],
         out_specs=[
-            pl.BlockSpec((2 * bricks, 1, block_x, 128), lambda step: (0, step, 0, 0)),
-            pl.BlockSpec((2, NG, NG), lambda step: (step, 0, 0)),
+            pl.BlockSpec(sent_block, lambda step: (0, 0, step, 0, 0)),
+            pl.BlockSpec((count, NG, NG), lambda step: (step, 0, 0)),
             whole((bricks, 8, slabs * atoms)),
+            anywhere,
         ],
         scratch_shapes=[
             pltpu.VMEM((parts, NG + window - block_x, NG), jnp.float32),
             pltpu.VMEM(tables.shape, tables.dtype),
             pltpu.VMEM(last.shape[1:], last.dtype),
-            pltpu.SemaphoreType.DMA((2,)),
+            pltpu.SemaphoreType.DMA((3,)),
         ],
-        compiler_params=pltpu.CompilerParams(vmem_limit_bytes=48 * 2**20),
-        name="solve",
+        compiler_params=pltpu.CompilerParams(vmem_limit_bytes=VMEM_BYTES),
+        name="spread_and_solve",
     )(kappa, pair, static, waves, cosine_row, tables, last)
 
 
 def sample_kernel(
-    block_x, block_y, window, pair_ref, atoms_ref, waves_ref, cosine_ref, full_ref, out_ref
+    block_x,
+    block_y,
+    window,
+    kappa_ref,
+    pair_ref,
+    atoms_ref,
+    waves_ref,
+    cosine_ref,
+    tables_hbm,
+    last_hbm,
+    later_hbm,
+    early_hbm,
+    sent_ref,
+    later_ref,
+    full_ref,
+    tables_ref,
+    last_ref,
+    semaphores,
 ):
     bricks = atoms_ref.shape[0]
     parts = waves_ref.shape[0]
-    block = out_ref.shape[2]
+    half = parts // 2
+    count = 4
+    block = atoms_ref.shape[2] * block_y // NG
+    fetches = [
+        pltpu.make_async_copy(tables_hbm, tables_ref, semaphores.at[0]),
+        pltpu.make_async_copy(last_hbm.at[pair_ref[0]], last_ref, semaphores.at[1]),
+        pltpu.make_async_copy(later_hbm, later_ref, semaphores.at[2]),
+        pltpu.make_async_copy(early_hbm, full_ref.at[pl.ds(0, half)], semaphores.at[3]),
+    ]
+    for fetch in fetches:
+        fetch.start()
+    for fetch in fetches[:3]:
+        fetch.wait()
+    pairs = half // 2
+    for step in range(half // count):
+        planes = [later_ref[count * step + part] for part in range(count)]
+        full = transform(planes, kappa_ref, half + count * step, tables_ref, last_ref)
+        for part in range(count):
+            full_ref[half + count * step + part] = full[NG * part : NG * (part + 1)]
+
+        def put(pair, brick, side, group, tile):
+            sent_ref[2 * brick + side, pairs * group + count // 2 * step + pair] = tile
+
+        send_blocks(full, block_x, block_y, put)
+    fetches[3].wait()
+
+    extra = sent_ref.shape[1] - 1
     base = 2 * block_y * pair_ref[0]
     lanes = pl.ds(pl.multiple_of(2 * block * pair_ref[0], 128), 2 * block)
     for brick in range(bricks):
@@ -891,55 +966,91 @@
         along = triple(values, split(second_factors(fields, base)))
         sums = jnp.sum(along * weights, axis=0, keepdims=True)
         for side in range(2):
-            out_ref[2 * brick + side] = sums[:, block * side : block * (side + 1)]
-
-
-def sample(block, block_x, block_y, window, pair, atoms, waves, cosine_row, full):
+            row = sums[:, block * side : block * (side + 1)]
+            sent_ref[2 * brick + side, extra] = jnp.zeros((8, 128), jnp.float32)
+            sent_ref[2 * brick + side, extra, 0:1, :] = row[:, 0:128]
+            sent_ref[2 * brick + side, extra, 1:2, 0 : block - 128] = row[:, 128:block]
+
+
+def solve_and_sample(
+    block_x, block_y, window, kappa, pair, atoms, waves, cosine_row, tables, last, later, early
+):
     bricks = atoms.shape[0]
     parts = waves.shape[0]
-    result = jax.ShapeDtypeStruct((2 * bricks, 1, block), jnp.float32)
+    pairs = parts // 4
+    anywhere = pl.BlockSpec(memory_space=pl.ANY)
+    scalars = pl.BlockSpec(memory_space=pltpu.SMEM)
+    result = jax.ShapeDtypeStruct((2 * bricks, block_x // 8 * pairs + 1, 8, 128), jnp.float32)
     return pl.pallas_call(
         functools.partial(sample_kernel, block_x, block_y, window),
         grid=(1,),
         out_shape=result,
-        in_specs=[pl.BlockSpec(memory_space=pltpu.SMEM)]
-        + whole_specs(atoms, waves, cosine_row, full),
+        in_specs=[scalars, scalars] + whole_specs(atoms, waves, cosine_row) + [anywhere] * 4,
         out_specs=whole(result.shape),
-        compiler_params=pltpu.CompilerParams(vmem_limit_bytes=48 * 2**20),
+        scratch_shapes=[
+            pltpu.VMEM((parts // 2, NG, NG), jnp.float32),
+            pltpu.VMEM((parts, NG, NG), jnp.float32),
+            pltpu.VMEM(tables.shape, tables.dtype),
+            pltpu.VMEM(last.shape[1:], last.dtype),
+            pltpu.SemaphoreType.DMA((4,)),
+        ],
+        compiler_params=pltpu.CompilerParams(vmem_limit_bytes=VMEM_BYTES),
         cost_estimate=pl.CostEstimate(
-            flops=12 * bricks * block * parts * window * NG,
-            bytes_accessed=4 * full.size,
-            transcendentals=0,
+            flops=24 * parts * NG * NG * NG, bytes_accessed=4 * early.size, transcendentals=0
         ),
-        name="sample",
-    )(pair, atoms, waves, cosine_row, full)
-
-
-def finish_kernel(block_y, got_ref, table_ref, out_ref):
+        name="solve_and_sample",
+    )(kappa, pair, atoms, waves, cosine_row, tables, last, later, early)
+
+
+def finish_kernel(
+    block_y, early_ref, later_ref, sums_ref, short_ref, charge_ref, table_ref, out_ref, energy_ref
+):
+    atoms = short_ref.shape[1]
     table = (table_ref[0], table_ref[1])
-    rows = []
-    for line in range(got_ref.shape[1]):
-        turned = got_ref[:, line, :].T
-        rows.append(jnp.concatenate([turned[0:block_y], turned[block_y:]], axis=1))
-    result = triple(split(jnp.concatenate(rows, axis=0)), table)
-    for line in range(got_ref.shape[1]):
+    lines = early_ref.shape[3]
+    rows = early_ref.shape[0] * early_ref.shape[2]
+    early = early_ref.reshape(rows, lines, 128)
+    later = later_ref.reshape(rows, lines, 128)
+    pieces = []
+    for line in range(lines):
+        turned = jnp.concatenate([early[:, line, :], later[:, line, :]], axis=0).T
+        pieces.append(jnp.concatenate([turned[0:block_y], turned[block_y:]], axis=1))
+    result = triple(split(jnp.concatenate(pieces, axis=0)), table)
+    for line in range(lines):
         out_ref[line] = result[block_y * line : block_y * (line + 1)]
 
-
-def finish(block_x, block_y, got, table):
-    step = 8
+    @pl.when(pl.program_id(0) == 0)
+    def _():
+        total = jnp.sum(sums_ref[:, 0], axis=0)
+        potential_at = jnp.concatenate([total[0:1, :], total[1:2, 0 : atoms - 128]], axis=1)
+        energy_ref[...] = short_ref[...] + 0.5 * charge_ref[...] * potential_at
+
+
+def finish(block_x, block_y, early, later, short, charge, table):
+    bricks2, groups, pairs = early.shape[:3]
+    atoms = short.shape[1]
     return pl.pallas_call(
         functools.partial(finish_kernel, block_y),
-        grid=(block_x // step,),
-        out_shape=jax.ShapeDtypeStruct((block_x, block_y, NG), jnp.float32),
+        grid=(groups,),
+        out_shape=[
+            jax.ShapeDtypeStruct((block_x, block_y, NG), jnp.float32),
+            jax.ShapeDtypeStruct((1, atoms), jnp.float32),
+        ],
         in_specs=[
-            pl.BlockSpec((NG // 2, step, 128), lambda index: (0, index, 0)),
-            pl.BlockSpec((2, NG, NG), lambda index: (0, 0, 0)),
+            pl.BlockSpec((bricks2, 1, pairs, 8, 128), lambda index: (0, index, 0, 0, 0)),
+            pl.BlockSpec((bricks2, pairs, 8, 128), lambda index: (0, index, 0, 0)),
+            pl.BlockSpec((bricks2, 1, 8, 128), lambda index: (0, groups * pairs, 0, 0)),
+            whole((1, atoms)),
+            whole((1, atoms)),
+            whole(table.shape),
         ],
-        out_specs=pl.BlockSpec((step, block_y, NG), lambda index: (index, 0, 0)),
+        out_specs=[
+            pl.BlockSpec((8, block_y, NG), lambda index: (index, 0, 0)),
+            whole((1, atoms)),
+        ],
         compiler_params=pltpu.CompilerParams(vmem_limit_bytes=32 * 2**20),
         name="finish",
-    )(got, table)
+    )(early, later, later, short, charge, table)
 
 
 def two_parts(table):
@@ -1041,29 +1152,47 @@
         last.append(two_parts(columns))
     cosine_row = np.cos(np.arange(128) * (2.0 * math.pi / NG)).astype(np.float32)[None]
     cosine_row = jnp.asarray(cosine_row)
-    sent, full, every_atom = solve(
+    tables = jnp.asarray(tables)
+    last = jnp.asarray(np.stack(last))
+    early, full, every_atom, later = spread_and_solve(
+        block_x, block_y, window, kappa, pair, every_field, waves, cosine_row, tables, last
+    )
+
+    def send(values):
+        got = exchange(values.reshape(values.shape[0], -1, 128), ("brick", "slab"), halves)
+        return got.reshape(values.shape)
+
+    early = send(early)
+    later = solve_and_sample(
         block_x,
         block_y,
         window,
         kappa,
         pair,
-        every_field,
+        every_atom,
         waves,
         cosine_row,
-        jnp.asarray(tables),
-        jnp.asarray(np.stack(last)),
-    )
-    got = exchange(sent.reshape(2 * count_x, -1, 128), ("brick", "slab"), halves)
-    partial = sample(
-        atoms, block_x, block_y, window, pair, every_atom, waves, cosine_row, full
-    )
+        tables,
+        last,
+        later,
+        full,
+    )
+    later = send(later)
     energy_short = energies(descriptor, energy_in, energy_hidden, energy_out)
-    partial, got = lax.optimization_barrier((partial, got))
-    potential_at = jnp.sum(exchange(partial, ("brick", "slab"), halves), axis=0)
-    atom_energy = energy_short + 0.5 * charge * potential_at
-    pairs = basis.reshape(-1, 2, NG).transpose(1, 0, 2).reshape(NG, NG)
-    potential = finish(
-        block_x, block_y, got.reshape(NG // 2, block_x, 128), jnp.asarray(two_parts(pairs))
+    source = np.arange(2 * count_x)[:, None] * parts
+    pairs = 2 * np.arange(parts // 2)[None, :]
+    order = np.concatenate(
+        [(source + pairs[:, : parts // 4]).ravel(), (source + pairs[:, parts // 4 :]).ravel()]
+    )
+    order = np.concatenate([order, order + 1])
+    potential, atom_energy = finish(
+        block_x,
+        block_y,
+        early,
+        later,
+        energy_short,
+        charge,
+        jnp.asarray(two_parts(basis[order])),
     )
     return atom_energy, potential
 
@@ -1081,7 +1210,7 @@
         P(None, "slab", "brick"),
     ) + (P(),) * 10
     bricks, slabs = mesh.shape["brick"], mesh.shape["slab"]
-    fits = 2 * NG == 128 * slabs and slabs % 2 == 0 and NG % (4 * bricks) == 0
+    fits = 2 * NG == 128 * slabs and NG % (16 * bricks) == 0
     return jax.shard_map(
         per_device if fits else per_device_general,
         mesh=mesh,

time: 124 us -> 102 us (0.82)
  local copies, waits for them, and re-layouts: 19.3 us -> 3.33 us
  waiting for transfers between devices: 32.8 us -> 24.9 us
  Pallas kernels: 54.1 us -> 56.6 us
    unnamed x52 -> x12, local copies, waits for them, and re-layouts: 19.1 us -> 1.98 us
    all_to_all x3, waiting for transfers between devices: 28.6 us -> 20.7 us  [exchange(): lax.all_to_all(values, axes, split_axis=0, concat_axis=0, tiled=True, axi...]
    pallas_call x1, Pallas kernels: 1.83 us -> 4.36 us  [energies(): pl.pallas_call(energy_kernel, grid=(1,), out_shape=result, in_specs=whole...]
  transfers between devices with their start and end apart: 5 -> 5, of which waited for: 4 -> 5; matrix products, arithmetic and copies ran while one was open for 0% -> 1% of each run, Pallas kernels for 9% -> 19%
where the time goes in v3:
time: 102 us
  Pallas kernels  56.6 us (55%)
  waiting for transfers between devices  24.9 us (24%)
  starting transfers between devices  16 us (16%)
  local copies, waits for them, and re-layouts  3.33 us (3%)
    all_to_all x3, waiting for transfers between devices, exchange(): lax.all_to_all(values, axes, split_axis=0, concat_axis=0, tiled=True, axi...  20.7 us
    pallas_call x1, Pallas kernels, spread_and_solve(): pl.pallas_call(functools.partial(spread_kernel, block_x, block_y, window)...  16.8 us
    pallas_call x1, Pallas kernels, networks(): pl.pallas_call(functools.partial(network_kernel, ghosts), grid=(1,), out_...  16 us
    pallas_call x1, Pallas kernels, solve_and_sample(): pl.pallas_call(functools.partial(sample_kernel, block_x, block_y, window)...  14.5 us
    all_to_all x3, starting transfers between devices, exchange(): lax.all_to_all(values, axes, split_axis=0, concat_axis=0, tiled=True, axi...  12.7 us
    pallas_call x1, Pallas kernels, energies(): pl.pallas_call(energy_kernel, grid=(1,), out_shape=result, in_specs=whole...  4.36 us
    pallas_call x1, Pallas kernels, finish(): pl.pallas_call(functools.partial(finish_kernel, block_y), grid=(groups,),...  3.58 us
    ppermute x1, starting transfers between devices, per_device(): upper = lax.ppermute(outgoing, 'brick', down)  3.33 us
  transfers between devices with their start and end apart: 5, of which 5 were waited for; matrix products, arithmetic and copies ran while one was open for 1% of the time, Pallas kernels for 19%

profile of v3, /device:TPU:0, one launch (start us, length us, event | category | flops | bytes accessed | tf_op | source)
XLA Modules:
  0.0 101.6 jit_solution(15062051916391044049)
XLA Ops:
  0.6 1.4 %collect_atoms.1 = (f32[8,256]{1,0:T(8,128)}, f32[8,256]{1,0:T(8,128)}) custom-call(f32[3,1,192]{2,1,0:T(1,128)} %positions_ref.1, s32[1,192]{1,0:T(1,128)} %types_ref.3, s32[1,192]{1,0:T(1,128)} %count_ref.1, s32[1,192]{1,0:T(1,128)} %send_ref.1), custom_call_target="tpu_custom_call" | custom-call | tf_op jit(solution)/shard_map/collect_atoms/pallas_call | solution.py:331
  2.0 3.3 %collective-permute-start.1 = (f32[8,256]{1,0:T(8,128)}, f32[8,256]{1,0:T(8,128)S(1)}, u32[]{:S(2)}, u32[]{:S(2)}) collective-permute-start(f32[8,256]{1,0:T(8,128)} %get-tuple-element.14), channel_id=1, source_target_pairs={{4,0},{8,4},{12,8},{16,12},{20,16},{24,20},{28,24},{0,28},{5,1},{9... | collective-permute-start | bytes 24584 | tf_op jit(solution)/shard_map/ppermute | solution.py:1116
  5.4 0.0 collective-permute-start
  5.4 1.6 %collective-permute-done.1.upper_ref = f32[8,256]{1,0:T(8,128)S(1)} collective-permute-done((f32[8,256]{1,0:T(8,128)}, f32[8,256]{1,0:T(8,128)S(1)}, u32[]{:S(2)}, u32[]{:S(2)}) %collective-permute-start.1) | collective-permute-done | bytes 8224 | tf_op jit(solution)/shard_map/ppermute | solution.py:1116
  7.0 0.0 copy-start.4
  7.0 2.6 %collective-permute-done.lower_ref = f32[8,256]{1,0:T(8,128)S(1)} collective-permute-done((f32[8,256]{1,0:T(8,128)}, f32[8,256]{1,0:T(8,128)S(1)}, u32[]{:S(2)}, u32[]{:S(2)}) %collective-permute-start) | collective-permute-done | bytes 8224 | tf_op jit(solution)/shard_map/ppermute | solution.py:1115
  9.6 0.0 copy-start.5
  9.6 0.0 copy-done.4
  9.6 0.6 copy-done.5
  10.2 16.0 %networks.1 = (f32[192,1600]{1,0:T(8,128)}, f32[1,192]{1,0:T(1,128)}, f32[32,8,192]{2,1,0:T(8,128)}) custom-call(s32[1]{0:T(128)} %bitcast.1.base_ref, f32[2]{0:T(128)} %charges_ref.1, f32[8,256]{1,0:T(8,128)} %get-tuple-element.13.own_ref, f32[8,256]{1,0:T(8,128)} %copy-done.5, f32[8,256]{1,0:T(8,128)} %copy-done.4, s32[64,192]{1,0:T(8,128)} %bitcast.20, ...), custom_call_target="tpu_custom_call" | custom-call | tf_op jit(solution)/shard_map/networks/pallas_call | solution.py:627
  26.1 4.2 %all-to-all-start = ((f32[32,8,192]{2,1,0:T(8,128)}), f32[32,8,192]{2,1,0:T(8,128)S(1)}, u32[]{:S(2)}, u32[]{:S(2)}) async-start(f32[32,8,192]{2,1,0:T(8,128)} %get-tuple-element.15), calls=%async_computation | async-start | bytes 524288 | tf_op jit(solution)/shard_map/all_to_all | solution.py:1108
  30.3 0.7 copy.27.waves_ref
  31.1 0.7 copy.26.kappa_ref
  31.7 9.0 %all-to-all-done.static_ref = f32[32,8,192]{2,1,0:T(8,128)S(1)} async-done(((f32[32,8,192]{2,1,0:T(8,128)}), f32[32,8,192]{2,1,0:T(8,128)S(1)}, u32[]{:S(2)}, u32[]{:S(2)}) %all-to-all-start) | async-done | bytes 196640 | tf_op jit(solution)/shard_map/all_to_all | solution.py:1108
  40.7 0.0 copy-start.3
  40.7 0.7 copy-done.3
  41.4 16.8 %spread_and_solve.1 = (f32[16,4,4,8,128]{4,3,2,1,0:T(8,128)}, f32[8,256,256]{2,1,0:T(8,128)}, f32[8,8,768]{2,1,0:T(8,128)}, f32[8,256,256]{2,1,0:T(8,128)}) custom-call(f32[16,2]{1,0:T(8,128)} %copy.26.kappa_ref, s32[1]{0:T(128)} %bitcast.pair_ref, f32[32,8,192]{2,1,0:T(8,128)} %copy-done.3, s32[16,2]{1,0:T(8,128)} %copy.27.waves_ref, ...), custom_call_target="tpu_custom_call" | custom-call | tf_op jit(solution)/shard_map/spread_and_solve/pallas_call | solution.py:875
  58.2 3.9 %all-to-all-start.1 = ((f32[16,128,128]{2,1,0:T(8,128)}), f32[16,128,128]{2,1,0:T(8,128)S(1)}, u32[]{:S(2)}, u32[]{:S(2)}) async-start(f32[16,128,128]{2,1,0:T(8,128)} %bitcast.19), calls=%async_computation.1 | async-start | bytes 2097152 | tf_op jit(solution)/shard_map/all_to_all | solution.py:1108
  62.1 14.5 %solve_and_sample.1 = f32[16,17,8,128]{3,2,1,0:T(8,128)} custom-call(f32[16,2]{1,0:T(8,128)} %copy.26.kappa_ref, s32[1]{0:T(128)} %bitcast.pair_ref, f32[8,8,768]{2,1,0:T(8,128)} %get-tuple-element.17.atoms_ref, s32[16,2]{1,0:T(8,128)} %copy.27.waves_ref, f32[1,128]{1,0:T(1,128)} %constant.64.clone.cosine_ref, ...), custom_call_target="tpu_custom_call" | custom-call | flops 6442450944 | bytes 2097152 | tf_op jit(solution)/shard_map/solve_and_sample/pallas_call | solution.py:984
  76.6 0.2 all-to-all-done.1
  76.8 4.7 %all-to-all-start.2 = ((f32[16,136,128]{2,1,0:T(8,128)}), f32[16,136,128]{2,1,0:T(8,128)S(1)}, u32[]{:S(2)}, u32[]{:S(2)}) async-start(f32[16,136,128]{2,1,0:T(8,128)} %bitcast.18), calls=%async_computation.2 | async-start | bytes 2228224 | tf_op jit(solution)/shard_map/all_to_all | solution.py:1108
  81.5 0.0 copy-start
  81.5 0.0 copy-start.2
  81.5 4.4 %energies.1.short_ref = f32[1,192]{1,0:T(1,128)} custom-call(f32[192,1600]{1,0:T(8,128)} %get-tuple-element.20.descriptor_ref, f32[240,1600]{1,0:T(8,128)} %bitcast.17, f32[2,240,240]{2,1,0:T(8,128)} %weight_hidden_ref.1, f32[1,240]{1,0:T(1,128)} %bitcast.22), custom_call_target="tpu_custom_call" | custom-call | flops 442368000 | bytes 1536000 | tf_op jit(solution)/shard_map/energies/pallas_call | solution.py:662
  85.9 11.5 %all-to-all-done.2 = f32[16,136,128]{2,1,0:T(8,128)S(1)} async-done(((f32[16,136,128]{2,1,0:T(8,128)}), f32[16,136,128]{2,1,0:T(8,128)S(1)}, u32[]{:S(2)}, u32[]{:S(2)}) %all-to-all-start.2) | async-done | bytes 1114144 | tf_op jit(solution)/shard_map/all_to_all | solution.py:1108
  97.4 0.0 copy-done
  97.4 0.0 copy-done.2
  97.4 0.0 copy-start.1
  97.4 0.7 copy-done.1
  98.1 3.6 %finish.1 = (f32[32,64,256]{2,1,0:T(8,128)}, f32[1,192]{1,0:T(1,128)}) custom-call(f32[16,4,4,8,128]{4,3,2,1,0:T(8,128)S(1)} %bitcast.15, f32[16,17,8,128]{3,2,1,0:T(8,128)S(1)} %bitcast.13, f32[16,17,8,128]{3,2,1,0:T(8,128)S(1)} %bitcast.14, f32[1,192]{1,0:T(1,128)S(1)} %copy-done.1, f32[1,192]{1,0:T(1,128)S(1)} %copy-done.2, bf16[2,256,256]{2,1,0:T(8,128)(2,1)S(1)} %copy-done), custom_call_target="tpu_custom_call" | custom-call | tf_op jit(solution)/shard_map/finish/pallas_call | solution.py:1032
  (4 shorter events, 0.0 us)
Async XLA Ops:
  2.0 4.9 %collective-permute-start.1 = (f32[8,256]{1,0:T(8,128)}, f32[8,256]{1,0:T(8,128)S(1)}, u32[]{:S(2)}, u32[]{:S(2)}) collective-permute-start(f32[8,256]{1,0:T(8,128)} %get-tuple-element.14), channel_id=1, source_target_pairs={{4,0},{8,4},{12,8},{16,12},{20,16},{24,20},{28,24},{0,28},{5,1},{9... | collective-permute-start | bytes 24584 | tf_op jit(solution)/shard_map/ppermute | solution.py:1116
  5.4 4.2 %collective-permute-start = (f32[8,256]{1,0:T(8,128)}, f32[8,256]{1,0:T(8,128)S(1)}, u32[]{:S(2)}, u32[]{:S(2)}) collective-permute-start(f32[8,256]{1,0:T(8,128)} %get-tuple-element.14), channel_id=1, source_target_pairs={{0,4},{4,8},{8,12},{12,16},{16,20},{20,24},{24,28},{28,0},{1,5},{5... | collective-permute-start | bytes 24584 | tf_op jit(solution)/shard_map/ppermute | solution.py:1115
  7.0 2.6 %copy-start.4 = (f32[8,256]{1,0:T(8,128)}, f32[8,256]{1,0:T(8,128)S(1)}, u32[]{:S(2)}) copy-start(f32[8,256]{1,0:T(8,128)S(1)} %collective-permute-done.1.upper_ref) | copy-start | bytes 24580
  9.6 0.6 copy-start.5
  26.1 14.6 %all-to-all-start = ((f32[32,8,192]{2,1,0:T(8,128)}), f32[32,8,192]{2,1,0:T(8,128)S(1)}, u32[]{:S(2)}, u32[]{:S(2)}) async-start(f32[32,8,192]{2,1,0:T(8,128)} %get-tuple-element.15), calls=%async_computation | async-start | bytes 524288 | tf_op jit(solution)/shard_map/all_to_all | solution.py:1108
  40.7 0.7 copy-start.3
  58.2 18.6 %all-to-all-start.1 = ((f32[16,128,128]{2,1,0:T(8,128)}), f32[16,128,128]{2,1,0:T(8,128)S(1)}, u32[]{:S(2)}, u32[]{:S(2)}) async-start(f32[16,128,128]{2,1,0:T(8,128)} %bitcast.19), calls=%async_computation.1 | async-start | bytes 2097152 | tf_op jit(solution)/shard_map/all_to_all | solution.py:1108
  76.8 20.6 %all-to-all-start.2 = ((f32[16,136,128]{2,1,0:T(8,128)}), f32[16,136,128]{2,1,0:T(8,128)S(1)}, u32[]{:S(2)}, u32[]{:S(2)}) async-start(f32[16,136,128]{2,1,0:T(8,128)} %bitcast.18), calls=%async_computation.2 | async-start | bytes 2228224 | tf_op jit(solution)/shard_map/all_to_all | solution.py:1108
  81.5 15.9 %copy-start = (bf16[2,256,256]{2,1,0:T(8,128)(2,1)S(1)}, bf16[2,256,256]{2,1,0:T(8,128)(2,1)}, u32[]{:S(2)}) copy-start(bf16[2,256,256]{2,1,0:T(8,128)(2,1)} %constant.67.clone.table_ref) | copy-start | bytes 786436
  81.5 15.9 %copy-start.2 = (f32[1,192]{1,0:T(1,128)S(1)}, f32[1,192]{1,0:T(1,128)}, u32[]{:S(2)}) copy-start(f32[1,192]{1,0:T(1,128)} %get-tuple-element.21.charge_ref) | copy-start | bytes 2308
  97.4 0.7 copy-start.1

commit v4 on v3

--- a/solution.py
+++ b/solution.py
@@ -282,6 +282,13 @@
 
 
 def triple(left, right, dims=((1,), (0,))):
+    (left_axis,), (right_axis,) = dims
+    if left[0].shape[left_axis] % 128 == 0:
+        return multiply(
+            jnp.concatenate([left[0], left[0], left[1]], axis=left_axis),
+            jnp.concatenate([right[0], right[1], right[0]], axis=right_axis),
+            dims,
+        )
     return (
         multiply(left[0], right[0], dims)
         + multiply(left[0], right[1], dims)
@@ -534,17 +541,18 @@
                 ]
 
     def body(step, carry):
-        one_group(pl.multiple_of(step * 2 * group, 2 * group))
-        one_group(pl.multiple_of(step * 2 * group + group, group))
+        for part in range(unroll):
+            one_group(pl.multiple_of(step * unroll * group + part * group, group))
         return carry
 
-    lax.fori_loop(0, rows // (2 * group), body, 0)
+    unroll = 4 if rows % (4 * group) == 0 else 1
+    lax.fori_loop(0, rows // (unroll * group), body, 0)
 
     chunks = (descriptor_ref.shape[1] + 127) // 128
     last = descriptor_ref.shape[1] - 128 * (chunks - 1)
 
-    def describe(step, carry):
-        band = pl.ds(pl.multiple_of(step * 8, 8), 8)
+    def describe_band(start):
+        band = pl.ds(start, 8)
         moments = [moments_ref[part, band, :] for part in range(4)]
         axis_part = [lane_pick(moments[part], lane & 15) for part in range(4)]
         for chunk in range(chunks):
@@ -556,9 +564,15 @@
                 descriptor_ref[band, 128 * chunk : 128 * chunk + 128] = total
             else:
                 descriptor_ref[band, 128 * chunk : 128 * chunk + last] = total[:, 0:last]
+
+    bands = 4 if atoms % 32 == 0 else 1
+
+    def describe(step, carry):
+        for part in range(bands):
+            describe_band(pl.multiple_of(step * 8 * bands + 8 * part, 8))
         return carry
 
-    lax.fori_loop(0, atoms // 8, describe, 0)
+    lax.fori_loop(0, atoms // (8 * bands), describe, 0)
 
     store = pltpu.make_async_copy(descriptor_ref, descriptor_hbm, semaphores.at[2])
     store.start()
@@ -731,10 +745,31 @@
     )
 
 
-def second_factors(fields, base):
-    rows = lax.broadcasted_iota(jnp.int32, (NG, fields.shape[1]), 0)
+def second_factors(fields, base, block_y, slabs, high_ref, low_ref):
+    atoms = fields.shape[1]
+    block = atoms // slabs
+    reach = block_y + 16
     start = fields[1:2, :].astype(jnp.int32) - base
-    return placed_weights((rows - start) & (NG - 1), weight_rows(fields[4:5, :]))
+    weights = weight_rows(fields[4:5, :])
+    for chunk in range(atoms // 128):
+        lanes = slice(128 * chunk, 128 * (chunk + 1))
+        first = 128 * chunk // block
+        last = (128 * chunk + 127) // block
+        top = first * block_y
+        rows = (last - first) * block_y + reach
+        pieces = [(top, min(rows, NG - top))]
+        if top + rows > NG:
+            pieces.append((0, top + rows - NG))
+        for row, count in pieces:
+            index = row + lax.broadcasted_iota(jnp.int32, (count, 128), 0)
+            table = split(
+                placed_weights(
+                    (index - start[:, lanes]) & (NG - 1), [weight[:, lanes] for weight in weights]
+                )
+            )
+            high_ref[row : row + count, lanes] = table[0]
+            low_ref[row : row + count, lanes] = table[1]
+    return high_ref[...], low_ref[...]
 
 
 def wave_of(index):
@@ -807,6 +842,7 @@
     tables_ref,
     last_ref,
     semaphores,
+    *second_refs,
 ):
     slabs = NG // block_y
     bricks = NG // block_x
@@ -814,8 +850,9 @@
     block = static_ref.shape[2]
     count = full_ref.shape[0]
     step = pl.program_id(0)
+    later = later_hbm.shape[0]
     store = pltpu.make_async_copy(
-        grid_ref.at[pl.ds(parts // 2, parts // 2), pl.ds(0, NG)], later_hbm, semaphores.at[2]
+        grid_ref.at[pl.ds(parts - later, later), pl.ds(0, NG)], later_hbm, semaphores.at[2]
     )
 
     @pl.when(step == 0)
@@ -831,10 +868,15 @@
             for brick in range(bricks):
                 atoms_ref[brick, :, lanes] = static_ref[slab * bricks + brick]
         grid_ref[...] = jnp.zeros_like(grid_ref)
+        for ref in second_refs:
+            ref[...] = jnp.zeros_like(ref)
         for brick in range(bricks):
             fields = atoms_ref[brick]
             table = split(first_third(fields, waves_ref, cosine_ref, window, fields[6:7, :]))
-            spread = triple(table, split(second_factors(fields, 0)), LANES)
+            second = second_factors(
+                fields, 0, block_y, slabs, second_refs[2 * (brick % 2)], second_refs[2 * (brick % 2) + 1]
+            )
+            spread = triple(table, second, LANES)
             rows = slice(block_x * brick, block_x * brick + window)
             for part in range(parts):
                 grid_ref[part, rows, :] += spread[part * window : part * window + window]
@@ -860,6 +902,10 @@
         store.wait()
 
 
+def early_pairs(parts):
+    return (5 * parts + 8) // 16
+
+
 def spread_and_solve(
     block_x, block_y, window, kappa, pair, static, waves, cosine_row, tables, last
 ):
@@ -867,19 +913,19 @@
     slabs = NG // block_y
     bricks = NG // block_x
     parts = waves.shape[0]
-    pairs = parts // 4
-    count = 4
+    pairs = early_pairs(parts)
+    count = 2
     anywhere = pl.BlockSpec(memory_space=pl.ANY)
     scalars = pl.BlockSpec(memory_space=pltpu.SMEM)
     sent_block = (2 * bricks, block_x // 8, count // 2, 8, 128)
     return pl.pallas_call(
         functools.partial(spread_kernel, block_x, block_y, window),
-        grid=(parts // 2 // count,),
+        grid=(2 * pairs // count,),
         out_shape=[
             jax.ShapeDtypeStruct((2 * bricks, block_x // 8, pairs, 8, 128), jnp.float32),
-            jax.ShapeDtypeStruct((parts // 2, NG, NG), jnp.float32),
+            jax.ShapeDtypeStruct((2 * pairs, NG, NG), jnp.float32),
             jax.ShapeDtypeStruct((bricks, 8, slabs * atoms), jnp.float32),
-            jax.ShapeDtypeStruct((parts // 2, NG, NG), jnp.float32),
+            jax.ShapeDtypeStruct((parts - 2 * pairs, NG, NG), jnp.float32),
         ],
         in_specs=[scalars, scalars]
         + whole_specs(static, waves, cosine_row)
@@ -895,7 +941,8 @@
             pltpu.VMEM(tables.shape, tables.dtype),
             pltpu.VMEM(last.shape[1:], last.dtype),
             pltpu.SemaphoreType.DMA((3,)),
-        ],
+        ]
+        + [pltpu.VMEM((NG, slabs * atoms), jnp.bfloat16)] * 4,
         compiler_params=pltpu.CompilerParams(vmem_limit_bytes=VMEM_BYTES),
         name="spread_and_solve",
     )(kappa, pair, static, waves, cosine_row, tables, last)
@@ -920,35 +967,36 @@
     tables_ref,
     last_ref,
     semaphores,
+    *second_refs,
 ):
     bricks = atoms_ref.shape[0]
     parts = waves_ref.shape[0]
-    half = parts // 2
-    count = 4
+    early = 2 * early_pairs(parts)
     block = atoms_ref.shape[2] * block_y // NG
     fetches = [
         pltpu.make_async_copy(tables_hbm, tables_ref, semaphores.at[0]),
         pltpu.make_async_copy(last_hbm.at[pair_ref[0]], last_ref, semaphores.at[1]),
         pltpu.make_async_copy(later_hbm, later_ref, semaphores.at[2]),
-        pltpu.make_async_copy(early_hbm, full_ref.at[pl.ds(0, half)], semaphores.at[3]),
+        pltpu.make_async_copy(early_hbm, full_ref.at[pl.ds(0, early)], semaphores.at[3]),
     ]
     for fetch in fetches:
         fetch.start()
     for fetch in fetches[:3]:
         fetch.wait()
-    pairs = half // 2
-    for step in range(half // count):
-        planes = [later_ref[count * step + part] for part in range(count)]
-        full = transform(planes, kappa_ref, half + count * step, tables_ref, last_ref)
-        for part in range(count):
-            full_ref[half + count * step + part] = full[NG * part : NG * (part + 1)]
-
-        def put(pair, brick, side, group, tile):
-            sent_ref[2 * brick + side, pairs * group + count // 2 * step + pair] = tile
-
-        send_blocks(full, block_x, block_y, put)
+    pairs = (parts - early) // 2
+    planes = [later_ref[part] for part in range(parts - early)]
+    full = transform(planes, kappa_ref, early, tables_ref, last_ref)
+    for part in range(parts - early):
+        full_ref[early + part] = full[NG * part : NG * (part + 1)]
+
+    def put(pair, brick, side, group, tile):
+        sent_ref[2 * brick + side, pairs * group + pair] = tile
+
+    send_blocks(full, block_x, block_y, put)
     fetches[3].wait()
 
+    for ref in second_refs:
+        ref[...] = jnp.zeros_like(ref)
     extra = sent_ref.shape[1] - 1
     base = 2 * block_y * pair_ref[0]
     lanes = pl.ds(pl.multiple_of(2 * block * pair_ref[0], 128), 2 * block)
@@ -963,7 +1011,10 @@
             if inside < window:
                 values.append(full_ref[part, 0 : window - inside, :])
         values = split(jnp.concatenate(values, axis=0))
-        along = triple(values, split(second_factors(fields, base)))
+        second = second_factors(
+            fields, base, block_y, 2, second_refs[2 * (brick % 2)], second_refs[2 * (brick % 2) + 1]
+        )
+        along = triple(values, second)
         sums = jnp.sum(along * weights, axis=0, keepdims=True)
         for side in range(2):
             row = sums[:, block * side : block * (side + 1)]
@@ -977,7 +1028,7 @@
 ):
     bricks = atoms.shape[0]
     parts = waves.shape[0]
-    pairs = parts // 4
+    pairs = parts // 2 - early_pairs(parts)
     anywhere = pl.BlockSpec(memory_space=pl.ANY)
     scalars = pl.BlockSpec(memory_space=pltpu.SMEM)
     result = jax.ShapeDtypeStruct((2 * bricks, block_x // 8 * pairs + 1, 8, 128), jnp.float32)
@@ -988,12 +1039,13 @@
         in_specs=[scalars, scalars] + whole_specs(atoms, waves, cosine_row) + [anywhere] * 4,
         out_specs=whole(result.shape),
         scratch_shapes=[
-            pltpu.VMEM((parts // 2, NG, NG), jnp.float32),
+            pltpu.VMEM((2 * pairs, NG, NG), jnp.float32),
             pltpu.VMEM((parts, NG, NG), jnp.float32),
             pltpu.VMEM(tables.shape, tables.dtype),
             pltpu.VMEM(last.shape[1:], last.dtype),
             pltpu.SemaphoreType.DMA((4,)),
-        ],
+        ]
+        + [pltpu.VMEM((NG, 2 * atoms.shape[2] * block_y // NG), jnp.bfloat16)] * 4,
         compiler_params=pltpu.CompilerParams(vmem_limit_bytes=VMEM_BYTES),
         cost_estimate=pl.CostEstimate(
             flops=24 * parts * NG * NG * NG, bytes_accessed=4 * early.size, transcendentals=0
@@ -1008,9 +1060,9 @@
     atoms = short_ref.shape[1]
     table = (table_ref[0], table_ref[1])
     lines = early_ref.shape[3]
-    rows = early_ref.shape[0] * early_ref.shape[2]
-    early = early_ref.reshape(rows, lines, 128)
-    later = later_ref.reshape(rows, lines, 128)
+    sources, _, pairs = early_ref.shape[:3]
+    early = early_ref.reshape(sources * pairs, lines, 128)
+    later = later_ref.reshape(sources * later_ref.shape[1], lines, 128)
     pieces = []
     for line in range(lines):
         turned = jnp.concatenate([early[:, line, :], later[:, line, :]], axis=0).T
@@ -1028,6 +1080,7 @@
 
 def finish(block_x, block_y, early, later, short, charge, table):
     bricks2, groups, pairs = early.shape[:3]
+    rest = (later.shape[1] - 1) // groups
     atoms = short.shape[1]
     return pl.pallas_call(
         functools.partial(finish_kernel, block_y),
@@ -1038,8 +1091,8 @@
         ],
         in_specs=[
             pl.BlockSpec((bricks2, 1, pairs, 8, 128), lambda index: (0, index, 0, 0, 0)),
-            pl.BlockSpec((bricks2, pairs, 8, 128), lambda index: (0, index, 0, 0)),
-            pl.BlockSpec((bricks2, 1, 8, 128), lambda index: (0, groups * pairs, 0, 0)),
+            pl.BlockSpec((bricks2, rest, 8, 128), lambda index: (0, index, 0, 0)),
+            pl.BlockSpec((bricks2, 1, 8, 128), lambda index: (0, groups * rest, 0, 0)),
             whole((1, atoms)),
             whole((1, atoms)),
             whole(table.shape),
@@ -1182,7 +1235,10 @@
     source = np.arange(2 * count_x)[:, None] * parts
     pairs = 2 * np.arange(parts // 2)[None, :]
     order = np.concatenate(
-        [(source + pairs[:, : parts // 4]).ravel(), (source + pairs[:, parts // 4 :]).ravel()]
+        [
+            (source + pairs[:, : early_pairs(parts)]).ravel(),
+            (source + pairs[:, early_pairs(parts) :]).ravel(),
+        ]
     )
     order = np.concatenate([order, order + 1])
     potential, atom_energy = finish(
@@ -1210,7 +1266,7 @@
         P(None, "slab", "brick"),
     ) + (P(),) * 10
     bricks, slabs = mesh.shape["brick"], mesh.shape["slab"]
-    fits = 2 * NG == 128 * slabs and NG % (16 * bricks) == 0
+    fits = 2 * NG == 128 * slabs and NG % (32 * bricks) == 0
     return jax.shard_map(
         per_device if fits else per_device_general,
         mesh=mesh,

time: 102 us -> 113 us (1.11)
  blocking collectives: 0 us -> 16.3 us
  starting transfers between devices: 16 us -> 11.2 us
  Pallas kernels: 56.6 us -> 54.2 us
  waiting for transfers between devices: 24.9 us -> 26.9 us
    all_to_all x0 -> x1, blocking collectives: none -> 16.3 us  [exchange(): lax.all_to_all(values, axes, split_axis=0, concat_axis=0, tiled=True, axi...]
    all_to_all x3 -> x2, starting transfers between devices: 12.7 us -> 7.86 us  [exchange(): lax.all_to_all(values, axes, split_axis=0, concat_axis=0, tiled=True, axi...]
    pallas_call x1, Pallas kernels: 16 us -> 13.9 us  [networks(): pl.pallas_call(functools.partial(network_kernel, ghosts), grid=(1,), out_...]
    all_to_all x3 -> x2, waiting for transfers between devices: 20.7 us -> 22.7 us  [exchange(): lax.all_to_all(values, axes, split_axis=0, concat_axis=0, tiled=True, axi...]
    pallas_call x1, Pallas kernels: 14.5 us -> 12.8 us  [solve_and_sample(): pl.pallas_call(functools.partial(sample_kernel, block_x, block_y, window)...]
    pallas_call x1, Pallas kernels: 16.8 us -> 18.1 us  [spread_and_solve(): pl.pallas_call(functools.partial(spread_kernel, block_x, block_y, window)...]
  transfers between devices with their start and end apart: 5 -> 4, of which waited for: 5 -> 4; matrix products, arithmetic and copies ran while one was open for 1% -> 1% of each run, Pallas kernels for 19% -> 4%
where the time goes in v4:
time: 113 us
  Pallas kernels  54.2 us (48%)
  waiting for transfers between devices  26.9 us (24%)
  blocking collectives  16.3 us (14%)
  starting transfers between devices  11.2 us (10%)
  local copies, waits for them, and re-layouts  3.36 us (3%)
    all_to_all x2, waiting for transfers between devices, exchange(): lax.all_to_all(values, axes, split_axis=0, concat_axis=0, tiled=True, axi...  22.7 us
    pallas_call x1, Pallas kernels, spread_and_solve(): pl.pallas_call(functools.partial(spread_kernel, block_x, block_y, window)...  18.1 us
    all_to_all x1, blocking collectives, exchange(): lax.all_to_all(values, axes, split_axis=0, concat_axis=0, tiled=True, axi...  16.3 us
    pallas_call x1, Pallas kernels, networks(): pl.pallas_call(functools.partial(network_kernel, ghosts), grid=(1,), out_...  13.9 us
    pallas_call x1, Pallas kernels, solve_and_sample(): pl.pallas_call(functools.partial(sample_kernel, block_x, block_y, window)...  12.8 us
    all_to_all x2, starting transfers between devices, exchange(): lax.all_to_all(values, axes, split_axis=0, concat_axis=0, tiled=True, axi...  7.86 us
    pallas_call x1, Pallas kernels, energies(): pl.pallas_call(energy_kernel, grid=(1,), out_shape=result, in_specs=whole...  4.36 us
    pallas_call x1, Pallas kernels, finish(): pl.pallas_call(functools.partial(finish_kernel, block_y), grid=(groups,),...  3.61 us
  transfers between devices with their start and end apart: 4, of which 4 were waited for; matrix products, arithmetic and copies ran while one was open for 1% of the time, Pallas kernels for 4%

profile of v4, /device:TPU:0, one launch (start us, length us, event | category | flops | bytes accessed | tf_op | source)
XLA Modules:
  0.0 112.6 jit_solution(4571804438228998879)
XLA Ops:
  0.6 1.4 %collect_atoms.1 = (f32[8,256]{1,0:T(8,128)}, f32[8,256]{1,0:T(8,128)}) custom-call(f32[3,1,192]{2,1,0:T(1,128)} %positions_ref.1, s32[1,192]{1,0:T(1,128)} %types_ref.3, s32[1,192]{1,0:T(1,128)} %count_ref.1, s32[1,192]{1,0:T(1,128)} %send_ref.1), custom_call_target="tpu_custom_call" | custom-call | tf_op jit(solution)/shard_map/collect_atoms/pallas_call | solution.py:338
  2.0 3.3 %collective-permute-start.1 = (f32[8,256]{1,0:T(8,128)}, f32[8,256]{1,0:T(8,128)S(1)}, u32[]{:S(2)}, u32[]{:S(2)}) collective-permute-start(f32[8,256]{1,0:T(8,128)} %get-tuple-element.14), channel_id=1, source_target_pairs={{4,0},{8,4},{12,8},{16,12},{20,16},{24,20},{28,24},{0,28},{5,1},{9... | collective-permute-start | bytes 24584 | tf_op jit(solution)/shard_map/ppermute | solution.py:1169
  5.4 0.0 collective-permute-start
  5.4 1.6 %collective-permute-done.1.upper_ref = f32[8,256]{1,0:T(8,128)S(1)} collective-permute-done((f32[8,256]{1,0:T(8,128)}, f32[8,256]{1,0:T(8,128)S(1)}, u32[]{:S(2)}, u32[]{:S(2)}) %collective-permute-start.1) | collective-permute-done | bytes 8224 | tf_op jit(solution)/shard_map/ppermute | solution.py:1169
  7.0 0.0 copy-start.4
  7.0 2.6 %collective-permute-done.lower_ref = f32[8,256]{1,0:T(8,128)S(1)} collective-permute-done((f32[8,256]{1,0:T(8,128)}, f32[8,256]{1,0:T(8,128)S(1)}, u32[]{:S(2)}, u32[]{:S(2)}) %collective-permute-start) | collective-permute-done | bytes 8224 | tf_op jit(solution)/shard_map/ppermute | solution.py:1168
  9.6 0.0 copy-start.5
  9.6 0.0 copy-done.4
  9.6 0.6 copy-done.5
  10.2 13.9 %networks.1 = (f32[192,1600]{1,0:T(8,128)}, f32[1,192]{1,0:T(1,128)}, f32[32,8,192]{2,1,0:T(8,128)}) custom-call(s32[1]{0:T(128)} %bitcast.1.base_ref, f32[2]{0:T(128)} %charges_ref.1, f32[8,256]{1,0:T(8,128)} %get-tuple-element.13.own_ref, f32[8,256]{1,0:T(8,128)} %copy-done.5, f32[8,256]{1,0:T(8,128)} %copy-done.4, s32[64,192]{1,0:T(8,128)} %bitcast.19, ...), custom_call_target="tpu_custom_call" | custom-call | tf_op jit(solution)/shard_map/networks/pallas_call | solution.py:641
  24.1 4.2 %all-to-all-start = ((f32[32,8,192]{2,1,0:T(8,128)}), f32[32,8,192]{2,1,0:T(8,128)S(1)}, u32[]{:S(2)}, u32[]{:S(2)}) async-start(f32[32,8,192]{2,1,0:T(8,128)} %get-tuple-element.15), calls=%async_computation | async-start | bytes 524288 | tf_op jit(solution)/shard_map/all_to_all | solution.py:1161
  28.3 0.7 copy.27.waves_ref
  29.0 0.7 copy.26.kappa_ref
  29.6 9.0 %all-to-all-done.static_ref = f32[32,8,192]{2,1,0:T(8,128)S(1)} async-done(((f32[32,8,192]{2,1,0:T(8,128)}), f32[32,8,192]{2,1,0:T(8,128)S(1)}, u32[]{:S(2)}, u32[]{:S(2)}) %all-to-all-start) | async-done | bytes 196640 | tf_op jit(solution)/shard_map/all_to_all | solution.py:1161
  38.6 0.0 copy-start.3
  38.6 0.7 copy-done.3
  39.4 18.1 %spread_and_solve.1 = (f32[16,4,5,8,128]{4,3,2,1,0:T(8,128)}, f32[10,256,256]{2,1,0:T(8,128)}, f32[8,8,768]{2,1,0:T(8,128)}, f32[6,256,256]{2,1,0:T(8,128)}) custom-call(f32[16,2]{1,0:T(8,128)} %copy.26.kappa_ref, s32[1]{0:T(128)} %bitcast.pair_ref, f32[32,8,192]{2,1,0:T(8,128)} %copy-done.3, s32[16,2]{1,0:T(8,128)} %copy.27.waves_ref, ...), custom_call_target="tpu_custom_call" | custom-call | tf_op jit(solution)/shard_map/spread_and_solve/pallas_call | solution.py:921
  57.4 12.8 %solve_and_sample.1 = f32[16,13,8,128]{3,2,1,0:T(8,128)} custom-call(f32[16,2]{1,0:T(8,128)} %copy.26.kappa_ref, s32[1]{0:T(128)} %bitcast.pair_ref, f32[8,8,768]{2,1,0:T(8,128)} %get-tuple-element.17.atoms_ref, s32[16,2]{1,0:T(8,128)} %copy.27.waves_ref, f32[1,128]{1,0:T(1,128)} %constant.64.clone.cosine_ref, ...), custom_call_target="tpu_custom_call" | custom-call | flops 6442450944 | bytes 2621440 | tf_op jit(solution)/shard_map/solve_and_sample/pallas_call | solution.py:1035
  70.2 16.3 %all_to_all.15 = f32[16,104,128]{2,1,0:T(8,128)S(1)} all-to-all(f32[16,104,128]{2,1,0:T(8,128)} %bitcast.18), channel_id=1, replica_groups={{0,1,4,5,8,9,12,13,16,17,20,21,24,25,28,29},{2,3,6,7,10,11,14,15,18,19,..., dimensions={0} | all-to-all | bytes 1703936 | tf_op jit(solution)/shard_map/all_to_all | solution.py:1161
  86.5 3.7 %all-to-all-start.1 = ((f32[16,160,128]{2,1,0:T(8,128)}), f32[16,160,128]{2,1,0:T(8,128)S(1)}, u32[]{:S(2)}, u32[]{:S(2)}) async-start(f32[16,160,128]{2,1,0:T(8,128)} %bitcast.6), calls=%async_computation.1 | async-start | bytes 2621440 | tf_op jit(solution)/shard_map/all_to_all | solution.py:1161
  90.2 0.0 copy-start
  90.2 0.0 copy-start.2
  90.2 4.4 %energies.1.short_ref = f32[1,192]{1,0:T(1,128)} custom-call(f32[192,1600]{1,0:T(8,128)} %get-tuple-element.20.descriptor_ref, f32[240,1600]{1,0:T(8,128)} %bitcast.17, f32[2,240,240]{2,1,0:T(8,128)} %weight_hidden_ref.1, f32[1,240]{1,0:T(1,128)} %bitcast.21), custom_call_target="tpu_custom_call" | custom-call | flops 442368000 | bytes 1536000 | tf_op jit(solution)/shard_map/energies/pallas_call | solution.py:676
  94.6 13.8 %all-to-all-done.1 = f32[16,160,128]{2,1,0:T(8,128)S(1)} async-done(((f32[16,160,128]{2,1,0:T(8,128)}), f32[16,160,128]{2,1,0:T(8,128)S(1)}, u32[]{:S(2)}, u32[]{:S(2)}) %all-to-all-start.1) | async-done | bytes 1310752 | tf_op jit(solution)/shard_map/all_to_all | solution.py:1161
  108.3 0.0 copy-done
  108.3 0.0 copy-done.2
  108.3 0.0 copy-start.1
  108.3 0.7 copy-done.1
  109.0 3.6 %finish.1 = (f32[32,64,256]{2,1,0:T(8,128)}, f32[1,192]{1,0:T(1,128)}) custom-call(f32[16,4,5,8,128]{4,3,2,1,0:T(8,128)S(1)} %bitcast.15, f32[16,13,8,128]{3,2,1,0:T(8,128)S(1)} %bitcast.13, f32[16,13,8,128]{3,2,1,0:T(8,128)S(1)} %bitcast.14, f32[1,192]{1,0:T(1,128)S(1)} %copy-done.1, f32[1,192]{1,0:T(1,128)S(1)} %copy-done.2, bf16[2,256,256]{2,1,0:T(8,128)(2,1)S(1)} %copy-done), custom_call_target="tpu_custom_call" | custom-call | tf_op jit(solution)/shard_map/finish/pallas_call | solution.py:1085
  (4 shorter events, 0.0 us)
Async XLA Ops:
  2.0 4.9 %collective-permute-start.1 = (f32[8,256]{1,0:T(8,128)}, f32[8,256]{1,0:T(8,128)S(1)}, u32[]{:S(2)}, u32[]{:S(2)}) collective-permute-start(f32[8,256]{1,0:T(8,128)} %get-tuple-element.14), channel_id=1, source_target_pairs={{4,0},{8,4},{12,8},{16,12},{20,16},{24,20},{28,24},{0,28},{5,1},{9... | collective-permute-start | bytes 24584 | tf_op jit(solution)/shard_map/ppermute | solution.py:1169
  5.4 4.2 %collective-permute-start = (f32[8,256]{1,0:T(8,128)}, f32[8,256]{1,0:T(8,128)S(1)}, u32[]{:S(2)}, u32[]{:S(2)}) collective-permute-start(f32[8,256]{1,0:T(8,128)} %get-tuple-element.14), channel_id=1, source_target_pairs={{0,4},{4,8},{8,12},{12,16},{16,20},{20,24},{24,28},{28,0},{1,5},{5... | collective-permute-start | bytes 24584 | tf_op jit(solution)/shard_map/ppermute | solution.py:1168
  7.0 2.6 %copy-start.4 = (f32[8,256]{1,0:T(8,128)}, f32[8,256]{1,0:T(8,128)S(1)}, u32[]{:S(2)}) copy-start(f32[8,256]{1,0:T(8,128)S(1)} %collective-permute-done.1.upper_ref) | copy-start | bytes 24580
  9.6 0.6 copy-start.5
  24.1 14.6 %all-to-all-start = ((f32[32,8,192]{2,1,0:T(8,128)}), f32[32,8,192]{2,1,0:T(8,128)S(1)}, u32[]{:S(2)}, u32[]{:S(2)}) async-start(f32[32,8,192]{2,1,0:T(8,128)} %get-tuple-element.15), calls=%async_computation | async-start | bytes 524288 | tf_op jit(solution)/shard_map/all_to_all | solution.py:1161
  38.6 0.7 copy-start.3
  86.5 21.8 %all-to-all-start.1 = ((f32[16,160,128]{2,1,0:T(8,128)}), f32[16,160,128]{2,1,0:T(8,128)S(1)}, u32[]{:S(2)}, u32[]{:S(2)}) async-start(f32[16,160,128]{2,1,0:T(8,128)} %bitcast.6), calls=%async_computation.1 | async-start | bytes 2621440 | tf_op jit(solution)/shard_map/all_to_all | solution.py:1161
  90.2 18.1 %copy-start = (bf16[2,256,256]{2,1,0:T(8,128)(2,1)S(1)}, bf16[2,256,256]{2,1,0:T(8,128)(2,1)}, u32[]{:S(2)}) copy-start(bf16[2,256,256]{2,1,0:T(8,128)(2,1)} %constant.67.clone.table_ref) | copy-start | bytes 786436
  90.2 18.1 %copy-start.2 = (f32[1,192]{1,0:T(1,128)S(1)}, f32[1,192]{1,0:T(1,128)}, u32[]{:S(2)}) copy-start(f32[1,192]{1,0:T(1,128)} %get-tuple-element.21.charge_ref) | copy-start | bytes 2308
  108.3 0.7 copy-start.1

commit v5 on v4

--- a/solution.py
+++ b/solution.py
@@ -3,7 +3,6 @@
 
 import jax
 import jax.numpy as jnp
-import ml_dtypes
 import numpy as np
 from jax import lax
 from jax.experimental import pallas as pl
@@ -299,6 +298,16 @@
 LANES = ((1,), (1,))
 
 
+def product(left, right, dims=((1,), (0,))):
+    return lax.dot_general(
+        left,
+        right,
+        (dims, ((), ())),
+        precision=lax.Precision.HIGH,
+        preferred_element_type=jnp.float32,
+    )
+
+
 def lane_pick(table, index):
     return jnp.take_along_axis(table, index, axis=1, mode="promise_in_bounds")
 
@@ -347,21 +356,11 @@
 
 
 def fitting_rows(descriptor_ref, weight_in_ref, weight_hidden_ref, weight_out_ref):
-    depth = weight_in_ref.shape[1]
-    first = depth // 256 * 256
-    hidden = triple(
-        split(descriptor_ref[:, 0:first]), split(weight_in_ref[:, 0:first]), LANES
-    )
-    if first < depth:
-        hidden = hidden + triple(
-            split(descriptor_ref[:, first:depth]), split(weight_in_ref[:, first:depth]), LANES
-        )
-    hidden = jnp.tanh(hidden)
+    hidden = jnp.tanh(product(descriptor_ref[...], weight_in_ref[...], LANES))
     for layer in range(weight_hidden_ref.shape[0]):
-        hidden = jnp.tanh(triple(split(hidden), split(weight_hidden_ref[layer]))) + hidden
+        hidden = jnp.tanh(product(hidden, weight_hidden_ref[layer])) + hidden
     width = hidden.shape[1]
-    out_weight = jnp.broadcast_to(weight_out_ref[...], (8, width))
-    return triple(split(out_weight), split(hidden), LANES)
+    return product(jnp.broadcast_to(weight_out_ref[...], (8, width)), hidden, LANES)
 
 
 def natural_order(rows):
@@ -745,6 +744,28 @@
     )
 
 
+def first_third_split(fields, waves_ref, cosine_ref, window, scale, high_ref, low_ref):
+    atoms = fields.shape[1]
+    third = third_factors(fields, waves_ref, cosine_ref) * scale
+    rows = lax.broadcasted_iota(jnp.int32, (window, atoms), 0)
+    first = placed_weights(
+        rows - fields[0:1, :].astype(jnp.int32), weight_rows(fields[3:4, :])
+    )
+    for chunk in range(atoms // 128):
+        lanes = slice(128 * chunk, 128 * (chunk + 1))
+        for part in range(0, third.shape[0], 2):
+            high, low = split(
+                jnp.concatenate(
+                    [first[:, lanes] * third[part + side : part + side + 1, lanes] for side in range(2)],
+                    axis=0,
+                )
+            )
+            place = slice(part * window, (part + 2) * window)
+            high_ref[place, lanes] = high
+            low_ref[place, lanes] = low
+    return high_ref[...], low_ref[...]
+
+
 def second_factors(fields, base, block_y, slabs, high_ref, low_ref):
     atoms = fields.shape[1]
     block = atoms // slabs
@@ -785,26 +806,25 @@
 
 def transform(planes, kappa_ref, first_part, tables_ref, last_ref):
     count = len(planes)
-    basis = (tables_ref[0], tables_ref[1])
-    turned = (tables_ref[2], tables_ref[3])
-    last = (last_ref[0], last_ref[1])
+    basis = tables_ref[0]
+    turned = tables_ref[1]
     square_x, damp_x = damping(lax.broadcasted_iota(jnp.int32, (NG, 1), 0))
     square_y, damp_y = damping(lax.broadcasted_iota(jnp.int32, (1, NG), 1))
     square_xy = square_x + square_y
     damp_xy = damp_x * damp_y
     columns = [slice(NG * part, NG * (part + 1)) for part in range(count)]
-    first = triple(basis, split(jnp.concatenate(planes, axis=1)))
+    first = product(basis, jnp.concatenate(planes, axis=1))
     first = jnp.concatenate([first[:, column] for column in columns], axis=0)
-    both = triple(split(first), turned)
+    both = product(first, turned)
     scaled = []
     for part in range(count):
         squared = square_xy + kappa_ref[first_part + part, 0]
         root = jnp.where(squared == 0.0, 1.0, 0.0)
         green = (1.0 - root) * (damp_xy * kappa_ref[first_part + part, 1]) / (squared + root)
         scaled.append(both[columns[part]] * green)
-    back = triple(turned, split(jnp.concatenate(scaled, axis=1)))
+    back = product(turned, jnp.concatenate(scaled, axis=1))
     back = jnp.concatenate([back[:, column] for column in columns], axis=0)
-    return triple(split(back), last)
+    return product(back, last_ref[...])
 
 
 def send_blocks(full, block_x, block_y, put):
@@ -842,9 +862,10 @@
     tables_ref,
     last_ref,
     semaphores,
-    *second_refs,
+    *pair_refs,
 ):
     slabs = NG // block_y
+    second_refs, first_refs = pair_refs[:4], pair_refs[4:]
     bricks = NG // block_x
     parts = waves_ref.shape[0]
     block = static_ref.shape[2]
@@ -872,7 +893,15 @@
             ref[...] = jnp.zeros_like(ref)
         for brick in range(bricks):
             fields = atoms_ref[brick]
-            table = split(first_third(fields, waves_ref, cosine_ref, window, fields[6:7, :]))
+            table = first_third_split(
+                fields,
+                waves_ref,
+                cosine_ref,
+                window,
+                fields[6:7, :],
+                first_refs[2 * (brick % 2)],
+                first_refs[2 * (brick % 2) + 1],
+            )
             second = second_factors(
                 fields, 0, block_y, slabs, second_refs[2 * (brick % 2)], second_refs[2 * (brick % 2) + 1]
             )
@@ -903,7 +932,7 @@
 
 
 def early_pairs(parts):
-    return (5 * parts + 8) // 16
+    return parts // 4
 
 
 def spread_and_solve(
@@ -914,7 +943,7 @@
     bricks = NG // block_x
     parts = waves.shape[0]
     pairs = early_pairs(parts)
-    count = 2
+    count = 4
     anywhere = pl.BlockSpec(memory_space=pl.ANY)
     scalars = pl.BlockSpec(memory_space=pltpu.SMEM)
     sent_block = (2 * bricks, block_x // 8, count // 2, 8, 128)
@@ -942,7 +971,8 @@
             pltpu.VMEM(last.shape[1:], last.dtype),
             pltpu.SemaphoreType.DMA((3,)),
         ]
-        + [pltpu.VMEM((NG, slabs * atoms), jnp.bfloat16)] * 4,
+        + [pltpu.VMEM((NG, slabs * atoms), jnp.bfloat16)] * 4
+        + [pltpu.VMEM((parts * window, slabs * atoms), jnp.bfloat16)] * 4,
         compiler_params=pltpu.CompilerParams(vmem_limit_bytes=VMEM_BYTES),
         name="spread_and_solve",
     )(kappa, pair, static, waves, cosine_row, tables, last)
@@ -1058,7 +1088,6 @@
     block_y, early_ref, later_ref, sums_ref, short_ref, charge_ref, table_ref, out_ref, energy_ref
 ):
     atoms = short_ref.shape[1]
-    table = (table_ref[0], table_ref[1])
     lines = early_ref.shape[3]
     sources, _, pairs = early_ref.shape[:3]
     early = early_ref.reshape(sources * pairs, lines, 128)
@@ -1067,7 +1096,7 @@
     for line in range(lines):
         turned = jnp.concatenate([early[:, line, :], later[:, line, :]], axis=0).T
         pieces.append(jnp.concatenate([turned[0:block_y], turned[block_y:]], axis=1))
-    result = triple(split(jnp.concatenate(pieces, axis=0)), table)
+    result = product(jnp.concatenate(pieces, axis=0), table_ref[...])
     for line in range(lines):
         out_ref[line] = result[block_y * line : block_y * (line + 1)]
 
@@ -1104,13 +1133,6 @@
         compiler_params=pltpu.CompilerParams(vmem_limit_bytes=32 * 2**20),
         name="finish",
     )(early, later, later, short, charge, table)
-
-
-def two_parts(table):
-    table = np.asarray(table, np.float32)
-    high = table.astype(ml_dtypes.bfloat16)
-    low = (table - high.astype(np.float32)).astype(ml_dtypes.bfloat16)
-    return np.stack([high, low])
 
 
 def real_basis():
@@ -1196,13 +1218,13 @@
         [squared, jnp.exp(-0.5 * squared) * jnp.where(ends, 1.0 / NG, 2.0 / NG)], axis=1
     )
     basis = real_basis()
-    tables = np.concatenate([two_parts(basis), two_parts(basis.T)])
+    tables = np.stack([basis, basis.T]).astype(np.float32)
     last = []
     for p in range(count_y // 2):
         points = (2 * block_y * p + np.arange(2 * block_y + 8)) % NG
         columns = np.zeros((NG, NG))
         columns[:, : points.size] = basis[:, points]
-        last.append(two_parts(columns))
+        last.append(columns.astype(np.float32))
     cosine_row = np.cos(np.arange(128) * (2.0 * math.pi / NG)).astype(np.float32)[None]
     cosine_row = jnp.asarray(cosine_row)
     tables = jnp.asarray(tables)
@@ -1248,7 +1270,7 @@
         later,
         energy_short,
         charge,
-        jnp.asarray(two_parts(basis[order])),
+        jnp.asarray(basis[order].astype(np.float32)),
     )
     return atom_energy, potential
 

time: 113 us -> 101 us (0.89)
  blocking collectives: 16.3 us -> 0 us
  starting transfers between devices: 11.2 us -> 16.2 us
  waiting for transfers between devices: 26.9 us -> 24.7 us
    all_to_all x1 -> x0, blocking collectives: 16.3 us -> none  [exchange(): lax.all_to_all(values, axes, split_axis=0, concat_axis=0, tiled=True, axi...]
    all_to_all x2 -> x3, starting transfers between devices: 7.86 us -> 12.9 us  [exchange(): lax.all_to_all(values, axes, split_axis=0, concat_axis=0, tiled=True, axi...]
    pallas_call x1, Pallas kernels: 12.8 us -> 15 us  [solve_and_sample(): pl.pallas_call(functools.partial(sample_kernel, block_x, block_y, window)...]
    all_to_all x2 -> x3, waiting for transfers between devices: 22.7 us -> 20.5 us  [exchange(): lax.all_to_all(values, axes, split_axis=0, concat_axis=0, tiled=True, axi...]
  transfers between devices with their start and end apart: 4 -> 5, of which waited for: 4 -> 4; matrix products, arithmetic and copies ran while one was open for 1% -> 1% of each run, Pallas kernels for 4% -> 19%
where the time goes in v5:
time: 101 us; the launch traced here: 100 us
  Pallas kernels  55.1 us (55%)
  waiting for transfers between devices  24.7 us (24%)
  starting transfers between devices  16.2 us (16%)
  local copies, waits for them, and re-layouts  3.33 us (3%)
    all_to_all x3, waiting for transfers between devices, exchange(): lax.all_to_all(values, axes, split_axis=0, concat_axis=0, tiled=True, axi...  20.5 us
    pallas_call x1, Pallas kernels, spread_and_solve(): pl.pallas_call(functools.partial(spread_kernel, block_x, block_y, window)...  17 us
    pallas_call x1, Pallas kernels, solve_and_sample(): pl.pallas_call(functools.partial(sample_kernel, block_x, block_y, window)...  15 us
    pallas_call x1, Pallas kernels, networks(): pl.pallas_call(functools.partial(network_kernel, ghosts), grid=(1,), out_...  13.9 us
    all_to_all x3, starting transfers between devices, exchange(): lax.all_to_all(values, axes, split_axis=0, concat_axis=0, tiled=True, axi...  12.9 us
    pallas_call x1, Pallas kernels, energies(): pl.pallas_call(energy_kernel, grid=(1,), out_shape=result, in_specs=whole...  4.31 us
    pallas_call x1, Pallas kernels, finish(): pl.pallas_call(functools.partial(finish_kernel, block_y), grid=(groups,),...  3.48 us
    ppermute x1, starting transfers between devices, per_device(): upper = lax.ppermute(outgoing, 'brick', down)  3.33 us
  transfers between devices with their start and end apart: 5, of which 4 were waited for; matrix products, arithmetic and copies ran while one was open for 1% of the time, Pallas kernels for 19%

profile of v5, /device:TPU:0, one launch (start us, length us, event | category | flops | bytes accessed | tf_op | source)
XLA Modules:
  0.0 100.2 jit_solution(7550408804990001616)
XLA Ops:
  0.6 1.4 %collect_atoms.1 = (f32[8,256]{1,0:T(8,128)}, f32[8,256]{1,0:T(8,128)}) custom-call(f32[3,1,192]{2,1,0:T(1,128)} %positions_ref.1, s32[1,192]{1,0:T(1,128)} %types_ref.3, s32[1,192]{1,0:T(1,128)} %count_ref.1, s32[1,192]{1,0:T(1,128)} %send_ref.1), custom_call_target="tpu_custom_call" | custom-call | tf_op jit(solution)/shard_map/collect_atoms/pallas_call | solution.py:347
  2.0 3.3 %collective-permute-start.1 = (f32[8,256]{1,0:T(8,128)}, f32[8,256]{1,0:T(8,128)S(1)}, u32[]{:S(2)}, u32[]{:S(2)}) collective-permute-start(f32[8,256]{1,0:T(8,128)} %get-tuple-element.14), channel_id=1, source_target_pairs={{4,0},{8,4},{12,8},{16,12},{20,16},{24,20},{28,24},{0,28},{5,1},{9... | collective-permute-start | bytes 24584 | tf_op jit(solution)/shard_map/ppermute | solution.py:1191
  5.4 0.0 collective-permute-start
  5.4 1.6 %collective-permute-done.1.upper_ref = f32[8,256]{1,0:T(8,128)S(1)} collective-permute-done((f32[8,256]{1,0:T(8,128)}, f32[8,256]{1,0:T(8,128)S(1)}, u32[]{:S(2)}, u32[]{:S(2)}) %collective-permute-start.1) | collective-permute-done | bytes 8224 | tf_op jit(solution)/shard_map/ppermute | solution.py:1191
  7.0 0.0 copy-start.4
  7.0 2.6 %collective-permute-done.lower_ref = f32[8,256]{1,0:T(8,128)S(1)} collective-permute-done((f32[8,256]{1,0:T(8,128)}, f32[8,256]{1,0:T(8,128)S(1)}, u32[]{:S(2)}, u32[]{:S(2)}) %collective-permute-start) | collective-permute-done | bytes 8224 | tf_op jit(solution)/shard_map/ppermute | solution.py:1190
  9.6 0.0 copy-start.5
  9.6 0.0 copy-done.4
  9.6 0.6 copy-done.5
  10.2 13.9 %networks.1 = (f32[192,1600]{1,0:T(8,128)}, f32[1,192]{1,0:T(1,128)}, f32[32,8,192]{2,1,0:T(8,128)}) custom-call(s32[1]{0:T(128)} %bitcast.1.base_ref, f32[2]{0:T(128)} %charges_ref.1, f32[8,256]{1,0:T(8,128)} %get-tuple-element.13.own_ref, f32[8,256]{1,0:T(8,128)} %copy-done.5, f32[8,256]{1,0:T(8,128)} %copy-done.4, s32[64,192]{1,0:T(8,128)} %bitcast.20, ...), custom_call_target="tpu_custom_call" | custom-call | tf_op jit(solution)/shard_map/networks/pallas_call | solution.py:640
  24.0 4.2 %all-to-all-start = ((f32[32,8,192]{2,1,0:T(8,128)}), f32[32,8,192]{2,1,0:T(8,128)S(1)}, u32[]{:S(2)}, u32[]{:S(2)}) async-start(f32[32,8,192]{2,1,0:T(8,128)} %get-tuple-element.15), calls=%async_computation | async-start | bytes 524288 | tf_op jit(solution)/shard_map/all_to_all | solution.py:1183
  28.2 0.7 copy.27.waves_ref
  28.9 0.7 copy.26.kappa_ref
  29.6 9.0 %all-to-all-done.static_ref = f32[32,8,192]{2,1,0:T(8,128)S(1)} async-done(((f32[32,8,192]{2,1,0:T(8,128)}), f32[32,8,192]{2,1,0:T(8,128)S(1)}, u32[]{:S(2)}, u32[]{:S(2)}) %all-to-all-start) | async-done | bytes 196640 | tf_op jit(solution)/shard_map/all_to_all | solution.py:1183
  38.6 0.0 copy-start.3
  38.6 0.7 copy-done.3
  39.3 17.0 %spread_and_solve.1 = (f32[16,4,4,8,128]{4,3,2,1,0:T(8,128)}, f32[8,256,256]{2,1,0:T(8,128)}, f32[8,8,768]{2,1,0:T(8,128)}, f32[8,256,256]{2,1,0:T(8,128)}) custom-call(f32[16,2]{1,0:T(8,128)} %copy.26.kappa_ref, s32[1]{0:T(128)} %bitcast.pair_ref, f32[32,8,192]{2,1,0:T(8,128)} %copy-done.3, s32[16,2]{1,0:T(8,128)} %copy.27.waves_ref, ...), custom_call_target="tpu_custom_call" | custom-call | tf_op jit(solution)/shard_map/spread_and_solve/pallas_call | solution.py:950
  56.3 3.9 %all-to-all-start.1 = ((f32[16,128,128]{2,1,0:T(8,128)}), f32[16,128,128]{2,1,0:T(8,128)S(1)}, u32[]{:S(2)}, u32[]{:S(2)}) async-start(f32[16,128,128]{2,1,0:T(8,128)} %bitcast.19), calls=%async_computation.1 | async-start | bytes 2097152 | tf_op jit(solution)/shard_map/all_to_all | solution.py:1183
  60.2 15.0 %solve_and_sample.1 = f32[16,17,8,128]{3,2,1,0:T(8,128)} custom-call(f32[16,2]{1,0:T(8,128)} %copy.26.kappa_ref, s32[1]{0:T(128)} %bitcast.pair_ref, f32[8,8,768]{2,1,0:T(8,128)} %get-tuple-element.17.atoms_ref, s32[16,2]{1,0:T(8,128)} %copy.27.waves_ref, f32[1,128]{1,0:T(1,128)} %constant.64.clone.cosine_ref, f32[2,256,256]{2,1,0:T(8,128)} %constant.65.clone.tables_hbm, ...), custom_call_target="tpu_custom_call" | custom-call | flops 6442450944 | bytes 2097152 | tf_op jit(solution)/shard_map/solve_and_sample/pallas_call | solution.py:1065
  75.2 0.0 all-to-all-done.1
  75.2 4.8 %all-to-all-start.2 = ((f32[16,136,128]{2,1,0:T(8,128)}), f32[16,136,128]{2,1,0:T(8,128)S(1)}, u32[]{:S(2)}, u32[]{:S(2)}) async-start(f32[16,136,128]{2,1,0:T(8,128)} %bitcast.18), calls=%async_computation.2 | async-start | bytes 2228224 | tf_op jit(solution)/shard_map/all_to_all | solution.py:1183
  80.1 0.0 copy-start
  80.1 0.0 copy-start.2
  80.1 4.3 %energies.1.short_ref = f32[1,192]{1,0:T(1,128)} custom-call(f32[192,1600]{1,0:T(8,128)} %get-tuple-element.20.descriptor_ref, f32[240,1600]{1,0:T(8,128)} %bitcast.17, f32[2,240,240]{2,1,0:T(8,128)} %weight_hidden_ref.1, f32[1,240]{1,0:T(1,128)} %bitcast.22), custom_call_target="tpu_custom_call" | custom-call | flops 442368000 | bytes 1536000 | tf_op jit(solution)/shard_map/energies/pallas_call | solution.py:675
  84.4 11.6 %all-to-all-done.2 = f32[16,136,128]{2,1,0:T(8,128)S(1)} async-done(((f32[16,136,128]{2,1,0:T(8,128)}), f32[16,136,128]{2,1,0:T(8,128)S(1)}, u32[]{:S(2)}, u32[]{:S(2)}) %all-to-all-start.2) | async-done | bytes 1114144 | tf_op jit(solution)/shard_map/all_to_all | solution.py:1183
  96.0 0.0 copy-done
  96.0 0.0 copy-done.2
  96.0 0.0 copy-start.1
  96.0 0.7 copy-done.1
  96.7 3.5 %finish.1 = (f32[32,64,256]{2,1,0:T(8,128)}, f32[1,192]{1,0:T(1,128)}) custom-call(f32[16,4,4,8,128]{4,3,2,1,0:T(8,128)S(1)} %bitcast.15, f32[16,17,8,128]{3,2,1,0:T(8,128)S(1)} %bitcast.13, f32[16,17,8,128]{3,2,1,0:T(8,128)S(1)} %bitcast.14, f32[1,192]{1,0:T(1,128)S(1)} %copy-done.1, f32[1,192]{1,0:T(1,128)S(1)} %copy-done.2, f32[256,256]{1,0:T(8,128)S(1)} %copy-done), custom_call_target="tpu_custom_call" | custom-call | tf_op jit(solution)/shard_map/finish/pallas_call | solution.py:1114
  (4 shorter events, 0.0 us)
Async XLA Ops:
  2.0 4.9 %collective-permute-start.1 = (f32[8,256]{1,0:T(8,128)}, f32[8,256]{1,0:T(8,128)S(1)}, u32[]{:S(2)}, u32[]{:S(2)}) collective-permute-start(f32[8,256]{1,0:T(8,128)} %get-tuple-element.14), channel_id=1, source_target_pairs={{4,0},{8,4},{12,8},{16,12},{20,16},{24,20},{28,24},{0,28},{5,1},{9... | collective-permute-start | bytes 24584 | tf_op jit(solution)/shard_map/ppermute | solution.py:1191
  5.4 4.2 %collective-permute-start = (f32[8,256]{1,0:T(8,128)}, f32[8,256]{1,0:T(8,128)S(1)}, u32[]{:S(2)}, u32[]{:S(2)}) collective-permute-start(f32[8,256]{1,0:T(8,128)} %get-tuple-element.14), channel_id=1, source_target_pairs={{0,4},{4,8},{8,12},{12,16},{16,20},{20,24},{24,28},{28,0},{1,5},{5... | collective-permute-start | bytes 24584 | tf_op jit(solution)/shard_map/ppermute | solution.py:1190
  7.0 2.6 %copy-start.4 = (f32[8,256]{1,0:T(8,128)}, f32[8,256]{1,0:T(8,128)S(1)}, u32[]{:S(2)}) copy-start(f32[8,256]{1,0:T(8,128)S(1)} %collective-permute-done.1.upper_ref) | copy-start | bytes 24580
  9.6 0.6 copy-start.5
  24.0 14.6 %all-to-all-start = ((f32[32,8,192]{2,1,0:T(8,128)}), f32[32,8,192]{2,1,0:T(8,128)S(1)}, u32[]{:S(2)}, u32[]{:S(2)}) async-start(f32[32,8,192]{2,1,0:T(8,128)} %get-tuple-element.15), calls=%async_computation | async-start | bytes 524288 | tf_op jit(solution)/shard_map/all_to_all | solution.py:1183
  38.6 0.7 copy-start.3
  56.3 18.9 %all-to-all-start.1 = ((f32[16,128,128]{2,1,0:T(8,128)}), f32[16,128,128]{2,1,0:T(8,128)S(1)}, u32[]{:S(2)}, u32[]{:S(2)}) async-start(f32[16,128,128]{2,1,0:T(8,128)} %bitcast.19), calls=%async_computation.1 | async-start | bytes 2097152 | tf_op jit(solution)/shard_map/all_to_all | solution.py:1183
  75.2 20.7 %all-to-all-start.2 = ((f32[16,136,128]{2,1,0:T(8,128)}), f32[16,136,128]{2,1,0:T(8,128)S(1)}, u32[]{:S(2)}, u32[]{:S(2)}) async-start(f32[16,136,128]{2,1,0:T(8,128)} %bitcast.18), calls=%async_computation.2 | async-start | bytes 2228224 | tf_op jit(solution)/shard_map/all_to_all | solution.py:1183
  80.1 15.9 %copy-start = (f32[256,256]{1,0:T(8,128)S(1)}, f32[256,256]{1,0:T(8,128)}, u32[]{:S(2)}) copy-start(f32[256,256]{1,0:T(8,128)} %constant.67.clone.table_ref) | copy-start | bytes 786436
  80.1 15.9 %copy-start.2 = (f32[1,192]{1,0:T(1,128)S(1)}, f32[1,192]{1,0:T(1,128)}, u32[]{:S(2)}) copy-start(f32[1,192]{1,0:T(1,128)} %get-tuple-element.21.charge_ref) | copy-start | bytes 2308
  96.0 0.7 copy-start.1

commit v6 on v5

--- a/solution.py
+++ b/solution.py
@@ -12,6 +12,7 @@
 NG = 256
 AXIS = 16
 VMEM_BYTES = 60 * 2**20
+REACH = 16
 
 
 HIGH = lax.Precision.HIGHEST
@@ -730,20 +731,6 @@
     return jnp.concatenate(pieces, axis=1)
 
 
-def first_third(fields, waves_ref, cosine_ref, window, scale):
-    atoms = fields.shape[1]
-    third = third_factors(fields, waves_ref, cosine_ref)
-    if scale is not None:
-        third = third * scale
-    rows = lax.broadcasted_iota(jnp.int32, (window, atoms), 0)
-    first = placed_weights(
-        rows - fields[0:1, :].astype(jnp.int32), weight_rows(fields[3:4, :])
-    )
-    return jnp.concatenate(
-        [first * third[part : part + 1, :] for part in range(third.shape[0])], axis=0
-    )
-
-
 def first_third_split(fields, waves_ref, cosine_ref, window, scale, high_ref, low_ref):
     atoms = fields.shape[1]
     third = third_factors(fields, waves_ref, cosine_ref) * scale
@@ -769,7 +756,7 @@
 def second_factors(fields, base, block_y, slabs, high_ref, low_ref):
     atoms = fields.shape[1]
     block = atoms // slabs
-    reach = block_y + 16
+    reach = block_y + REACH
     start = fields[1:2, :].astype(jnp.int32) - base
     weights = weight_rows(fields[4:5, :])
     for chunk in range(atoms // 128):
@@ -812,19 +799,19 @@
     square_y, damp_y = damping(lax.broadcasted_iota(jnp.int32, (1, NG), 1))
     square_xy = square_x + square_y
     damp_xy = damp_x * damp_y
-    columns = [slice(NG * part, NG * (part + 1)) for part in range(count)]
-    first = product(basis, jnp.concatenate(planes, axis=1))
-    first = jnp.concatenate([first[:, column] for column in columns], axis=0)
-    both = product(first, turned)
+    bands = [slice(NG * part, NG * (part + 1)) for part in range(count)]
+
+    def flip(values):
+        return jnp.concatenate([values[band].T for band in bands], axis=0)
+
+    both = product(flip(product(jnp.concatenate(planes, axis=0), turned)), turned)
     scaled = []
     for part in range(count):
         squared = square_xy + kappa_ref[first_part + part, 0]
         root = jnp.where(squared == 0.0, 1.0, 0.0)
         green = (1.0 - root) * (damp_xy * kappa_ref[first_part + part, 1]) / (squared + root)
-        scaled.append(both[columns[part]] * green)
-    back = product(turned, jnp.concatenate(scaled, axis=1))
-    back = jnp.concatenate([back[:, column] for column in columns], axis=0)
-    return product(back, last_ref[...])
+        scaled.append(both[bands[part]] * green)
+    return product(flip(product(jnp.concatenate(scaled, axis=0), basis)), last_ref[...])
 
 
 def send_blocks(full, block_x, block_y, put):
@@ -997,7 +984,7 @@
     tables_ref,
     last_ref,
     semaphores,
-    *second_refs,
+    packed_ref,
 ):
     bricks = atoms_ref.shape[0]
     parts = waves_ref.shape[0]
@@ -1025,29 +1012,49 @@
     send_blocks(full, block_x, block_y, put)
     fetches[3].wait()
 
-    for ref in second_refs:
-        ref[...] = jnp.zeros_like(ref)
+    reach = block_y + REACH
+    lane = lax.broadcasted_iota(jnp.int32, (NG, 128), 1)
+    for part in range(parts):
+        for side in range(2):
+            values = full_ref[part, :, 128 * side : 128 * (side + 1)]
+            high = values.astype(jnp.bfloat16).astype(jnp.float32)
+            again = pltpu.roll(high, reach, 1)
+            low = pltpu.roll(values - high, 2 * reach - 128, 1)
+            packed_ref[side, part, 0:NG, 0:128] = jnp.where(lane < reach, high, again)
+            packed_ref[side, part, 0:NG, 128:NG] = jnp.where(
+                lane < 2 * reach - 128, again, jnp.where(lane < 3 * reach - 128, low, 0.0)
+            )
+            packed_ref[side, part, NG : NG + window - block_x, :] = packed_ref[
+                side, part, 0 : window - block_x, :
+            ]
     extra = sent_ref.shape[1] - 1
     base = 2 * block_y * pair_ref[0]
     lanes = pl.ds(pl.multiple_of(2 * block * pair_ref[0], 128), 2 * block)
     for brick in range(bricks):
         fields = atoms_ref[brick, :, lanes]
-        weights = first_third(fields, waves_ref, cosine_ref, window, None)
-        start = block_x * brick
-        inside = min(window, NG - start)
-        values = []
-        for part in range(parts):
-            values.append(full_ref[part, start : start + inside, :])
-            if inside < window:
-                values.append(full_ref[part, 0 : window - inside, :])
-        values = split(jnp.concatenate(values, axis=0))
-        second = second_factors(
-            fields, base, block_y, 2, second_refs[2 * (brick % 2)], second_refs[2 * (brick % 2) + 1]
-        )
-        along = triple(values, second)
-        sums = jnp.sum(along * weights, axis=0, keepdims=True)
+        thirds = third_factors(fields, waves_ref, cosine_ref)
+        rows = slice(block_x * brick, block_x * brick + window)
         for side in range(2):
-            row = sums[:, block * side : block * (side + 1)]
+            here = slice(block * side, block * (side + 1))
+            third = thirds[:, here]
+            ours = fields[:, here]
+            index = lax.broadcasted_iota(jnp.int32, (window, block), 0)
+            first = placed_weights(
+                index - ours[0:1, :].astype(jnp.int32), weight_rows(ours[3:4, :])
+            )
+            index = lax.broadcasted_iota(jnp.int32, (reach, block), 0)
+            start = ours[1:2, :].astype(jnp.int32) - (base + block_y * side)
+            high, low = split(placed_weights(index - start, weight_rows(ours[4:5, :])))
+            rest = jnp.zeros((NG - 3 * reach, block), jnp.bfloat16)
+            second = jnp.concatenate([high, low, high, rest], axis=0)
+            values = jnp.concatenate(
+                [packed_ref[side, part, rows, :] for part in range(parts)], axis=0
+            )
+            along = multiply(values.astype(jnp.bfloat16), second, ((1,), (0,)))
+            total = jnp.zeros((window, block), jnp.float32)
+            for part in range(parts):
+                total = total + along[window * part : window * (part + 1)] * third[part : part + 1]
+            row = jnp.sum(total * first, axis=0, keepdims=True)
             sent_ref[2 * brick + side, extra] = jnp.zeros((8, 128), jnp.float32)
             sent_ref[2 * brick + side, extra, 0:1, :] = row[:, 0:128]
             sent_ref[2 * brick + side, extra, 1:2, 0 : block - 128] = row[:, 128:block]
@@ -1075,7 +1082,7 @@
             pltpu.VMEM(last.shape[1:], last.dtype),
             pltpu.SemaphoreType.DMA((4,)),
         ]
-        + [pltpu.VMEM((NG, 2 * atoms.shape[2] * block_y // NG), jnp.bfloat16)] * 4,
+        + [pltpu.VMEM((2, parts, NG + window - block_x, NG), jnp.float32)],
         compiler_params=pltpu.CompilerParams(vmem_limit_bytes=VMEM_BYTES),
         cost_estimate=pl.CostEstimate(
             flops=24 * parts * NG * NG * NG, bytes_accessed=4 * early.size, transcendentals=0
@@ -1221,7 +1228,10 @@
     tables = np.stack([basis, basis.T]).astype(np.float32)
     last = []
     for p in range(count_y // 2):
-        points = (2 * block_y * p + np.arange(2 * block_y + 8)) % NG
+        points = np.concatenate(
+            [np.arange(2 * block_y), block_y + np.arange(block_y + REACH)]
+        )
+        points = (2 * block_y * p + points) % NG
         columns = np.zeros((NG, NG))
         columns[:, : points.size] = basis[:, points]
         last.append(columns.astype(np.float32))

time: 101 us -> 101 us (level)
    pallas_call x1, Pallas kernels: 17 us -> 18.5 us  [spread_and_solve(): pl.pallas_call(functools.partial(spread_kernel, block_x, block_y, window)...]
  transfers between devices with their start and end apart: 5 -> 5, of which waited for: 4 -> 5; matrix products, arithmetic and copies ran while one was open for 1% -> 1% of each run, Pallas kernels for 19% -> 18%
where the time goes in v6:
time: 101 us
  Pallas kernels  55.6 us (55%)
  waiting for transfers between devices  25.4 us (25%)
  starting transfers between devices  15.6 us (15%)
  local copies, waits for them, and re-layouts  3.33 us (3%)
    all_to_all x3, waiting for transfers between devices, exchange(): lax.all_to_all(values, axes, split_axis=0, concat_axis=0, tiled=True, axi...  21.2 us
    pallas_call x1, Pallas kernels, spread_and_solve(): pl.pallas_call(functools.partial(spread_kernel, block_x, block_y, window)...  18.5 us
    pallas_call x1, Pallas kernels, solve_and_sample(): pl.pallas_call(functools.partial(sample_kernel, block_x, block_y, window)...  14 us
    pallas_call x1, Pallas kernels, networks(): pl.pallas_call(functools.partial(network_kernel, ghosts), grid=(1,), out_...  13.9 us
    all_to_all x3, starting transfers between devices, exchange(): lax.all_to_all(values, axes, split_axis=0, concat_axis=0, tiled=True, axi...  12.3 us
    pallas_call x1, Pallas kernels, energies(): pl.pallas_call(energy_kernel, grid=(1,), out_shape=result, in_specs=whole...  4.31 us
    pallas_call x1, Pallas kernels, finish(): pl.pallas_call(functools.partial(finish_kernel, block_y), grid=(groups,),...  3.48 us
    ppermute x1, starting transfers between devices, per_device(): upper = lax.ppermute(outgoing, 'brick', down)  3.33 us
  transfers between devices with their start and end apart: 5, of which 5 were waited for; matrix products, arithmetic and copies ran while one was open for 1% of the time, Pallas kernels for 18%

profile of v6, /device:TPU:0, one launch (start us, length us, event | category | flops | bytes accessed | tf_op | source)
XLA Modules:
  0.0 100.7 jit_solution(15031877553481706037)
XLA Ops:
  0.6 1.4 %collect_atoms.1 = (f32[8,256]{1,0:T(8,128)}, f32[8,256]{1,0:T(8,128)}) custom-call(f32[3,1,192]{2,1,0:T(1,128)} %positions_ref.1, s32[1,192]{1,0:T(1,128)} %types_ref.3, s32[1,192]{1,0:T(1,128)} %count_ref.1, s32[1,192]{1,0:T(1,128)} %send_ref.1), custom_call_target="tpu_custom_call" | custom-call | tf_op jit(solution)/shard_map/collect_atoms/pallas_call | solution.py:348
  2.0 3.3 %collective-permute-start.1 = (f32[8,256]{1,0:T(8,128)}, f32[8,256]{1,0:T(8,128)S(1)}, u32[]{:S(2)}, u32[]{:S(2)}) collective-permute-start(f32[8,256]{1,0:T(8,128)} %get-tuple-element.14), channel_id=1, source_target_pairs={{4,0},{8,4},{12,8},{16,12},{20,16},{24,20},{28,24},{0,28},{5,1},{9... | collective-permute-start | bytes 24584 | tf_op jit(solution)/shard_map/ppermute | solution.py:1198
  5.4 0.0 collective-permute-start
  5.4 1.6 %collective-permute-done.1.upper_ref = f32[8,256]{1,0:T(8,128)S(1)} collective-permute-done((f32[8,256]{1,0:T(8,128)}, f32[8,256]{1,0:T(8,128)S(1)}, u32[]{:S(2)}, u32[]{:S(2)}) %collective-permute-start.1) | collective-permute-done | bytes 8224 | tf_op jit(solution)/shard_map/ppermute | solution.py:1198
  7.0 0.0 copy-start.4
  7.0 2.6 %collective-permute-done.lower_ref = f32[8,256]{1,0:T(8,128)S(1)} collective-permute-done((f32[8,256]{1,0:T(8,128)}, f32[8,256]{1,0:T(8,128)S(1)}, u32[]{:S(2)}, u32[]{:S(2)}) %collective-permute-start) | collective-permute-done | bytes 8224 | tf_op jit(solution)/shard_map/ppermute | solution.py:1197
  9.6 0.0 copy-start.5
  9.6 0.0 copy-done.4
  9.6 0.6 copy-done.5
  10.2 13.9 %networks.1 = (f32[192,1600]{1,0:T(8,128)}, f32[1,192]{1,0:T(1,128)}, f32[32,8,192]{2,1,0:T(8,128)}) custom-call(s32[1]{0:T(128)} %bitcast.1.base_ref, f32[2]{0:T(128)} %charges_ref.1, f32[8,256]{1,0:T(8,128)} %get-tuple-element.13.own_ref, f32[8,256]{1,0:T(8,128)} %copy-done.5, f32[8,256]{1,0:T(8,128)} %copy-done.4, s32[64,192]{1,0:T(8,128)} %bitcast.20, ...), custom_call_target="tpu_custom_call" | custom-call | tf_op jit(solution)/shard_map/networks/pallas_call | solution.py:641
  24.0 4.2 %all-to-all-start = ((f32[32,8,192]{2,1,0:T(8,128)}), f32[32,8,192]{2,1,0:T(8,128)S(1)}, u32[]{:S(2)}, u32[]{:S(2)}) async-start(f32[32,8,192]{2,1,0:T(8,128)} %get-tuple-element.15), calls=%async_computation | async-start | bytes 524288 | tf_op jit(solution)/shard_map/all_to_all | solution.py:1190
  28.2 0.7 copy.27.waves_ref
  28.9 0.7 copy.26.kappa_ref
  29.6 9.0 %all-to-all-done.static_ref = f32[32,8,192]{2,1,0:T(8,128)S(1)} async-done(((f32[32,8,192]{2,1,0:T(8,128)}), f32[32,8,192]{2,1,0:T(8,128)S(1)}, u32[]{:S(2)}, u32[]{:S(2)}) %all-to-all-start) | async-done | bytes 196640 | tf_op jit(solution)/shard_map/all_to_all | solution.py:1190
  38.6 0.0 copy-start.3
  38.6 0.7 copy-done.3
  39.3 18.5 %spread_and_solve.1 = (f32[16,4,4,8,128]{4,3,2,1,0:T(8,128)}, f32[8,256,256]{2,1,0:T(8,128)}, f32[8,8,768]{2,1,0:T(8,128)}, f32[8,256,256]{2,1,0:T(8,128)}) custom-call(f32[16,2]{1,0:T(8,128)} %copy.26.kappa_ref, s32[1]{0:T(128)} %bitcast.pair_ref, f32[32,8,192]{2,1,0:T(8,128)} %copy-done.3, s32[16,2]{1,0:T(8,128)} %copy.27.waves_ref, ...), custom_call_target="tpu_custom_call" | custom-call | tf_op jit(solution)/shard_map/spread_and_solve/pallas_call | solution.py:937
  57.8 3.9 %all-to-all-start.1 = ((f32[16,128,128]{2,1,0:T(8,128)}), f32[16,128,128]{2,1,0:T(8,128)S(1)}, u32[]{:S(2)}, u32[]{:S(2)}) async-start(f32[16,128,128]{2,1,0:T(8,128)} %bitcast.19), calls=%async_computation.1 | async-start | bytes 2097152 | tf_op jit(solution)/shard_map/all_to_all | solution.py:1190
  61.7 14.0 %solve_and_sample.1 = f32[16,17,8,128]{3,2,1,0:T(8,128)} custom-call(f32[16,2]{1,0:T(8,128)} %copy.26.kappa_ref, s32[1]{0:T(128)} %bitcast.pair_ref, f32[8,8,768]{2,1,0:T(8,128)} %get-tuple-element.17.atoms_ref, s32[16,2]{1,0:T(8,128)} %copy.27.waves_ref, f32[1,128]{1,0:T(1,128)} %constant.64.clone.cosine_ref, f32[2,256,256]{2,1,0:T(8,128)} %constant.65.clone.tables_hbm, ...), custom_call_target="tpu_custom_call" | custom-call | flops 6442450944 | bytes 2097152 | tf_op jit(solution)/shard_map/solve_and_sample/pallas_call | solution.py:1072
  75.7 0.7 all-to-all-done.1
  76.4 4.2 %all-to-all-start.2 = ((f32[16,136,128]{2,1,0:T(8,128)}), f32[16,136,128]{2,1,0:T(8,128)S(1)}, u32[]{:S(2)}, u32[]{:S(2)}) async-start(f32[16,136,128]{2,1,0:T(8,128)} %bitcast.18), calls=%async_computation.2 | async-start | bytes 2228224 | tf_op jit(solution)/shard_map/all_to_all | solution.py:1190
  80.6 0.0 copy-start
  80.6 0.0 copy-start.2
  80.6 4.3 %energies.1.short_ref = f32[1,192]{1,0:T(1,128)} custom-call(f32[192,1600]{1,0:T(8,128)} %get-tuple-element.20.descriptor_ref, f32[240,1600]{1,0:T(8,128)} %bitcast.17, f32[2,240,240]{2,1,0:T(8,128)} %weight_hidden_ref.1, f32[1,240]{1,0:T(1,128)} %bitcast.22), custom_call_target="tpu_custom_call" | custom-call | flops 442368000 | bytes 1536000 | tf_op jit(solution)/shard_map/energies/pallas_call | solution.py:676
  84.9 11.6 %all-to-all-done.2 = f32[16,136,128]{2,1,0:T(8,128)S(1)} async-done(((f32[16,136,128]{2,1,0:T(8,128)}), f32[16,136,128]{2,1,0:T(8,128)S(1)}, u32[]{:S(2)}, u32[]{:S(2)}) %all-to-all-start.2) | async-done | bytes 1114144 | tf_op jit(solution)/shard_map/all_to_all | solution.py:1190
  96.5 0.0 copy-done
  96.5 0.0 copy-done.2
  96.5 0.0 copy-start.1
  96.5 0.7 copy-done.1
  97.2 3.5 %finish.1 = (f32[32,64,256]{2,1,0:T(8,128)}, f32[1,192]{1,0:T(1,128)}) custom-call(f32[16,4,4,8,128]{4,3,2,1,0:T(8,128)S(1)} %bitcast.15, f32[16,17,8,128]{3,2,1,0:T(8,128)S(1)} %bitcast.13, f32[16,17,8,128]{3,2,1,0:T(8,128)S(1)} %bitcast.14, f32[1,192]{1,0:T(1,128)S(1)} %copy-done.1, f32[1,192]{1,0:T(1,128)S(1)} %copy-done.2, f32[256,256]{1,0:T(8,128)S(1)} %copy-done), custom_call_target="tpu_custom_call" | custom-call | tf_op jit(solution)/shard_map/finish/pallas_call | solution.py:1121
  (4 shorter events, 0.0 us)
Async XLA Ops:
  2.0 4.9 %collective-permute-start.1 = (f32[8,256]{1,0:T(8,128)}, f32[8,256]{1,0:T(8,128)S(1)}, u32[]{:S(2)}, u32[]{:S(2)}) collective-permute-start(f32[8,256]{1,0:T(8,128)} %get-tuple-element.14), channel_id=1, source_target_pairs={{4,0},{8,4},{12,8},{16,12},{20,16},{24,20},{28,24},{0,28},{5,1},{9... | collective-permute-start | bytes 24584 | tf_op jit(solution)/shard_map/ppermute | solution.py:1198
  5.4 4.2 %collective-permute-start = (f32[8,256]{1,0:T(8,128)}, f32[8,256]{1,0:T(8,128)S(1)}, u32[]{:S(2)}, u32[]{:S(2)}) collective-permute-start(f32[8,256]{1,0:T(8,128)} %get-tuple-element.14), channel_id=1, source_target_pairs={{0,4},{4,8},{8,12},{12,16},{16,20},{20,24},{24,28},{28,0},{1,5},{5... | collective-permute-start | bytes 24584 | tf_op jit(solution)/shard_map/ppermute | solution.py:1197
  7.0 2.6 %copy-start.4 = (f32[8,256]{1,0:T(8,128)}, f32[8,256]{1,0:T(8,128)S(1)}, u32[]{:S(2)}) copy-start(f32[8,256]{1,0:T(8,128)S(1)} %collective-permute-done.1.upper_ref) | copy-start | bytes 24580
  9.6 0.6 copy-start.5
  24.0 14.6 %all-to-all-start = ((f32[32,8,192]{2,1,0:T(8,128)}), f32[32,8,192]{2,1,0:T(8,128)S(1)}, u32[]{:S(2)}, u32[]{:S(2)}) async-start(f32[32,8,192]{2,1,0:T(8,128)} %get-tuple-element.15), calls=%async_computation | async-start | bytes 524288 | tf_op jit(solution)/shard_map/all_to_all | solution.py:1190
  38.6 0.7 copy-start.3
  57.8 18.6 %all-to-all-start.1 = ((f32[16,128,128]{2,1,0:T(8,128)}), f32[16,128,128]{2,1,0:T(8,128)S(1)}, u32[]{:S(2)}, u32[]{:S(2)}) async-start(f32[16,128,128]{2,1,0:T(8,128)} %bitcast.19), calls=%async_computation.1 | async-start | bytes 2097152 | tf_op jit(solution)/shard_map/all_to_all | solution.py:1190
  76.4 20.1 %all-to-all-start.2 = ((f32[16,136,128]{2,1,0:T(8,128)}), f32[16,136,128]{2,1,0:T(8,128)S(1)}, u32[]{:S(2)}, u32[]{:S(2)}) async-start(f32[16,136,128]{2,1,0:T(8,128)} %bitcast.18), calls=%async_computation.2 | async-start | bytes 2228224 | tf_op jit(solution)/shard_map/all_to_all | solution.py:1190
  80.6 15.9 %copy-start = (f32[256,256]{1,0:T(8,128)S(1)}, f32[256,256]{1,0:T(8,128)}, u32[]{:S(2)}) copy-start(f32[256,256]{1,0:T(8,128)} %constant.67.clone.table_ref) | copy-start | bytes 786436
  80.6 15.9 %copy-start.2 = (f32[1,192]{1,0:T(1,128)S(1)}, f32[1,192]{1,0:T(1,128)}, u32[]{:S(2)}) copy-start(f32[1,192]{1,0:T(1,128)} %get-tuple-element.21.charge_ref) | copy-start | bytes 2308
  96.5 0.7 copy-start.1

commit v7 on v6

--- a/solution.py
+++ b/solution.py
@@ -799,19 +799,19 @@
     square_y, damp_y = damping(lax.broadcasted_iota(jnp.int32, (1, NG), 1))
     square_xy = square_x + square_y
     damp_xy = damp_x * damp_y
-    bands = [slice(NG * part, NG * (part + 1)) for part in range(count)]
-
-    def flip(values):
-        return jnp.concatenate([values[band].T for band in bands], axis=0)
-
-    both = product(flip(product(jnp.concatenate(planes, axis=0), turned)), turned)
+    columns = [slice(NG * part, NG * (part + 1)) for part in range(count)]
+    first = product(basis, jnp.concatenate(planes, axis=1))
+    first = jnp.concatenate([first[:, column] for column in columns], axis=0)
+    both = product(first, turned)
     scaled = []
     for part in range(count):
         squared = square_xy + kappa_ref[first_part + part, 0]
         root = jnp.where(squared == 0.0, 1.0, 0.0)
         green = (1.0 - root) * (damp_xy * kappa_ref[first_part + part, 1]) / (squared + root)
-        scaled.append(both[bands[part]] * green)
-    return product(flip(product(jnp.concatenate(scaled, axis=0), basis)), last_ref[...])
+        scaled.append(both[columns[part]] * green)
+    back = product(turned, jnp.concatenate(scaled, axis=1))
+    back = jnp.concatenate([back[:, column] for column in columns], axis=0)
+    return product(back, last_ref[...])
 
 
 def send_blocks(full, block_x, block_y, put):
@@ -841,6 +841,7 @@
     cosine_ref,
     tables_hbm,
     last_hbm,
+    short_hbm,
     sent_ref,
     full_ref,
     atoms_ref,
@@ -923,7 +924,7 @@
 
 
 def spread_and_solve(
-    block_x, block_y, window, kappa, pair, static, waves, cosine_row, tables, last
+    block_x, block_y, window, kappa, pair, static, waves, cosine_row, tables, last, short
 ):
     devices, _, atoms = static.shape
     slabs = NG // block_y
@@ -945,7 +946,7 @@
         ],
         in_specs=[scalars, scalars]
         + whole_specs(static, waves, cosine_row)
-        + [anywhere, anywhere],
+        + [anywhere, anywhere, anywhere],
         out_specs=[
             pl.BlockSpec(sent_block, lambda step: (0, 0, step, 0, 0)),
             pl.BlockSpec((count, NG, NG), lambda step: (step, 0, 0)),
@@ -962,7 +963,7 @@
         + [pltpu.VMEM((parts * window, slabs * atoms), jnp.bfloat16)] * 4,
         compiler_params=pltpu.CompilerParams(vmem_limit_bytes=VMEM_BYTES),
         name="spread_and_solve",
-    )(kappa, pair, static, waves, cosine_row, tables, last)
+    )(kappa, pair, static, waves, cosine_row, tables, last, short)
 
 
 def sample_kernel(
@@ -1092,9 +1093,30 @@
 
 
 def finish_kernel(
-    block_y, early_ref, later_ref, sums_ref, short_ref, charge_ref, table_ref, out_ref, energy_ref
+    block_y,
+    early_ref,
+    later_ref,
+    sums_ref,
+    short_hbm,
+    charge_hbm,
+    table_ref,
+    out_ref,
+    energy_ref,
+    short_ref,
+    charge_ref,
+    semaphores,
 ):
     atoms = short_ref.shape[1]
+    fetches = [
+        pltpu.make_async_copy(short_hbm, short_ref, semaphores.at[0]),
+        pltpu.make_async_copy(charge_hbm, charge_ref, semaphores.at[1]),
+    ]
+
+    @pl.when(pl.program_id(0) == 0)
+    def _():
+        for fetch in fetches:
+            fetch.start()
+
     lines = early_ref.shape[3]
     sources, _, pairs = early_ref.shape[:3]
     early = early_ref.reshape(sources * pairs, lines, 128)
@@ -1109,6 +1131,8 @@
 
     @pl.when(pl.program_id(0) == 0)
     def _():
+        for fetch in fetches:
+            fetch.wait()
         total = jnp.sum(sums_ref[:, 0], axis=0)
         potential_at = jnp.concatenate([total[0:1, :], total[1:2, 0 : atoms - 128]], axis=1)
         energy_ref[...] = short_ref[...] + 0.5 * charge_ref[...] * potential_at
@@ -1129,13 +1153,18 @@
             pl.BlockSpec((bricks2, 1, pairs, 8, 128), lambda index: (0, index, 0, 0, 0)),
             pl.BlockSpec((bricks2, rest, 8, 128), lambda index: (0, index, 0, 0)),
             pl.BlockSpec((bricks2, 1, 8, 128), lambda index: (0, groups * rest, 0, 0)),
-            whole((1, atoms)),
-            whole((1, atoms)),
+            pl.BlockSpec(memory_space=pltpu.HBM),
+            pl.BlockSpec(memory_space=pltpu.HBM),
             whole(table.shape),
         ],
         out_specs=[
             pl.BlockSpec((8, block_y, NG), lambda index: (index, 0, 0)),
             whole((1, atoms)),
+        ],
+        scratch_shapes=[
+            pltpu.VMEM((1, atoms), jnp.float32),
+            pltpu.VMEM((1, atoms), jnp.float32),
+            pltpu.SemaphoreType.DMA((2,)),
         ],
         compiler_params=pltpu.CompilerParams(vmem_limit_bytes=32 * 2**20),
         name="finish",
@@ -1239,8 +1268,19 @@
     cosine_row = jnp.asarray(cosine_row)
     tables = jnp.asarray(tables)
     last = jnp.asarray(np.stack(last))
+    energy_short = energies(descriptor, energy_in, energy_hidden, energy_out)
     early, full, every_atom, later = spread_and_solve(
-        block_x, block_y, window, kappa, pair, every_field, waves, cosine_row, tables, last
+        block_x,
+        block_y,
+        window,
+        kappa,
+        pair,
+        every_field,
+        waves,
+        cosine_row,
+        tables,
+        last,
+        energy_short,
     )
 
     def send(values):
@@ -1263,7 +1303,6 @@
         full,
     )
     later = send(later)
-    energy_short = energies(descriptor, energy_in, energy_hidden, energy_out)
     source = np.arange(2 * count_x)[:, None] * parts
     pairs = 2 * np.arange(parts // 2)[None, :]
     order = np.concatenate(

time: 101 us -> 99.5 us (0.985)
  blocking collectives: 0 us -> 20.4 us
  waiting for transfers between devices: 25.4 us -> 10.2 us
  starting transfers between devices: 15.6 us -> 11.2 us
  Pallas kernels: 55.6 us -> 53.6 us
    all_to_all x0 -> x1, blocking collectives: none -> 20.4 us  [exchange(): lax.all_to_all(values, axes, split_axis=0, concat_axis=0, tiled=True, axi...]
    all_to_all x3 -> x2, waiting for transfers between devices: 21.2 us -> 6.02 us  [exchange(): lax.all_to_all(values, axes, split_axis=0, concat_axis=0, tiled=True, axi...]
    all_to_all x3 -> x2, starting transfers between devices: 12.3 us -> 7.85 us  [exchange(): lax.all_to_all(values, axes, split_axis=0, concat_axis=0, tiled=True, axi...]
    pallas_call x1, Pallas kernels: 18.5 us -> 17 us  [spread_and_solve(): pl.pallas_call(functools.partial(spread_kernel, block_x, block_y, window)...]
  transfers between devices with their start and end apart: 5 -> 4, of which waited for: 5 -> 4; matrix products, arithmetic and copies ran while one was open for 1% -> 1% of each run, Pallas kernels for 18% -> 18%
where the time goes in v7:
time: 99.5 us; the launch traced here: 99.1 us
  Pallas kernels  53.6 us (54%)
  blocking collectives  20.4 us (21%)
  starting transfers between devices  11.2 us (11%)
  waiting for transfers between devices  10.2 us (10%)
  local copies, waits for them, and re-layouts  2.68 us (3%)
    all_to_all x1, blocking collectives, exchange(): lax.all_to_all(values, axes, split_axis=0, concat_axis=0, tiled=True, axi...  20.4 us
    pallas_call x1, Pallas kernels, spread_and_solve(): pl.pallas_call(functools.partial(spread_kernel, block_x, block_y, window)...  17 us
    pallas_call x1, Pallas kernels, networks(): pl.pallas_call(functools.partial(network_kernel, ghosts), grid=(1,), out_...  13.9 us
    pallas_call x1, Pallas kernels, solve_and_sample(): pl.pallas_call(functools.partial(sample_kernel, block_x, block_y, window)...  13.5 us
    all_to_all x2, starting transfers between devices, exchange(): lax.all_to_all(values, axes, split_axis=0, concat_axis=0, tiled=True, axi...  7.85 us
    all_to_all x2, waiting for transfers between devices, exchange(): lax.all_to_all(values, axes, split_axis=0, concat_axis=0, tiled=True, axi...  6.02 us
    pallas_call x1, Pallas kernels, energies(): pl.pallas_call(energy_kernel, grid=(1,), out_shape=result, in_specs=whole...  4.33 us
    pallas_call x1, Pallas kernels, finish(): pl.pallas_call(functools.partial(finish_kernel, block_y), grid=(groups,),...  3.56 us
  transfers between devices with their start and end apart: 4, of which 4 were waited for; matrix products, arithmetic and copies ran while one was open for 1% of the time, Pallas kernels for 18%

profile of v7, /device:TPU:0, one launch (start us, length us, event | category | flops | bytes accessed | tf_op | source)
XLA Modules:
  0.0 99.1 jit_solution(1327874150188575318)
XLA Ops:
  0.6 1.4 %collect_atoms.1 = (f32[8,256]{1,0:T(8,128)}, f32[8,256]{1,0:T(8,128)}) custom-call(f32[3,1,192]{2,1,0:T(1,128)} %positions_ref.1, s32[1,192]{1,0:T(1,128)} %types_ref.3, s32[1,192]{1,0:T(1,128)} %count_ref.1, s32[1,192]{1,0:T(1,128)} %send_ref.1), custom_call_target="tpu_custom_call" | custom-call | tf_op jit(solution)/shard_map/collect_atoms/pallas_call | solution.py:348
  2.0 3.3 %collective-permute-start.1 = (f32[8,256]{1,0:T(8,128)}, f32[8,256]{1,0:T(8,128)S(1)}, u32[]{:S(2)}, u32[]{:S(2)}) collective-permute-start(f32[8,256]{1,0:T(8,128)} %get-tuple-element.14), channel_id=1, source_target_pairs={{4,0},{8,4},{12,8},{16,12},{20,16},{24,20},{28,24},{0,28},{5,1},{9... | collective-permute-start | bytes 24584 | tf_op jit(solution)/shard_map/ppermute | solution.py:1227
  5.4 0.0 collective-permute-start
  5.4 1.6 %collective-permute-done.1.upper_ref = f32[8,256]{1,0:T(8,128)S(1)} collective-permute-done((f32[8,256]{1,0:T(8,128)}, f32[8,256]{1,0:T(8,128)S(1)}, u32[]{:S(2)}, u32[]{:S(2)}) %collective-permute-start.1) | collective-permute-done | bytes 8224 | tf_op jit(solution)/shard_map/ppermute | solution.py:1227
  7.0 0.0 copy-start.4
  7.0 2.6 %collective-permute-done.lower_ref = f32[8,256]{1,0:T(8,128)S(1)} collective-permute-done((f32[8,256]{1,0:T(8,128)}, f32[8,256]{1,0:T(8,128)S(1)}, u32[]{:S(2)}, u32[]{:S(2)}) %collective-permute-start) | collective-permute-done | bytes 8224 | tf_op jit(solution)/shard_map/ppermute | solution.py:1226
  9.6 0.0 copy-start.5
  9.6 0.0 copy-done.4
  9.6 0.6 copy-done.5
  10.2 13.9 %networks.1 = (f32[192,1600]{1,0:T(8,128)}, f32[1,192]{1,0:T(1,128)}, f32[32,8,192]{2,1,0:T(8,128)}) custom-call(s32[1]{0:T(128)} %bitcast.1.base_ref, f32[2]{0:T(128)} %charges_ref.1, f32[8,256]{1,0:T(8,128)} %get-tuple-element.13.own_ref, f32[8,256]{1,0:T(8,128)} %copy-done.5, f32[8,256]{1,0:T(8,128)} %copy-done.4, s32[64,192]{1,0:T(8,128)} %bitcast.20, ...), custom_call_target="tpu_custom_call" | custom-call | tf_op jit(solution)/shard_map/networks/pallas_call | solution.py:641
  24.0 4.0 %all-to-all-start = ((f32[32,8,192]{2,1,0:T(8,128)}), f32[32,8,192]{2,1,0:T(8,128)S(1)}, u32[]{:S(2)}, u32[]{:S(2)}) async-start(f32[32,8,192]{2,1,0:T(8,128)} %get-tuple-element.15), calls=%async_computation | async-start | bytes 524288 | tf_op jit(solution)/shard_map/all_to_all | solution.py:1219
  28.0 0.7 copy.27.waves_ref
  28.7 0.7 copy.26.kappa_ref
  29.4 4.3 %energies.1.short_hbm = f32[1,192]{1,0:T(1,128)} custom-call(f32[192,1600]{1,0:T(8,128)} %get-tuple-element.16.descriptor_ref, f32[240,1600]{1,0:T(8,128)} %bitcast.17, f32[2,240,240]{2,1,0:T(8,128)} %weight_hidden_ref.1, f32[1,240]{1,0:T(1,128)} %bitcast.22), custom_call_target="tpu_custom_call" | custom-call | flops 442368000 | bytes 1536000 | tf_op jit(solution)/shard_map/energies/pallas_call | solution.py:676
  33.8 4.8 %all-to-all-done.static_ref = f32[32,8,192]{2,1,0:T(8,128)S(1)} async-done(((f32[32,8,192]{2,1,0:T(8,128)}), f32[32,8,192]{2,1,0:T(8,128)S(1)}, u32[]{:S(2)}, u32[]{:S(2)}) %all-to-all-start) | async-done | bytes 196640 | tf_op jit(solution)/shard_map/all_to_all | solution.py:1219
  38.6 0.0 copy-start.3
  38.6 0.7 copy-done.3
  39.3 17.0 %spread_and_solve.1 = (f32[16,4,4,8,128]{4,3,2,1,0:T(8,128)}, f32[8,256,256]{2,1,0:T(8,128)}, f32[8,8,768]{2,1,0:T(8,128)}, f32[8,256,256]{2,1,0:T(8,128)}) custom-call(f32[16,2]{1,0:T(8,128)} %copy.26.kappa_ref, s32[1]{0:T(128)} %bitcast.pair_ref, f32[32,8,192]{2,1,0:T(8,128)} %copy-done.3, s32[16,2]{1,0:T(8,128)} %copy.27.waves_ref, ...), custom_call_target="tpu_custom_call" | custom-call | tf_op jit(solution)/shard_map/spread_and_solve/pallas_call | solution.py:938
  56.3 3.9 %all-to-all-start.1 = ((f32[16,128,128]{2,1,0:T(8,128)}), f32[16,128,128]{2,1,0:T(8,128)S(1)}, u32[]{:S(2)}, u32[]{:S(2)}) async-start(f32[16,128,128]{2,1,0:T(8,128)} %bitcast.19), calls=%async_computation.1 | async-start | bytes 2097152 | tf_op jit(solution)/shard_map/all_to_all | solution.py:1219
  60.2 13.5 %solve_and_sample.1 = f32[16,17,8,128]{3,2,1,0:T(8,128)} custom-call(f32[16,2]{1,0:T(8,128)} %copy.26.kappa_ref, s32[1]{0:T(128)} %bitcast.pair_ref, f32[8,8,768]{2,1,0:T(8,128)} %get-tuple-element.18.atoms_ref, s32[16,2]{1,0:T(8,128)} %copy.27.waves_ref, f32[1,128]{1,0:T(1,128)} %constant.64.clone.cosine_ref, f32[2,256,256]{2,1,0:T(8,128)} %constant.65.clone.tables_hbm, ...), custom_call_target="tpu_custom_call" | custom-call | flops 6442450944 | bytes 2097152 | tf_op jit(solution)/shard_map/solve_and_sample/pallas_call | solution.py:1073
  73.7 0.0 copy-start
  73.7 0.0 copy-start.1
  73.7 0.0 copy-start.2
  73.7 1.2 %all-to-all-done.1 = f32[16,128,128]{2,1,0:T(8,128)S(1)} async-done(((f32[16,128,128]{2,1,0:T(8,128)}), f32[16,128,128]{2,1,0:T(8,128)S(1)}, u32[]{:S(2)}, u32[]{:S(2)}) %all-to-all-start.1) | async-done | bytes 1048608 | tf_op jit(solution)/shard_map/all_to_all | solution.py:1219
  74.9 20.4 %all_to_all.15 = f32[16,136,128]{2,1,0:T(8,128)S(1)} all-to-all(f32[16,136,128]{2,1,0:T(8,128)} %bitcast.18), channel_id=1, replica_groups={{0,1,4,5,8,9,12,13,16,17,20,21,24,25,28,29},{2,3,6,7,10,11,14,15,18,19,..., dimensions={0} | all-to-all | bytes 2228224 | tf_op jit(solution)/shard_map/all_to_all | solution.py:1219
  95.3 0.0 copy-done
  95.3 0.0 copy-done.1
  95.3 0.0 copy-done.2
  95.3 3.6 %finish.1 = (f32[32,64,256]{2,1,0:T(8,128)}, f32[1,192]{1,0:T(1,128)}) custom-call(f32[16,4,4,8,128]{4,3,2,1,0:T(8,128)S(1)} %bitcast.15, f32[16,17,8,128]{3,2,1,0:T(8,128)S(1)} %bitcast.13, f32[16,17,8,128]{3,2,1,0:T(8,128)S(1)} %bitcast.14, f32[1,192]{1,0:T(1,128)S(1)} %copy-done.1, f32[1,192]{1,0:T(1,128)S(1)} %copy-done.2, f32[256,256]{1,0:T(8,128)S(1)} %copy-done), custom_call_target="tpu_custom_call" | custom-call | tf_op jit(solution)/shard_map/finish/pallas_call | solution.py:1145
  (4 shorter events, 0.0 us)
Async XLA Ops:
  2.0 4.9 %collective-permute-start.1 = (f32[8,256]{1,0:T(8,128)}, f32[8,256]{1,0:T(8,128)S(1)}, u32[]{:S(2)}, u32[]{:S(2)}) collective-permute-start(f32[8,256]{1,0:T(8,128)} %get-tuple-element.14), channel_id=1, source_target_pairs={{4,0},{8,4},{12,8},{16,12},{20,16},{24,20},{28,24},{0,28},{5,1},{9... | collective-permute-start | bytes 24584 | tf_op jit(solution)/shard_map/ppermute | solution.py:1227
  5.4 4.2 %collective-permute-start = (f32[8,256]{1,0:T(8,128)}, f32[8,256]{1,0:T(8,128)S(1)}, u32[]{:S(2)}, u32[]{:S(2)}) collective-permute-start(f32[8,256]{1,0:T(8,128)} %get-tuple-element.14), channel_id=1, source_target_pairs={{0,4},{4,8},{8,12},{12,16},{16,20},{20,24},{24,28},{28,0},{1,5},{5... | collective-permute-start | bytes 24584 | tf_op jit(solution)/shard_map/ppermute | solution.py:1226
  7.0 2.6 %copy-start.4 = (f32[8,256]{1,0:T(8,128)}, f32[8,256]{1,0:T(8,128)S(1)}, u32[]{:S(2)}) copy-start(f32[8,256]{1,0:T(8,128)S(1)} %collective-permute-done.1.upper_ref) | copy-start | bytes 24580
  9.6 0.6 copy-start.5
  24.0 14.6 %all-to-all-start = ((f32[32,8,192]{2,1,0:T(8,128)}), f32[32,8,192]{2,1,0:T(8,128)S(1)}, u32[]{:S(2)}, u32[]{:S(2)}) async-start(f32[32,8,192]{2,1,0:T(8,128)} %get-tuple-element.15), calls=%async_computation | async-start | bytes 524288 | tf_op jit(solution)/shard_map/all_to_all | solution.py:1219
  38.6 0.7 copy-start.3
  56.3 18.6 %all-to-all-start.1 = ((f32[16,128,128]{2,1,0:T(8,128)}), f32[16,128,128]{2,1,0:T(8,128)S(1)}, u32[]{:S(2)}, u32[]{:S(2)}) async-start(f32[16,128,128]{2,1,0:T(8,128)} %bitcast.19), calls=%async_computation.1 | async-start | bytes 2097152 | tf_op jit(solution)/shard_map/all_to_all | solution.py:1219
  73.7 21.6 %copy-start = (f32[256,256]{1,0:T(8,128)S(1)}, f32[256,256]{1,0:T(8,128)}, u32[]{:S(2)}) copy-start(f32[256,256]{1,0:T(8,128)} %constant.67.clone.table_ref) | copy-start | bytes 786436
  73.7 21.6 %copy-start.1 = (f32[1,192]{1,0:T(1,128)S(1)}, f32[1,192]{1,0:T(1,128)}, u32[]{:S(2)}) copy-start(f32[1,192]{1,0:T(1,128)} %energies.1.short_hbm) | copy-start | bytes 2308
  73.7 21.6 %copy-start.2 = (f32[1,192]{1,0:T(1,128)S(1)}, f32[1,192]{1,0:T(1,128)}, u32[]{:S(2)}) copy-start(f32[1,192]{1,0:T(1,128)} %get-tuple-element.21.charge_hbm) | copy-start | bytes 2308

commit v8 on v7

--- a/solution.py
+++ b/solution.py
@@ -356,6 +356,36 @@
     )(*arrays)
 
 
+def place_kernel(base_ref, cell_x_ref, cell_y_ref, cell_z_ref, fraction_ref, copies_ref):
+    atoms = cell_x_ref.shape[1]
+    fields = jnp.concatenate(
+        [
+            cell_x_ref[...].astype(jnp.float32),
+            (cell_y_ref[...] + base_ref[0]).astype(jnp.float32),
+            cell_z_ref[...].astype(jnp.float32),
+        ]
+        + [fraction_ref[axis] for axis in range(3)]
+        + [jnp.zeros((2, atoms), jnp.float32)],
+        axis=0,
+    )
+    for copy in range(copies_ref.shape[0]):
+        copies_ref[copy] = fields
+
+
+def place_rows(copies, base, cells, fraction):
+    arrays = (*cells, fraction)
+    result = jax.ShapeDtypeStruct((copies, 8, cells[0].shape[1]), jnp.float32)
+    return pl.pallas_call(
+        place_kernel,
+        grid=(1,),
+        out_shape=result,
+        in_specs=[pl.BlockSpec(memory_space=pltpu.SMEM)] + whole_specs(*arrays),
+        out_specs=whole(result.shape),
+        compiler_params=pltpu.CompilerParams(vmem_limit_bytes=VMEM_BYTES),
+        name="place_rows",
+    )(base, *arrays)
+
+
 def fitting_rows(descriptor_ref, weight_in_ref, weight_hidden_ref, weight_out_ref):
     hidden = jnp.tanh(product(descriptor_ref[...], weight_in_ref[...], LANES))
     for layer in range(weight_hidden_ref.shape[0]):
@@ -386,17 +416,12 @@
 
 def network_kernel(
     ghosts,
-    base_ref,
     charges_ref,
     own_ref,
     lower_ref,
     upper_ref,
     slots_ref,
     types_ref,
-    cell_x_ref,
-    cell_y_ref,
-    cell_z_ref,
-    fraction_ref,
     first_ref,
     second_ref,
     third_ref,
@@ -545,7 +570,7 @@
             one_group(pl.multiple_of(step * unroll * group + part * group, group))
         return carry
 
-    unroll = 4 if rows % (4 * group) == 0 else 1
+    unroll = rows // group
     lax.fori_loop(0, rows // (unroll * group), body, 0)
 
     chunks = (descriptor_ref.shape[1] + 127) // 128
@@ -565,7 +590,7 @@
             else:
                 descriptor_ref[band, 128 * chunk : 128 * chunk + last] = total[:, 0:last]
 
-    bands = 4 if atoms % 32 == 0 else 1
+    bands = 8 if atoms % 64 == 0 else 1
 
     def describe(step, carry):
         for part in range(bands):
@@ -582,18 +607,8 @@
     kind = types_ref[...].astype(jnp.float32)
     charge = (1.0 - kind) * charges_ref[0] + kind * charges_ref[1] + natural_order(shift)
     charge_ref[...] = charge
-    fields = jnp.concatenate(
-        [
-            cell_x_ref[...].astype(jnp.float32),
-            (cell_y_ref[...] + base_ref[0]).astype(jnp.float32),
-            cell_z_ref[...].astype(jnp.float32),
-        ]
-        + [fraction_ref[axis] for axis in range(3)]
-        + [charge, jnp.zeros((1, atoms), jnp.float32)],
-        axis=0,
-    )
     for copy in range(copies_ref.shape[0]):
-        copies_ref[copy] = fields
+        copies_ref[copy] = charge
     store.wait()
 
 
@@ -612,15 +627,12 @@
 def networks(
     copies,
     ghosts,
-    base,
     charge_base,
     own,
     lower,
     upper,
     neighbours,
     types,
-    cells,
-    fraction,
     embed,
     weight_in,
     weight_hidden,
@@ -631,18 +643,18 @@
     spots = jnp.asarray(spot_table(embed[2].shape[1], desc))
     anywhere = pl.BlockSpec(memory_space=pl.ANY)
     scalars = pl.BlockSpec(memory_space=pltpu.SMEM)
-    blocks = (own, lower, upper, neighbours[0].T, types, *cells, fraction, *embed, spots)
+    blocks = (own, lower, upper, neighbours[0].T, types, *embed, spots)
     weight_out = weight_out.reshape(1, -1)
     results = [
         jax.ShapeDtypeStruct((atoms, desc), jnp.float32),
         jax.ShapeDtypeStruct((1, atoms), jnp.float32),
-        jax.ShapeDtypeStruct((copies, 8, atoms), jnp.float32),
+        jax.ShapeDtypeStruct((copies, 1, atoms), jnp.float32),
     ]
     return pl.pallas_call(
         functools.partial(network_kernel, ghosts),
         grid=(1,),
         out_shape=results,
-        in_specs=[scalars, scalars]
+        in_specs=[scalars]
         + whole_specs(*blocks)
         + [anywhere, anywhere]
         + whole_specs(weight_out),
@@ -659,7 +671,7 @@
         ],
         compiler_params=pltpu.CompilerParams(vmem_limit_bytes=VMEM_BYTES),
         name="networks",
-    )(base, charge_base, *blocks, weight_in.T, weight_hidden, weight_out)
+    )(charge_base, *blocks, weight_in.T, weight_hidden, weight_out)
 
 
 def energy_kernel(descriptor_ref, weight_in_ref, weight_hidden_ref, weight_out_ref, energy_ref):
@@ -837,6 +849,7 @@
     kappa_ref,
     pair_ref,
     static_ref,
+    charge_ref,
     waves_ref,
     cosine_ref,
     tables_hbm,
@@ -876,6 +889,7 @@
             lanes = slice(block * slab, block * (slab + 1))
             for brick in range(bricks):
                 atoms_ref[brick, :, lanes] = static_ref[slab * bricks + brick]
+                atoms_ref[brick, 6:7, lanes] = charge_ref[slab * bricks + brick]
         grid_ref[...] = jnp.zeros_like(grid_ref)
         for ref in second_refs:
             ref[...] = jnp.zeros_like(ref)
@@ -924,7 +938,7 @@
 
 
 def spread_and_solve(
-    block_x, block_y, window, kappa, pair, static, waves, cosine_row, tables, last, short
+    block_x, block_y, window, kappa, pair, static, charge, waves, cosine_row, tables, last, short
 ):
     devices, _, atoms = static.shape
     slabs = NG // block_y
@@ -945,7 +959,7 @@
             jax.ShapeDtypeStruct((parts - 2 * pairs, NG, NG), jnp.float32),
         ],
         in_specs=[scalars, scalars]
-        + whole_specs(static, waves, cosine_row)
+        + whole_specs(static, charge, waves, cosine_row)
         + [anywhere, anywhere, anywhere],
         out_specs=[
             pl.BlockSpec(sent_block, lambda step: (0, 0, step, 0, 0)),
@@ -963,7 +977,7 @@
         + [pltpu.VMEM((parts * window, slabs * atoms), jnp.bfloat16)] * 4,
         compiler_params=pltpu.CompilerParams(vmem_limit_bytes=VMEM_BYTES),
         name="spread_and_solve",
-    )(kappa, pair, static, waves, cosine_row, tables, last, short)
+    )(kappa, pair, static, charge, waves, cosine_row, tables, last, short)
 
 
 def sample_kernel(
@@ -1225,24 +1239,29 @@
     down = [((i + 1) % count_x, i) for i in range(count_x)]
     lower = lax.ppermute(outgoing, "brick", up)
     upper = lax.ppermute(outgoing, "brick", down)
-    descriptor, charge, fields = networks(
+    places = place_rows(
+        count_x * count_y,
+        (slab * block_y).astype(jnp.int32).reshape(1),
+        (cell_x, cell_y, cell_z),
+        spline_fraction,
+    )
+    every_place = exchange(places, ("slab", "brick"))
+    descriptor, charge, charge_copies = networks(
         count_x * count_y,
         ghosts,
-        (slab * block_y).astype(jnp.int32).reshape(1),
         charge_base,
         own,
         lower,
         upper,
         neighbours,
         types,
-        (cell_x, cell_y, cell_z),
-        spline_fraction,
         (embed_first, embed_second, embed_third),
         wannier_in,
         wannier_hidden,
         wannier_out,
     )
-    every_field = exchange(fields, ("slab", "brick"))
+    charge_copies, every_place = lax.optimization_barrier((charge_copies, every_place))
+    every_charge = exchange(charge_copies, ("slab", "brick"))
 
     part = (2 * brick + slab % 2) * parts + jnp.arange(parts, dtype=jnp.int32)
     wave = wave_of(part)
@@ -1275,7 +1294,8 @@
         window,
         kappa,
         pair,
-        every_field,
+        every_place,
+        every_charge,
         waves,
         cosine_row,
         tables,

time: 99.5 us -> 102 us (1.025)
  starting transfers between devices: 11.2 us -> 17.3 us
  waiting for transfers between devices: 10.2 us -> 6.83 us
    all_to_all x2 -> x3, starting transfers between devices: 7.85 us -> 14.9 us  [exchange(): lax.all_to_all(values, axes, split_axis=0, concat_axis=0, tiled=True, axi...]
    all_to_all x2 -> x3, waiting for transfers between devices: 6.02 us -> 2.7 us  [exchange(): lax.all_to_all(values, axes, split_axis=0, concat_axis=0, tiled=True, axi...]
    pallas_call x1, Pallas kernels: 13.9 us -> 12.4 us  [networks(): pl.pallas_call(functools.partial(network_kernel, ghosts), grid=(1,), out_...]
    pallas_call x0 -> x1, Pallas kernels: none -> 1.46 us  [place_rows(): pl.pallas_call(place_kernel, grid=(1,), out_shape=result, in_specs=[pl.Bl...]
  transfers between devices with their start and end apart: 4 -> 5, of which waited for: 4 -> 4; matrix products, arithmetic and copies ran while one was open for 1% -> 1% of each run, Pallas kernels for 18% -> 31%
where the time goes in v8:
time: 102 us
  Pallas kernels  53.5 us (52%)
  blocking collectives  20.4 us (20%)
  starting transfers between devices  17.3 us (17%)
  waiting for transfers between devices  6.83 us (7%)
  local copies, waits for them, and re-layouts  2.55 us (2%)
    all_to_all x1, blocking collectives, exchange(): lax.all_to_all(values, axes, split_axis=0, concat_axis=0, tiled=True, axi...  20.4 us
    pallas_call x1, Pallas kernels, spread_and_solve(): pl.pallas_call(functools.partial(spread_kernel, block_x, block_y, window)...  16.8 us
    all_to_all x3, starting transfers between devices, exchange(): lax.all_to_all(values, axes, split_axis=0, concat_axis=0, tiled=True, axi...  14.9 us
    pallas_call x1, Pallas kernels, solve_and_sample(): pl.pallas_call(functools.partial(sample_kernel, block_x, block_y, window)...  13.5 us
    pallas_call x1, Pallas kernels, networks(): pl.pallas_call(functools.partial(network_kernel, ghosts), grid=(1,), out_...  12.4 us
    pallas_call x1, Pallas kernels, energies(): pl.pallas_call(energy_kernel, grid=(1,), out_shape=result, in_specs=whole...  4.34 us
    pallas_call x1, Pallas kernels, finish(): pl.pallas_call(functools.partial(finish_kernel, block_y), grid=(groups,),...  3.56 us
    all_to_all x3, waiting for transfers between devices, exchange(): lax.all_to_all(values, axes, split_axis=0, concat_axis=0, tiled=True, axi...  2.7 us
  transfers between devices with their start and end apart: 5, of which 4 were waited for; matrix products, arithmetic and copies ran while one was open for 1% of the time, Pallas kernels for 31%

profile of v8, /device:TPU:0, one launch (start us, length us, event | category | flops | bytes accessed | tf_op | source)
XLA Modules:
  0.0 101.6 jit_solution(2365992691154046495)
XLA Ops:
  0.6 1.5 %place_rows.1 = f32[32,8,192]{2,1,0:T(8,128)} custom-call(s32[1]{0:T(128)} %bitcast.5.base_ref, s32[1,192]{1,0:T(1,128)} %cell_x_ref.1, s32[1,192]{1,0:T(1,128)} %cell_y_ref.1, s32[1,192]{1,0:T(1,128)} %cell_z_ref.1, f32[3,1,192]{2,1,0:T(1,128)} %fraction_ref.1), custom_call_target="tpu_custom_call" | custom-call | tf_op jit(solution)/shard_map/place_rows/pallas_call | solution.py:378
  2.1 7.3 %all-to-all-start = ((f32[32,8,192]{2,1,0:T(8,128)}), f32[32,8,192]{2,1,0:T(8,128)S(1)}, u32[]{:S(2)}, u32[]{:S(2)}) async-start(f32[32,8,192]{2,1,0:T(8,128)} %place_rows.1), calls=%async_computation | async-start | bytes 524288 | tf_op jit(solution)/shard_map/all_to_all | solution.py:1233
  9.4 1.4 %collect_atoms.1 = (f32[8,256]{1,0:T(8,128)}, f32[8,256]{1,0:T(8,128)}) custom-call(f32[3,1,192]{2,1,0:T(1,128)} %positions_ref.1, s32[1,192]{1,0:T(1,128)} %types_ref.3, s32[1,192]{1,0:T(1,128)} %count_ref.1, s32[1,192]{1,0:T(1,128)} %send_ref.1), custom_call_target="tpu_custom_call" | custom-call | tf_op jit(solution)/shard_map/collect_atoms/pallas_call | solution.py:348
  10.8 2.4 %collective-permute-start.1 = (f32[8,256]{1,0:T(8,128)}, f32[8,256]{1,0:T(8,128)S(1)}, u32[]{:S(2)}, u32[]{:S(2)}) collective-permute-start(f32[8,256]{1,0:T(8,128)} %get-tuple-element.16), channel_id=1, source_target_pairs={{4,0},{8,4},{12,8},{16,12},{20,16},{24,20},{28,24},{0,28},{5,1},{9... | collective-permute-start | bytes 24584 | tf_op jit(solution)/shard_map/ppermute | solution.py:1241
  13.2 0.0 collective-permute-start
  13.3 1.5 %collective-permute-done.1.upper_ref = f32[8,256]{1,0:T(8,128)S(1)} collective-permute-done((f32[8,256]{1,0:T(8,128)}, f32[8,256]{1,0:T(8,128)S(1)}, u32[]{:S(2)}, u32[]{:S(2)}) %collective-permute-start.1) | collective-permute-done | bytes 8224 | tf_op jit(solution)/shard_map/ppermute | solution.py:1241
  14.8 0.0 copy-start.5
  14.8 2.6 %collective-permute-done.lower_ref = f32[8,256]{1,0:T(8,128)S(1)} collective-permute-done((f32[8,256]{1,0:T(8,128)}, f32[8,256]{1,0:T(8,128)S(1)}, u32[]{:S(2)}, u32[]{:S(2)}) %collective-permute-start) | collective-permute-done | bytes 8224 | tf_op jit(solution)/shard_map/ppermute | solution.py:1240
  17.4 0.0 copy-start.6
  17.4 0.0 copy-done.5
  17.4 0.6 copy-done.6
  18.0 12.4 %networks.1 = (f32[192,1600]{1,0:T(8,128)}, f32[1,192]{1,0:T(1,128)}, f32[32,1,192]{2,1,0:T(1,128)}) custom-call(f32[2]{0:T(128)} %charges_ref.1, f32[8,256]{1,0:T(8,128)} %get-tuple-element.15.own_ref, f32[8,256]{1,0:T(8,128)} %copy-done.6, f32[8,256]{1,0:T(8,128)} %copy-done.5, s32[64,192]{1,0:T(8,128)} %bitcast.20, s32[1,192]{1,0:T(1,128)} %types_ref.3, ...), custom_call_target="tpu_custom_call" | custom-call | tf_op jit(solution)/shard_map/networks/pallas_call | solution.py:653
  30.4 0.0 all-to-all-done.static_ref
  30.4 0.0 copy-start.3
  30.4 3.7 %all-to-all-start.1 = ((f32[32,1,192]{2,1,0:T(1,128)}), f32[32,1,192]{2,1,0:T(1,128)S(1)}, u32[]{:S(2)}, u32[]{:S(2)}) async-start(f32[32,1,192]{2,1,0:T(1,128)} %get-tuple-element.19), calls=%async_computation.1 | async-start | bytes 65536 | tf_op jit(solution)/shard_map/all_to_all | solution.py:1233
  34.2 0.7 copy.27.waves_ref
  34.9 0.7 copy.26.kappa_ref
  35.5 4.3 %energies.1.short_hbm = f32[1,192]{1,0:T(1,128)} custom-call(f32[192,1600]{1,0:T(8,128)} %get-tuple-element.20.descriptor_ref, f32[240,1600]{1,0:T(8,128)} %bitcast.17, f32[2,240,240]{2,1,0:T(8,128)} %weight_hidden_ref.1, f32[1,240]{1,0:T(1,128)} %bitcast.22), custom_call_target="tpu_custom_call" | custom-call | flops 442368000 | bytes 1536000 | tf_op jit(solution)/shard_map/energies/pallas_call | solution.py:688
  39.9 0.0 copy-done.3
  39.9 1.5 %all-to-all-done.1.charge_ref = f32[32,1,192]{2,1,0:T(1,128)S(1)} async-done(((f32[32,1,192]{2,1,0:T(1,128)}), f32[32,1,192]{2,1,0:T(1,128)S(1)}, u32[]{:S(2)}, u32[]{:S(2)}) %all-to-all-start.1) | async-done | bytes 24608 | tf_op jit(solution)/shard_map/all_to_all | solution.py:1233
  41.4 0.0 copy-start.4
  41.4 0.6 copy-done.4
  42.0 16.8 %spread_and_solve.1 = (f32[16,4,4,8,128]{4,3,2,1,0:T(8,128)}, f32[8,256,256]{2,1,0:T(8,128)}, f32[8,8,768]{2,1,0:T(8,128)}, f32[8,256,256]{2,1,0:T(8,128)}) custom-call(f32[16,2]{1,0:T(8,128)} %copy.26.kappa_ref, s32[1]{0:T(128)} %bitcast.pair_ref, f32[32,8,192]{2,1,0:T(8,128)} %copy-done.3, f32[32,1,192]{2,1,0:T(1,128)} %copy-done.4, ...), custom_call_target="tpu_custom_call" | custom-call | tf_op jit(solution)/shard_map/spread_and_solve/pallas_call | solution.py:952
  58.9 3.9 %all-to-all-start.2 = ((f32[16,128,128]{2,1,0:T(8,128)}), f32[16,128,128]{2,1,0:T(8,128)S(1)}, u32[]{:S(2)}, u32[]{:S(2)}) async-start(f32[16,128,128]{2,1,0:T(8,128)} %bitcast.19), calls=%async_computation.2 | async-start | bytes 2097152 | tf_op jit(solution)/shard_map/all_to_all | solution.py:1233
  62.8 13.5 %solve_and_sample.1 = f32[16,17,8,128]{3,2,1,0:T(8,128)} custom-call(f32[16,2]{1,0:T(8,128)} %copy.26.kappa_ref, s32[1]{0:T(128)} %bitcast.pair_ref, f32[8,8,768]{2,1,0:T(8,128)} %get-tuple-element.22.atoms_ref, s32[16,2]{1,0:T(8,128)} %copy.27.waves_ref, f32[1,128]{1,0:T(1,128)} %constant.64.clone.cosine_ref, f32[2,256,256]{2,1,0:T(8,128)} %constant.65.clone.tables_hbm, ...), custom_call_target="tpu_custom_call" | custom-call | flops 6442450944 | bytes 2097152 | tf_op jit(solution)/shard_map/solve_and_sample/pallas_call | solution.py:1087
  76.3 0.0 copy-start
  76.3 0.0 copy-start.1
  76.3 0.0 copy-start.2
  76.3 1.2 %all-to-all-done.2 = f32[16,128,128]{2,1,0:T(8,128)S(1)} async-done(((f32[16,128,128]{2,1,0:T(8,128)}), f32[16,128,128]{2,1,0:T(8,128)S(1)}, u32[]{:S(2)}, u32[]{:S(2)}) %all-to-all-start.2) | async-done | bytes 1048608 | tf_op jit(solution)/shard_map/all_to_all | solution.py:1233
  77.5 20.4 %all_to_all.20 = f32[16,136,128]{2,1,0:T(8,128)S(1)} all-to-all(f32[16,136,128]{2,1,0:T(8,128)} %bitcast.18), channel_id=1, replica_groups={{0,1,4,5,8,9,12,13,16,17,20,21,24,25,28,29},{2,3,6,7,10,11,14,15,18,19,..., dimensions={0} | all-to-all | bytes 2228224 | tf_op jit(solution)/shard_map/all_to_all | solution.py:1233
  97.8 0.0 copy-done
  97.8 0.0 copy-done.1
  97.8 0.0 copy-done.2
  97.9 3.6 %finish.1 = (f32[32,64,256]{2,1,0:T(8,128)}, f32[1,192]{1,0:T(1,128)}) custom-call(f32[16,4,4,8,128]{4,3,2,1,0:T(8,128)S(1)} %bitcast.15, f32[16,17,8,128]{3,2,1,0:T(8,128)S(1)} %bitcast.13, f32[16,17,8,128]{3,2,1,0:T(8,128)S(1)} %bitcast.14, f32[1,192]{1,0:T(1,128)S(1)} %copy-done.1, f32[1,192]{1,0:T(1,128)S(1)} %copy-done.2, f32[256,256]{1,0:T(8,128)S(1)} %copy-done), custom_call_target="tpu_custom_call" | custom-call | tf_op jit(solution)/shard_map/finish/pallas_call | solution.py:1159
  (4 shorter events, 0.0 us)
Async XLA Ops:
  2.1 28.3 %all-to-all-start = ((f32[32,8,192]{2,1,0:T(8,128)}), f32[32,8,192]{2,1,0:T(8,128)S(1)}, u32[]{:S(2)}, u32[]{:S(2)}) async-start(f32[32,8,192]{2,1,0:T(8,128)} %place_rows.1), calls=%async_computation | async-start | bytes 524288 | tf_op jit(solution)/shard_map/all_to_all | solution.py:1233
  10.8 4.0 %collective-permute-start.1 = (f32[8,256]{1,0:T(8,128)}, f32[8,256]{1,0:T(8,128)S(1)}, u32[]{:S(2)}, u32[]{:S(2)}) collective-permute-start(f32[8,256]{1,0:T(8,128)} %get-tuple-element.16), channel_id=1, source_target_pairs={{4,0},{8,4},{12,8},{16,12},{20,16},{24,20},{28,24},{0,28},{5,1},{9... | collective-permute-start | bytes 24584 | tf_op jit(solution)/shard_map/ppermute | solution.py:1241
  13.2 4.2 %collective-permute-start = (f32[8,256]{1,0:T(8,128)}, f32[8,256]{1,0:T(8,128)S(1)}, u32[]{:S(2)}, u32[]{:S(2)}) collective-permute-start(f32[8,256]{1,0:T(8,128)} %get-tuple-element.16), channel_id=1, source_target_pairs={{0,4},{4,8},{8,12},{12,16},{16,20},{20,24},{24,28},{28,0},{1,5},{5... | collective-permute-start | bytes 24584 | tf_op jit(solution)/shard_map/ppermute | solution.py:1240
  14.8 2.6 %copy-start.5 = (f32[8,256]{1,0:T(8,128)}, f32[8,256]{1,0:T(8,128)S(1)}, u32[]{:S(2)}) copy-start(f32[8,256]{1,0:T(8,128)S(1)} %collective-permute-done.1.upper_ref) | copy-start | bytes 24580
  17.4 0.6 copy-start.6
  30.4 9.5 %copy-start.3 = (f32[32,8,192]{2,1,0:T(8,128)}, f32[32,8,192]{2,1,0:T(8,128)S(1)}, u32[]{:S(2)}) copy-start(f32[32,8,192]{2,1,0:T(8,128)S(1)} %all-to-all-done.static_ref) | copy-start | bytes 589828
  30.4 11.0 %all-to-all-start.1 = ((f32[32,1,192]{2,1,0:T(1,128)}), f32[32,1,192]{2,1,0:T(1,128)S(1)}, u32[]{:S(2)}, u32[]{:S(2)}) async-start(f32[32,1,192]{2,1,0:T(1,128)} %get-tuple-element.19), calls=%async_computation.1 | async-start | bytes 65536 | tf_op jit(solution)/shard_map/all_to_all | solution.py:1233
  41.4 0.6 copy-start.4
  58.9 18.6 %all-to-all-start.2 = ((f32[16,128,128]{2,1,0:T(8,128)}), f32[16,128,128]{2,1,0:T(8,128)S(1)}, u32[]{:S(2)}, u32[]{:S(2)}) async-start(f32[16,128,128]{2,1,0:T(8,128)} %bitcast.19), calls=%async_computation.2 | async-start | bytes 2097152 | tf_op jit(solution)/shard_map/all_to_all | solution.py:1233
  76.3 21.6 %copy-start = (f32[256,256]{1,0:T(8,128)S(1)}, f32[256,256]{1,0:T(8,128)}, u32[]{:S(2)}) copy-start(f32[256,256]{1,0:T(8,128)} %constant.67.clone.table_ref) | copy-start | bytes 786436
  76.3 21.6 %copy-start.1 = (f32[1,192]{1,0:T(1,128)S(1)}, f32[1,192]{1,0:T(1,128)}, u32[]{:S(2)}) copy-start(f32[1,192]{1,0:T(1,128)} %energies.1.short_hbm) | copy-start | bytes 2308
  76.3 21.6 %copy-start.2 = (f32[1,192]{1,0:T(1,128)S(1)}, f32[1,192]{1,0:T(1,128)}, u32[]{:S(2)}) copy-start(f32[1,192]{1,0:T(1,128)} %get-tuple-element.25.charge_hbm) | copy-start | bytes 2308

commit v9 on v8

--- a/solution.py
+++ b/solution.py
@@ -1245,6 +1245,7 @@
         (cell_x, cell_y, cell_z),
         spline_fraction,
     )
+    places, upper = lax.optimization_barrier((places, upper))
     every_place = exchange(places, ("slab", "brick"))
     descriptor, charge, charge_copies = networks(
         count_x * count_y,

time: 102 us -> 103 us (level)
  starting transfers between devices: 17.3 us -> 18.6 us
    ppermute x1, waiting for transfers between devices: 1.53 us -> 0.12 us  [per_device(): upper = lax.ppermute(outgoing, 'brick', down)]
    ppermute x1, waiting for transfers between devices: 2.61 us -> 3.94 us  [per_device(): lower = lax.ppermute(outgoing, 'brick', up)]
where the time goes in v9:
time: 103 us
  Pallas kernels  53.5 us (52%)
  blocking collectives  20.4 us (20%)
  starting transfers between devices  18.6 us (18%)
  waiting for transfers between devices  6.76 us (7%)
  local copies, waits for them, and re-layouts  2.55 us (2%)
    all_to_all x1, blocking collectives, exchange(): lax.all_to_all(values, axes, split_axis=0, concat_axis=0, tiled=True, axi...  20.4 us
    pallas_call x1, Pallas kernels, spread_and_solve(): pl.pallas_call(functools.partial(spread_kernel, block_x, block_y, window)...  16.8 us
    all_to_all x3, starting transfers between devices, exchange(): lax.all_to_all(values, axes, split_axis=0, concat_axis=0, tiled=True, axi...  15 us
    pallas_call x1, Pallas kernels, solve_and_sample(): pl.pallas_call(functools.partial(sample_kernel, block_x, block_y, window)...  13.5 us
    pallas_call x1, Pallas kernels, networks(): pl.pallas_call(functools.partial(network_kernel, ghosts), grid=(1,), out_...  12.4 us
    pallas_call x1, Pallas kernels, energies(): pl.pallas_call(energy_kernel, grid=(1,), out_shape=result, in_specs=whole...  4.34 us
    ppermute x1, waiting for transfers between devices, per_device(): lower = lax.ppermute(outgoing, 'brick', up)  3.94 us
    pallas_call x1, Pallas kernels, finish(): pl.pallas_call(functools.partial(finish_kernel, block_y), grid=(groups,),...  3.56 us
  transfers between devices with their start and end apart: 5, of which 4 were waited for; matrix products, arithmetic and copies ran while one was open for 1% of the time, Pallas kernels for 31%

profile of v9, /device:TPU:0, one launch (start us, length us, event | category | flops | bytes accessed | tf_op | source)
XLA Modules:
  0.0 102.8 jit_solution(13744500536552617197)
XLA Ops:
  0.6 1.4 %collect_atoms.1 = (f32[8,256]{1,0:T(8,128)}, f32[8,256]{1,0:T(8,128)}) custom-call(f32[3,1,192]{2,1,0:T(1,128)} %positions_ref.1, s32[1,192]{1,0:T(1,128)} %types_ref.3, s32[1,192]{1,0:T(1,128)} %count_ref.1, s32[1,192]{1,0:T(1,128)} %send_ref.1), custom_call_target="tpu_custom_call" | custom-call | tf_op jit(solution)/shard_map/collect_atoms/pallas_call | solution.py:348
  2.0 3.3 %collective-permute-start.1 = (f32[8,256]{1,0:T(8,128)}, f32[8,256]{1,0:T(8,128)S(1)}, u32[]{:S(2)}, u32[]{:S(2)}) collective-permute-start(f32[8,256]{1,0:T(8,128)} %get-tuple-element.18), channel_id=1, source_target_pairs={{4,0},{8,4},{12,8},{16,12},{20,16},{24,20},{28,24},{0,28},{5,1},{9... | collective-permute-start | bytes 24584 | tf_op jit(solution)/shard_map/ppermute | solution.py:1241
  5.4 1.5 %place_rows.1 = f32[32,8,192]{2,1,0:T(8,128)} custom-call(s32[1]{0:T(128)} %bitcast.1.base_ref, s32[1,192]{1,0:T(1,128)} %cell_x_ref.1, s32[1,192]{1,0:T(1,128)} %cell_y_ref.1, s32[1,192]{1,0:T(1,128)} %cell_z_ref.1, f32[3,1,192]{2,1,0:T(1,128)} %fraction_ref.1), custom_call_target="tpu_custom_call" | custom-call | tf_op jit(solution)/shard_map/place_rows/pallas_call | solution.py:378
  6.8 0.1 collective-permute-done.1.upper_ref
  7.0 0.0 copy-start.5
  7.0 6.0 %all-to-all-start = ((f32[32,8,192]{2,1,0:T(8,128)}), f32[32,8,192]{2,1,0:T(8,128)S(1)}, u32[]{:S(2)}, u32[]{:S(2)}) async-start(f32[32,8,192]{2,1,0:T(8,128)} %place_rows.1), calls=%async_computation | async-start | bytes 524288 | tf_op jit(solution)/shard_map/all_to_all | solution.py:1233
  13.0 0.3 collective-permute-start
  13.3 3.9 %collective-permute-done.lower_ref = f32[8,256]{1,0:T(8,128)S(1)} collective-permute-done((f32[8,256]{1,0:T(8,128)}, f32[8,256]{1,0:T(8,128)S(1)}, u32[]{:S(2)}, u32[]{:S(2)}) %collective-permute-start) | collective-permute-done | bytes 8224 | tf_op jit(solution)/shard_map/ppermute | solution.py:1240
  17.3 0.0 copy-start.6
  17.3 0.0 copy-done.5
  17.3 0.6 copy-done.6
  17.8 12.4 %networks.1 = (f32[192,1600]{1,0:T(8,128)}, f32[1,192]{1,0:T(1,128)}, f32[32,1,192]{2,1,0:T(1,128)}) custom-call(f32[2]{0:T(128)} %charges_ref.1, f32[8,256]{1,0:T(8,128)} %get-tuple-element.17.own_ref, f32[8,256]{1,0:T(8,128)} %copy-done.6, f32[8,256]{1,0:T(8,128)} %copy-done.5, s32[64,192]{1,0:T(8,128)} %bitcast.20, s32[1,192]{1,0:T(1,128)} %types_ref.3, ...), custom_call_target="tpu_custom_call" | custom-call | tf_op jit(solution)/shard_map/networks/pallas_call | solution.py:653
  30.2 0.0 all-to-all-done.static_ref
  30.2 0.0 copy-start.3
  30.3 5.1 %all-to-all-start.1 = ((f32[32,1,192]{2,1,0:T(1,128)}), f32[32,1,192]{2,1,0:T(1,128)S(1)}, u32[]{:S(2)}, u32[]{:S(2)}) async-start(f32[32,1,192]{2,1,0:T(1,128)} %get-tuple-element.23), calls=%async_computation.1 | async-start | bytes 65536 | tf_op jit(solution)/shard_map/all_to_all | solution.py:1233
  35.4 0.7 copy.27.waves_ref
  36.0 0.7 copy.26.kappa_ref
  36.7 4.3 %energies.1.short_hbm = f32[1,192]{1,0:T(1,128)} custom-call(f32[192,1600]{1,0:T(8,128)} %get-tuple-element.24.descriptor_ref, f32[240,1600]{1,0:T(8,128)} %bitcast.17, f32[2,240,240]{2,1,0:T(8,128)} %weight_hidden_ref.1, f32[1,240]{1,0:T(1,128)} %bitcast.22), custom_call_target="tpu_custom_call" | custom-call | flops 442368000 | bytes 1536000 | tf_op jit(solution)/shard_map/energies/pallas_call | solution.py:688
  41.1 0.0 copy-done.3
  41.1 1.5 %all-to-all-done.1.charge_ref = f32[32,1,192]{2,1,0:T(1,128)S(1)} async-done(((f32[32,1,192]{2,1,0:T(1,128)}), f32[32,1,192]{2,1,0:T(1,128)S(1)}, u32[]{:S(2)}, u32[]{:S(2)}) %all-to-all-start.1) | async-done | bytes 24608 | tf_op jit(solution)/shard_map/all_to_all | solution.py:1233
  42.6 0.0 copy-start.4
  42.6 0.6 copy-done.4
  43.2 16.8 %spread_and_solve.1 = (f32[16,4,4,8,128]{4,3,2,1,0:T(8,128)}, f32[8,256,256]{2,1,0:T(8,128)}, f32[8,8,768]{2,1,0:T(8,128)}, f32[8,256,256]{2,1,0:T(8,128)}) custom-call(f32[16,2]{1,0:T(8,128)} %copy.26.kappa_ref, s32[1]{0:T(128)} %bitcast.pair_ref, f32[32,8,192]{2,1,0:T(8,128)} %copy-done.3, f32[32,1,192]{2,1,0:T(1,128)} %copy-done.4, ...), custom_call_target="tpu_custom_call" | custom-call | tf_op jit(solution)/shard_map/spread_and_solve/pallas_call | solution.py:952
  60.1 3.9 %all-to-all-start.2 = ((f32[16,128,128]{2,1,0:T(8,128)}), f32[16,128,128]{2,1,0:T(8,128)S(1)}, u32[]{:S(2)}, u32[]{:S(2)}) async-start(f32[16,128,128]{2,1,0:T(8,128)} %bitcast.19), calls=%async_computation.2 | async-start | bytes 2097152 | tf_op jit(solution)/shard_map/all_to_all | solution.py:1233
  63.9 13.5 %solve_and_sample.1 = f32[16,17,8,128]{3,2,1,0:T(8,128)} custom-call(f32[16,2]{1,0:T(8,128)} %copy.26.kappa_ref, s32[1]{0:T(128)} %bitcast.pair_ref, f32[8,8,768]{2,1,0:T(8,128)} %get-tuple-element.26.atoms_ref, s32[16,2]{1,0:T(8,128)} %copy.27.waves_ref, f32[1,128]{1,0:T(1,128)} %constant.64.clone.cosine_ref, f32[2,256,256]{2,1,0:T(8,128)} %constant.65.clone.tables_hbm, ...), custom_call_target="tpu_custom_call" | custom-call | flops 6442450944 | bytes 2097152 | tf_op jit(solution)/shard_map/solve_and_sample/pallas_call | solution.py:1087
  77.4 0.0 copy-start
  77.5 0.0 copy-start.1
  77.5 0.0 copy-start.2
  77.5 1.2 %all-to-all-done.2 = f32[16,128,128]{2,1,0:T(8,128)S(1)} async-done(((f32[16,128,128]{2,1,0:T(8,128)}), f32[16,128,128]{2,1,0:T(8,128)S(1)}, u32[]{:S(2)}, u32[]{:S(2)}) %all-to-all-start.2) | async-done | bytes 1048608 | tf_op jit(solution)/shard_map/all_to_all | solution.py:1233
  78.6 20.4 %all_to_all.20 = f32[16,136,128]{2,1,0:T(8,128)S(1)} all-to-all(f32[16,136,128]{2,1,0:T(8,128)} %bitcast.18), channel_id=1, replica_groups={{0,1,4,5,8,9,12,13,16,17,20,21,24,25,28,29},{2,3,6,7,10,11,14,15,18,19,..., dimensions={0} | all-to-all | bytes 2228224 | tf_op jit(solution)/shard_map/all_to_all | solution.py:1233
  99.0 0.0 copy-done
  99.0 0.0 copy-done.1
  99.0 0.0 copy-done.2
  99.0 3.6 %finish.1 = (f32[32,64,256]{2,1,0:T(8,128)}, f32[1,192]{1,0:T(1,128)}) custom-call(f32[16,4,4,8,128]{4,3,2,1,0:T(8,128)S(1)} %bitcast.15, f32[16,17,8,128]{3,2,1,0:T(8,128)S(1)} %bitcast.13, f32[16,17,8,128]{3,2,1,0:T(8,128)S(1)} %bitcast.14, f32[1,192]{1,0:T(1,128)S(1)} %copy-done.1, f32[1,192]{1,0:T(1,128)S(1)} %copy-done.2, f32[256,256]{1,0:T(8,128)S(1)} %copy-done), custom_call_target="tpu_custom_call" | custom-call | tf_op jit(solution)/shard_map/finish/pallas_call | solution.py:1159
  (4 shorter events, 0.0 us)
Async XLA Ops:
  2.0 4.9 %collective-permute-start.1 = (f32[8,256]{1,0:T(8,128)}, f32[8,256]{1,0:T(8,128)S(1)}, u32[]{:S(2)}, u32[]{:S(2)}) collective-permute-start(f32[8,256]{1,0:T(8,128)} %get-tuple-element.18), channel_id=1, source_target_pairs={{4,0},{8,4},{12,8},{16,12},{20,16},{24,20},{28,24},{0,28},{5,1},{9... | collective-permute-start | bytes 24584 | tf_op jit(solution)/shard_map/ppermute | solution.py:1241
  7.0 10.3 %copy-start.5 = (f32[8,256]{1,0:T(8,128)}, f32[8,256]{1,0:T(8,128)S(1)}, u32[]{:S(2)}) copy-start(f32[8,256]{1,0:T(8,128)S(1)} %collective-permute-done.1.upper_ref) | copy-start | bytes 24580
  7.0 23.3 %all-to-all-start = ((f32[32,8,192]{2,1,0:T(8,128)}), f32[32,8,192]{2,1,0:T(8,128)S(1)}, u32[]{:S(2)}, u32[]{:S(2)}) async-start(f32[32,8,192]{2,1,0:T(8,128)} %place_rows.1), calls=%async_computation | async-start | bytes 524288 | tf_op jit(solution)/shard_map/all_to_all | solution.py:1233
  13.0 4.3 %collective-permute-start = (f32[8,256]{1,0:T(8,128)}, f32[8,256]{1,0:T(8,128)S(1)}, u32[]{:S(2)}, u32[]{:S(2)}) collective-permute-start(f32[8,256]{1,0:T(8,128)} %get-tuple-element.18), channel_id=1, source_target_pairs={{0,4},{4,8},{8,12},{12,16},{16,20},{20,24},{24,28},{28,0},{1,5},{5... | collective-permute-start | bytes 24584 | tf_op jit(solution)/shard_map/ppermute | solution.py:1240
  17.3 0.6 copy-start.6
  30.2 10.8 %copy-start.3 = (f32[32,8,192]{2,1,0:T(8,128)}, f32[32,8,192]{2,1,0:T(8,128)S(1)}, u32[]{:S(2)}) copy-start(f32[32,8,192]{2,1,0:T(8,128)S(1)} %all-to-all-done.static_ref) | copy-start | bytes 589828
  30.3 12.3 %all-to-all-start.1 = ((f32[32,1,192]{2,1,0:T(1,128)}), f32[32,1,192]{2,1,0:T(1,128)S(1)}, u32[]{:S(2)}, u32[]{:S(2)}) async-start(f32[32,1,192]{2,1,0:T(1,128)} %get-tuple-element.23), calls=%async_computation.1 | async-start | bytes 65536 | tf_op jit(solution)/shard_map/all_to_all | solution.py:1233
  42.6 0.6 copy-start.4
  60.1 18.6 %all-to-all-start.2 = ((f32[16,128,128]{2,1,0:T(8,128)}), f32[16,128,128]{2,1,0:T(8,128)S(1)}, u32[]{:S(2)}, u32[]{:S(2)}) async-start(f32[16,128,128]{2,1,0:T(8,128)} %bitcast.19), calls=%async_computation.2 | async-start | bytes 2097152 | tf_op jit(solution)/shard_map/all_to_all | solution.py:1233
  77.4 21.6 %copy-start = (f32[256,256]{1,0:T(8,128)S(1)}, f32[256,256]{1,0:T(8,128)}, u32[]{:S(2)}) copy-start(f32[256,256]{1,0:T(8,128)} %constant.67.clone.table_ref) | copy-start | bytes 786436
  77.5 21.6 %copy-start.1 = (f32[1,192]{1,0:T(1,128)S(1)}, f32[1,192]{1,0:T(1,128)}, u32[]{:S(2)}) copy-start(f32[1,192]{1,0:T(1,128)} %energies.1.short_hbm) | copy-start | bytes 2308
  77.5 21.6 %copy-start.2 = (f32[1,192]{1,0:T(1,128)S(1)}, f32[1,192]{1,0:T(1,128)}, u32[]{:S(2)}) copy-start(f32[1,192]{1,0:T(1,128)} %get-tuple-element.29.charge_hbm) | copy-start | bytes 2308

commit v10 on v7

--- a/solution.py
+++ b/solution.py
@@ -13,6 +13,7 @@
 AXIS = 16
 VMEM_BYTES = 60 * 2**20
 REACH = 16
+FIELDS = 7
 
 
 HIGH = lax.Precision.HIGHEST
@@ -414,6 +415,7 @@
     padded_ref,
     weight_in_ref,
     weight_hidden_ref,
+    row_ref,
     semaphores,
 ):
     fetches = [
@@ -545,7 +547,7 @@
             one_group(pl.multiple_of(step * unroll * group + part * group, group))
         return carry
 
-    unroll = 4 if rows % (4 * group) == 0 else 1
+    unroll = rows // group
     lax.fori_loop(0, rows // (unroll * group), body, 0)
 
     chunks = (descriptor_ref.shape[1] + 127) // 128
@@ -565,7 +567,7 @@
             else:
                 descriptor_ref[band, 128 * chunk : 128 * chunk + last] = total[:, 0:last]
 
-    bands = 4 if atoms % 32 == 0 else 1
+    bands = 8 if atoms % 64 == 0 else 1
 
     def describe(step, carry):
         for part in range(bands):
@@ -582,18 +584,16 @@
     kind = types_ref[...].astype(jnp.float32)
     charge = (1.0 - kind) * charges_ref[0] + kind * charges_ref[1] + natural_order(shift)
     charge_ref[...] = charge
-    fields = jnp.concatenate(
-        [
-            cell_x_ref[...].astype(jnp.float32),
-            (cell_y_ref[...] + base_ref[0]).astype(jnp.float32),
-            cell_z_ref[...].astype(jnp.float32),
-        ]
-        + [fraction_ref[axis] for axis in range(3)]
-        + [charge, jnp.zeros((1, atoms), jnp.float32)],
-        axis=0,
-    )
+    fields = [
+        cell_x_ref[...].astype(jnp.float32),
+        (cell_y_ref[...] + base_ref[0]).astype(jnp.float32),
+        cell_z_ref[...].astype(jnp.float32),
+    ]
+    fields = fields + [fraction_ref[axis] for axis in range(3)] + [charge]
+    for place, field in enumerate(fields):
+        row_ref[:, atoms * place : atoms * (place + 1)] = field
     for copy in range(copies_ref.shape[0]):
-        copies_ref[copy] = fields
+        copies_ref[copy] = row_ref[...]
     store.wait()
 
 
@@ -636,7 +636,7 @@
     results = [
         jax.ShapeDtypeStruct((atoms, desc), jnp.float32),
         jax.ShapeDtypeStruct((1, atoms), jnp.float32),
-        jax.ShapeDtypeStruct((copies, 8, atoms), jnp.float32),
+        jax.ShapeDtypeStruct((copies, 1, FIELDS * atoms), jnp.float32),
     ]
     return pl.pallas_call(
         functools.partial(network_kernel, ghosts),
@@ -655,6 +655,7 @@
             pltpu.VMEM((3, 128, 128), jnp.float32),
             pltpu.VMEM((width, desc), jnp.float32),
             pltpu.VMEM(weight_hidden.shape, jnp.float32),
+            pltpu.VMEM((1, FIELDS * atoms), jnp.float32),
             pltpu.SemaphoreType.DMA((3,)),
         ],
         compiler_params=pltpu.CompilerParams(vmem_limit_bytes=VMEM_BYTES),
@@ -856,7 +857,7 @@
     second_refs, first_refs = pair_refs[:4], pair_refs[4:]
     bricks = NG // block_x
     parts = waves_ref.shape[0]
-    block = static_ref.shape[2]
+    block = static_ref.shape[2] // FIELDS
     count = full_ref.shape[0]
     step = pl.program_id(0)
     later = later_hbm.shape[0]
@@ -875,8 +876,10 @@
         for slab in range(slabs):
             lanes = slice(block * slab, block * (slab + 1))
             for brick in range(bricks):
-                atoms_ref[brick, :, lanes] = static_ref[slab * bricks + brick]
-        grid_ref[...] = jnp.zeros_like(grid_ref)
+                for field in range(FIELDS):
+                    atoms_ref[brick, field : field + 1, lanes] = static_ref[
+                        slab * bricks + brick, :, block * field : block * (field + 1)
+                    ]
         for ref in second_refs:
             ref[...] = jnp.zeros_like(ref)
         for brick in range(bricks):
@@ -894,10 +897,16 @@
                 fields, 0, block_y, slabs, second_refs[2 * (brick % 2)], second_refs[2 * (brick % 2) + 1]
             )
             spread = triple(table, second, LANES)
-            rows = slice(block_x * brick, block_x * brick + window)
+            start = block_x * brick
+            extra = window - block_x
             for part in range(parts):
-                grid_ref[part, rows, :] += spread[part * window : part * window + window]
-        extra = window - block_x
+                shared = spread[part * window : part * window + extra]
+                if brick > 0:
+                    shared = shared + grid_ref[part, start : start + extra, :]
+                grid_ref[part, start : start + extra, :] = shared
+                grid_ref[part, start + extra : start + window, :] = spread[
+                    part * window + extra : part * window + window
+                ]
         for part in range(parts):
             grid_ref[part, 0:extra, :] += grid_ref[part, NG : NG + extra, :]
         store.start()
@@ -926,7 +935,7 @@
 def spread_and_solve(
     block_x, block_y, window, kappa, pair, static, waves, cosine_row, tables, last, short
 ):
-    devices, _, atoms = static.shape
+    atoms = static.shape[2] // FIELDS
     slabs = NG // block_y
     bricks = NG // block_x
     parts = waves.shape[0]

time: 99.5 us -> 96.3 us (0.968)
  waiting for transfers between devices: 10.2 us -> 8.33 us
  Pallas kernels: 53.6 us -> 52.3 us
    all_to_all x2, waiting for transfers between devices: 6.02 us -> 4.17 us  [exchange(): lax.all_to_all(values, axes, split_axis=0, concat_axis=0, tiled=True, axi...]
    pallas_call x1, Pallas kernels: 13.9 us -> 12.5 us  [networks(): pl.pallas_call(functools.partial(network_kernel, ghosts), grid=(1,), out_...]
  transfers between devices with their start and end apart: 4 -> 4, of which waited for: 4 -> 4; matrix products, arithmetic and copies ran while one was open for 1% -> 1% of each run, Pallas kernels for 18% -> 19%
where the time goes in v10:
time: 96.3 us; the launch traced here: 95.8 us
  Pallas kernels  52.3 us (54%)
  blocking collectives  20.4 us (21%)
  starting transfers between devices  11.2 us (12%)
  waiting for transfers between devices  8.33 us (9%)
  local copies, waits for them, and re-layouts  2.63 us (3%)
    all_to_all x1, blocking collectives, exchange(): lax.all_to_all(values, axes, split_axis=0, concat_axis=0, tiled=True, axi...  20.4 us
    pallas_call x1, Pallas kernels, spread_and_solve(): pl.pallas_call(functools.partial(spread_kernel, block_x, block_y, window)...  17.1 us
    pallas_call x1, Pallas kernels, solve_and_sample(): pl.pallas_call(functools.partial(sample_kernel, block_x, block_y, window)...  13.5 us
    pallas_call x1, Pallas kernels, networks(): pl.pallas_call(functools.partial(network_kernel, ghosts), grid=(1,), out_...  12.5 us
    all_to_all x2, starting transfers between devices, exchange(): lax.all_to_all(values, axes, split_axis=0, concat_axis=0, tiled=True, axi...  7.86 us
    pallas_call x1, Pallas kernels, energies(): pl.pallas_call(energy_kernel, grid=(1,), out_shape=result, in_specs=whole...  4.33 us
    all_to_all x2, waiting for transfers between devices, exchange(): lax.all_to_all(values, axes, split_axis=0, concat_axis=0, tiled=True, axi...  4.17 us
    pallas_call x1, Pallas kernels, finish(): pl.pallas_call(functools.partial(finish_kernel, block_y), grid=(groups,),...  3.56 us
  transfers between devices with their start and end apart: 4, of which 4 were waited for; matrix products, arithmetic and copies ran while one was open for 1% of the time, Pallas kernels for 19%

profile of v10, /device:TPU:0, one launch (start us, length us, event | category | flops | bytes accessed | tf_op | source)
XLA Modules:
  0.0 95.8 jit_solution(17888997598351138485)
XLA Ops:
  0.6 1.4 %collect_atoms.1 = (f32[8,256]{1,0:T(8,128)}, f32[8,256]{1,0:T(8,128)}) custom-call(f32[3,1,192]{2,1,0:T(1,128)} %positions_ref.1, s32[1,192]{1,0:T(1,128)} %types_ref.3, s32[1,192]{1,0:T(1,128)} %count_ref.1, s32[1,192]{1,0:T(1,128)} %send_ref.1), custom_call_target="tpu_custom_call" | custom-call | tf_op jit(solution)/shard_map/collect_atoms/pallas_call | solution.py:349
  2.0 3.3 %collective-permute-start.1 = (f32[8,256]{1,0:T(8,128)}, f32[8,256]{1,0:T(8,128)S(1)}, u32[]{:S(2)}, u32[]{:S(2)}) collective-permute-start(f32[8,256]{1,0:T(8,128)} %get-tuple-element.14), channel_id=1, source_target_pairs={{4,0},{8,4},{12,8},{16,12},{20,16},{24,20},{28,24},{0,28},{5,1},{9... | collective-permute-start | bytes 24584 | tf_op jit(solution)/shard_map/ppermute | solution.py:1236
  5.4 0.0 collective-permute-start
  5.4 1.6 %collective-permute-done.1.upper_ref = f32[8,256]{1,0:T(8,128)S(1)} collective-permute-done((f32[8,256]{1,0:T(8,128)}, f32[8,256]{1,0:T(8,128)S(1)}, u32[]{:S(2)}, u32[]{:S(2)}) %collective-permute-start.1) | collective-permute-done | bytes 8224 | tf_op jit(solution)/shard_map/ppermute | solution.py:1236
  7.0 0.0 copy-start.4
  7.0 2.6 %collective-permute-done.lower_ref = f32[8,256]{1,0:T(8,128)S(1)} collective-permute-done((f32[8,256]{1,0:T(8,128)}, f32[8,256]{1,0:T(8,128)S(1)}, u32[]{:S(2)}, u32[]{:S(2)}) %collective-permute-start) | collective-permute-done | bytes 8224 | tf_op jit(solution)/shard_map/ppermute | solution.py:1235
  9.6 0.0 copy-start.5
  9.6 0.0 copy-done.4
  9.6 0.6 copy-done.5
  10.2 12.5 %networks.1 = (f32[192,1600]{1,0:T(8,128)}, f32[1,192]{1,0:T(1,128)}, f32[32,1,1344]{2,1,0:T(1,128)}) custom-call(s32[1]{0:T(128)} %bitcast.1.base_ref, f32[2]{0:T(128)} %charges_ref.1, f32[8,256]{1,0:T(8,128)} %get-tuple-element.13.own_ref, f32[8,256]{1,0:T(8,128)} %copy-done.5, f32[8,256]{1,0:T(8,128)} %copy-done.4, s32[64,192]{1,0:T(8,128)} %bitcast.20, ...), custom_call_target="tpu_custom_call" | custom-call | tf_op jit(solution)/shard_map/networks/pallas_call | solution.py:641
  22.7 4.0 %all-to-all-start = ((f32[32,1,1344]{2,1,0:T(1,128)}), f32[32,1,1344]{2,1,0:T(1,128)S(1)}, u32[]{:S(2)}, u32[]{:S(2)}) async-start(f32[32,1,1344]{2,1,0:T(1,128)} %get-tuple-element.15), calls=%async_computation | async-start | bytes 360448 | tf_op jit(solution)/shard_map/all_to_all | solution.py:1228
  26.7 0.7 copy.27.waves_ref
  27.4 0.7 copy.26.kappa_ref
  28.0 4.3 %energies.1.short_hbm = f32[1,192]{1,0:T(1,128)} custom-call(f32[192,1600]{1,0:T(8,128)} %get-tuple-element.16.descriptor_ref, f32[240,1600]{1,0:T(8,128)} %bitcast.17, f32[2,240,240]{2,1,0:T(8,128)} %weight_hidden_ref.1, f32[1,240]{1,0:T(1,128)} %bitcast.22), custom_call_target="tpu_custom_call" | custom-call | flops 442368000 | bytes 1536000 | tf_op jit(solution)/shard_map/energies/pallas_call | solution.py:677
  32.4 3.0 %all-to-all-done.static_ref = f32[32,1,1344]{2,1,0:T(1,128)S(1)} async-done(((f32[32,1,1344]{2,1,0:T(1,128)}), f32[32,1,1344]{2,1,0:T(1,128)S(1)}, u32[]{:S(2)}, u32[]{:S(2)}) %all-to-all-start) | async-done | bytes 172064 | tf_op jit(solution)/shard_map/all_to_all | solution.py:1228
  35.4 0.0 copy-start.3
  35.4 0.7 copy-done.3
  36.0 17.1 %spread_and_solve.1 = (f32[16,4,4,8,128]{4,3,2,1,0:T(8,128)}, f32[8,256,256]{2,1,0:T(8,128)}, f32[8,8,768]{2,1,0:T(8,128)}, f32[8,256,256]{2,1,0:T(8,128)}) custom-call(f32[16,2]{1,0:T(8,128)} %copy.26.kappa_ref, s32[1]{0:T(128)} %bitcast.pair_ref, f32[32,1,1344]{2,1,0:T(1,128)} %copy-done.3, s32[16,2]{1,0:T(8,128)} %copy.27.waves_ref, ...), custom_call_target="tpu_custom_call" | custom-call | tf_op jit(solution)/shard_map/spread_and_solve/pallas_call | solution.py:947
  53.1 3.9 %all-to-all-start.1 = ((f32[16,128,128]{2,1,0:T(8,128)}), f32[16,128,128]{2,1,0:T(8,128)S(1)}, u32[]{:S(2)}, u32[]{:S(2)}) async-start(f32[16,128,128]{2,1,0:T(8,128)} %bitcast.19), calls=%async_computation.1 | async-start | bytes 2097152 | tf_op jit(solution)/shard_map/all_to_all | solution.py:1228
  57.0 13.5 %solve_and_sample.1 = f32[16,17,8,128]{3,2,1,0:T(8,128)} custom-call(f32[16,2]{1,0:T(8,128)} %copy.26.kappa_ref, s32[1]{0:T(128)} %bitcast.pair_ref, f32[8,8,768]{2,1,0:T(8,128)} %get-tuple-element.18.atoms_ref, s32[16,2]{1,0:T(8,128)} %copy.27.waves_ref, f32[1,128]{1,0:T(1,128)} %constant.64.clone.cosine_ref, f32[2,256,256]{2,1,0:T(8,128)} %constant.65.clone.tables_hbm, ...), custom_call_target="tpu_custom_call" | custom-call | flops 6442450944 | bytes 2097152 | tf_op jit(solution)/shard_map/solve_and_sample/pallas_call | solution.py:1082
  70.5 0.0 copy-start
  70.5 0.0 copy-start.1
  70.5 0.0 copy-start.2
  70.5 1.2 %all-to-all-done.1 = f32[16,128,128]{2,1,0:T(8,128)S(1)} async-done(((f32[16,128,128]{2,1,0:T(8,128)}), f32[16,128,128]{2,1,0:T(8,128)S(1)}, u32[]{:S(2)}, u32[]{:S(2)}) %all-to-all-start.1) | async-done | bytes 1048608 | tf_op jit(solution)/shard_map/all_to_all | solution.py:1228
  71.7 20.4 %all_to_all.15 = f32[16,136,128]{2,1,0:T(8,128)S(1)} all-to-all(f32[16,136,128]{2,1,0:T(8,128)} %bitcast.18), channel_id=1, replica_groups={{0,1,4,5,8,9,12,13,16,17,20,21,24,25,28,29},{2,3,6,7,10,11,14,15,18,19,..., dimensions={0} | all-to-all | bytes 2228224 | tf_op jit(solution)/shard_map/all_to_all | solution.py:1228
  92.1 0.0 copy-done
  92.1 0.0 copy-done.1
  92.1 0.0 copy-done.2
  92.1 3.6 %finish.1 = (f32[32,64,256]{2,1,0:T(8,128)}, f32[1,192]{1,0:T(1,128)}) custom-call(f32[16,4,4,8,128]{4,3,2,1,0:T(8,128)S(1)} %bitcast.15, f32[16,17,8,128]{3,2,1,0:T(8,128)S(1)} %bitcast.13, f32[16,17,8,128]{3,2,1,0:T(8,128)S(1)} %bitcast.14, f32[1,192]{1,0:T(1,128)S(1)} %copy-done.1, f32[1,192]{1,0:T(1,128)S(1)} %copy-done.2, f32[256,256]{1,0:T(8,128)S(1)} %copy-done), custom_call_target="tpu_custom_call" | custom-call | tf_op jit(solution)/shard_map/finish/pallas_call | solution.py:1154
  (4 shorter events, 0.0 us)
Async XLA Ops:
  2.0 4.9 %collective-permute-start.1 = (f32[8,256]{1,0:T(8,128)}, f32[8,256]{1,0:T(8,128)S(1)}, u32[]{:S(2)}, u32[]{:S(2)}) collective-permute-start(f32[8,256]{1,0:T(8,128)} %get-tuple-element.14), channel_id=1, source_target_pairs={{4,0},{8,4},{12,8},{16,12},{20,16},{24,20},{28,24},{0,28},{5,1},{9... | collective-permute-start | bytes 24584 | tf_op jit(solution)/shard_map/ppermute | solution.py:1236
  5.4 4.2 %collective-permute-start = (f32[8,256]{1,0:T(8,128)}, f32[8,256]{1,0:T(8,128)S(1)}, u32[]{:S(2)}, u32[]{:S(2)}) collective-permute-start(f32[8,256]{1,0:T(8,128)} %get-tuple-element.14), channel_id=1, source_target_pairs={{0,4},{4,8},{8,12},{12,16},{16,20},{20,24},{24,28},{28,0},{1,5},{5... | collective-permute-start | bytes 24584 | tf_op jit(solution)/shard_map/ppermute | solution.py:1235
  7.0 2.6 %copy-start.4 = (f32[8,256]{1,0:T(8,128)}, f32[8,256]{1,0:T(8,128)S(1)}, u32[]{:S(2)}) copy-start(f32[8,256]{1,0:T(8,128)S(1)} %collective-permute-done.1.upper_ref) | copy-start | bytes 24580
  9.6 0.6 copy-start.5
  22.7 12.7 %all-to-all-start = ((f32[32,1,1344]{2,1,0:T(1,128)}), f32[32,1,1344]{2,1,0:T(1,128)S(1)}, u32[]{:S(2)}, u32[]{:S(2)}) async-start(f32[32,1,1344]{2,1,0:T(1,128)} %get-tuple-element.15), calls=%async_computation | async-start | bytes 360448 | tf_op jit(solution)/shard_map/all_to_all | solution.py:1228
  35.4 0.7 copy-start.3
  53.1 18.6 %all-to-all-start.1 = ((f32[16,128,128]{2,1,0:T(8,128)}), f32[16,128,128]{2,1,0:T(8,128)S(1)}, u32[]{:S(2)}, u32[]{:S(2)}) async-start(f32[16,128,128]{2,1,0:T(8,128)} %bitcast.19), calls=%async_computation.1 | async-start | bytes 2097152 | tf_op jit(solution)/shard_map/all_to_all | solution.py:1228
  70.5 21.6 %copy-start = (f32[256,256]{1,0:T(8,128)S(1)}, f32[256,256]{1,0:T(8,128)}, u32[]{:S(2)}) copy-start(f32[256,256]{1,0:T(8,128)} %constant.67.clone.table_ref) | copy-start | bytes 786436
  70.5 21.6 %copy-start.1 = (f32[1,192]{1,0:T(1,128)S(1)}, f32[1,192]{1,0:T(1,128)}, u32[]{:S(2)}) copy-start(f32[1,192]{1,0:T(1,128)} %energies.1.short_hbm) | copy-start | bytes 2308
  70.5 21.6 %copy-start.2 = (f32[1,192]{1,0:T(1,128)S(1)}, f32[1,192]{1,0:T(1,128)}, u32[]{:S(2)}) copy-start(f32[1,192]{1,0:T(1,128)} %get-tuple-element.21.charge_hbm) | copy-start | bytes 2308

commit v11 on v10

--- a/solution.py
+++ b/solution.py
@@ -844,9 +844,10 @@
     last_hbm,
     short_hbm,
     sent_ref,
-    full_ref,
+    full_hbm,
     atoms_ref,
     later_hbm,
+    full_ref,
     grid_ref,
     tables_ref,
     last_ref,
@@ -858,74 +859,79 @@
     bricks = NG // block_x
     parts = waves_ref.shape[0]
     block = static_ref.shape[2] // FIELDS
-    count = full_ref.shape[0]
-    step = pl.program_id(0)
     later = later_hbm.shape[0]
     store = pltpu.make_async_copy(
         grid_ref.at[pl.ds(parts - later, later), pl.ds(0, NG)], later_hbm, semaphores.at[2]
     )
-
-    @pl.when(step == 0)
-    def _():
-        fetches = [
-            pltpu.make_async_copy(tables_hbm, tables_ref, semaphores.at[0]),
-            pltpu.make_async_copy(last_hbm.at[pair_ref[0]], last_ref, semaphores.at[1]),
-        ]
-        for fetch in fetches:
-            fetch.start()
-        for slab in range(slabs):
-            lanes = slice(block * slab, block * (slab + 1))
-            for brick in range(bricks):
-                for field in range(FIELDS):
-                    atoms_ref[brick, field : field + 1, lanes] = static_ref[
-                        slab * bricks + brick, :, block * field : block * (field + 1)
-                    ]
-        for ref in second_refs:
-            ref[...] = jnp.zeros_like(ref)
+    fetches = [
+        pltpu.make_async_copy(tables_hbm, tables_ref, semaphores.at[0]),
+        pltpu.make_async_copy(last_hbm.at[pair_ref[0]], last_ref, semaphores.at[1]),
+    ]
+    for fetch in fetches:
+        fetch.start()
+    for slab in range(slabs):
+        lanes = slice(block * slab, block * (slab + 1))
         for brick in range(bricks):
-            fields = atoms_ref[brick]
-            table = first_third_split(
-                fields,
-                waves_ref,
-                cosine_ref,
-                window,
-                fields[6:7, :],
-                first_refs[2 * (brick % 2)],
-                first_refs[2 * (brick % 2) + 1],
+            for field in range(FIELDS):
+                atoms_ref[brick, field : field + 1, lanes] = static_ref[
+                    slab * bricks + brick, :, block * field : block * (field + 1)
+                ]
+    for ref in second_refs:
+        ref[...] = jnp.zeros_like(ref)
+    for brick in range(bricks):
+        fields = atoms_ref[brick]
+        table = first_third_split(
+            fields,
+            waves_ref,
+            cosine_ref,
+            window,
+            fields[6:7, :],
+            first_refs[2 * (brick % 2)],
+            first_refs[2 * (brick % 2) + 1],
+        )
+        second = second_factors(
+            fields, 0, block_y, slabs, second_refs[2 * (brick % 2)], second_refs[2 * (brick % 2) + 1]
+        )
+        spread = triple(table, second, LANES)
+        start = block_x * brick
+        extra = window - block_x
+        for part in range(parts):
+            shared = spread[part * window : part * window + extra]
+            if brick > 0:
+                shared = shared + grid_ref[part, start : start + extra, :]
+            grid_ref[part, start : start + extra, :] = shared
+            grid_ref[part, start + extra : start + window, :] = spread[
+                part * window + extra : part * window + window
+            ]
+    for part in range(parts):
+        grid_ref[part, 0:extra, :] += grid_ref[part, NG : NG + extra, :]
+    store.start()
+    for fetch in fetches:
+        fetch.wait()
+
+    count = 4
+    outs = []
+    for step in range(full_hbm.shape[0] // count):
+        planes = [grid_ref[count * step + part, 0:NG, :] for part in range(count)]
+        full = transform(planes, kappa_ref, count * step, tables_ref, last_ref)
+        for part in range(count):
+            full_ref[count * step + part] = full[NG * part : NG * (part + 1)]
+
+        def put(pair, brick, side, group, tile):
+            sent_ref[2 * brick + side, group, count // 2 * step + pair] = tile
+
+        send_blocks(full, block_x, block_y, put)
+        ours = pl.ds(count * step, count)
+        outs.append(
+            pltpu.make_async_copy(
+                full_ref.at[ours], full_hbm.at[ours], semaphores.at[3 + step]
             )
-            second = second_factors(
-                fields, 0, block_y, slabs, second_refs[2 * (brick % 2)], second_refs[2 * (brick % 2) + 1]
-            )
-            spread = triple(table, second, LANES)
-            start = block_x * brick
-            extra = window - block_x
-            for part in range(parts):
-                shared = spread[part * window : part * window + extra]
-                if brick > 0:
-                    shared = shared + grid_ref[part, start : start + extra, :]
-                grid_ref[part, start : start + extra, :] = shared
-                grid_ref[part, start + extra : start + window, :] = spread[
-                    part * window + extra : part * window + window
-                ]
-        for part in range(parts):
-            grid_ref[part, 0:extra, :] += grid_ref[part, NG : NG + extra, :]
-        store.start()
-        for fetch in fetches:
-            fetch.wait()
-
-    planes = [grid_ref[count * step + part, 0:NG, :] for part in range(count)]
-    full = transform(planes, kappa_ref, count * step, tables_ref, last_ref)
-    for part in range(count):
-        full_ref[part] = full[NG * part : NG * (part + 1)]
-
-    def put(pair, brick, side, group, tile):
-        sent_ref[2 * brick + side, group, pair] = tile
-
-    send_blocks(full, block_x, block_y, put)
-
-    @pl.when(step == pl.num_programs(0) - 1)
-    def _():
-        store.wait()
+        )
+    for out in outs:
+        out.start()
+    for out in outs:
+        out.wait()
+    store.wait()
 
 
 def early_pairs(parts):
@@ -940,13 +946,12 @@
     bricks = NG // block_x
     parts = waves.shape[0]
     pairs = early_pairs(parts)
-    count = 4
     anywhere = pl.BlockSpec(memory_space=pl.ANY)
     scalars = pl.BlockSpec(memory_space=pltpu.SMEM)
-    sent_block = (2 * bricks, block_x // 8, count // 2, 8, 128)
+    sent_block = (2 * bricks, block_x // 8, pairs, 8, 128)
     return pl.pallas_call(
         functools.partial(spread_kernel, block_x, block_y, window),
-        grid=(2 * pairs // count,),
+        grid=(1,),
         out_shape=[
             jax.ShapeDtypeStruct((2 * bricks, block_x // 8, pairs, 8, 128), jnp.float32),
             jax.ShapeDtypeStruct((2 * pairs, NG, NG), jnp.float32),
@@ -957,16 +962,17 @@
         + whole_specs(static, waves, cosine_row)
         + [anywhere, anywhere, anywhere],
         out_specs=[
-            pl.BlockSpec(sent_block, lambda step: (0, 0, step, 0, 0)),
-            pl.BlockSpec((count, NG, NG), lambda step: (step, 0, 0)),
+            whole(sent_block),
+            anywhere,
             whole((bricks, 8, slabs * atoms)),
             anywhere,
         ],
         scratch_shapes=[
+            pltpu.VMEM((2 * pairs, NG, NG), jnp.float32),
             pltpu.VMEM((parts, NG + window - block_x, NG), jnp.float32),
             pltpu.VMEM(tables.shape, tables.dtype),
             pltpu.VMEM(last.shape[1:], last.dtype),
-            pltpu.SemaphoreType.DMA((3,)),
+            pltpu.SemaphoreType.DMA((3 + pairs // 2,)),
         ]
         + [pltpu.VMEM((NG, slabs * atoms), jnp.bfloat16)] * 4
         + [pltpu.VMEM((parts * window, slabs * atoms), jnp.bfloat16)] * 4,

time: 96.3 us -> 97 us (level)
  transfers between devices with their start and end apart: 4 -> 4, of which waited for: 4 -> 4; matrix products, arithmetic and copies ran while one was open for 1% -> 1% of each run, Pallas kernels for 19% -> 18%
where the time goes in v11:
time: 97 us; the launch traced here: 96.5 us
  Pallas kernels  53 us (55%)
  blocking collectives  20.4 us (21%)
  starting transfers between devices  11.2 us (12%)
  waiting for transfers between devices  8.37 us (9%)
  local copies, waits for them, and re-layouts  2.63 us (3%)
    all_to_all x1, blocking collectives, exchange(): lax.all_to_all(values, axes, split_axis=0, concat_axis=0, tiled=True, axi...  20.4 us
    pallas_call x1, Pallas kernels, spread_and_solve(): pl.pallas_call(functools.partial(spread_kernel, block_x, block_y, window)...  17.8 us
    pallas_call x1, Pallas kernels, solve_and_sample(): pl.pallas_call(functools.partial(sample_kernel, block_x, block_y, window)...  13.5 us
    pallas_call x1, Pallas kernels, networks(): pl.pallas_call(functools.partial(network_kernel, ghosts), grid=(1,), out_...  12.5 us
    all_to_all x2, starting transfers between devices, exchange(): lax.all_to_all(values, axes, split_axis=0, concat_axis=0, tiled=True, axi...  7.82 us
    pallas_call x1, Pallas kernels, energies(): pl.pallas_call(energy_kernel, grid=(1,), out_shape=result, in_specs=whole...  4.33 us
    all_to_all x2, waiting for transfers between devices, exchange(): lax.all_to_all(values, axes, split_axis=0, concat_axis=0, tiled=True, axi...  4.21 us
    pallas_call x1, Pallas kernels, finish(): pl.pallas_call(functools.partial(finish_kernel, block_y), grid=(groups,),...  3.56 us
  transfers between devices with their start and end apart: 4, of which 4 were waited for; matrix products, arithmetic and copies ran while one was open for 1% of the time, Pallas kernels for 18%

profile of v11, /device:TPU:0, one launch (start us, length us, event | category | flops | bytes accessed | tf_op | source)
XLA Modules:
  0.0 96.5 jit_solution(3840729014981359808)
XLA Ops:
  0.6 1.4 %collect_atoms.1 = (f32[8,256]{1,0:T(8,128)}, f32[8,256]{1,0:T(8,128)}) custom-call(f32[3,1,192]{2,1,0:T(1,128)} %positions_ref.1, s32[1,192]{1,0:T(1,128)} %types_ref.3, s32[1,192]{1,0:T(1,128)} %count_ref.1, s32[1,192]{1,0:T(1,128)} %send_ref.1), custom_call_target="tpu_custom_call" | custom-call | tf_op jit(solution)/shard_map/collect_atoms/pallas_call | solution.py:349
  2.0 3.3 %collective-permute-start.1 = (f32[8,256]{1,0:T(8,128)}, f32[8,256]{1,0:T(8,128)S(1)}, u32[]{:S(2)}, u32[]{:S(2)}) collective-permute-start(f32[8,256]{1,0:T(8,128)} %get-tuple-element.14), channel_id=1, source_target_pairs={{4,0},{8,4},{12,8},{16,12},{20,16},{24,20},{28,24},{0,28},{5,1},{9... | collective-permute-start | bytes 24584 | tf_op jit(solution)/shard_map/ppermute | solution.py:1242
  5.4 0.0 collective-permute-start
  5.4 1.6 %collective-permute-done.1.upper_ref = f32[8,256]{1,0:T(8,128)S(1)} collective-permute-done((f32[8,256]{1,0:T(8,128)}, f32[8,256]{1,0:T(8,128)S(1)}, u32[]{:S(2)}, u32[]{:S(2)}) %collective-permute-start.1) | collective-permute-done | bytes 8224 | tf_op jit(solution)/shard_map/ppermute | solution.py:1242
  7.0 0.0 copy-start.4
  7.0 2.6 %collective-permute-done.lower_ref = f32[8,256]{1,0:T(8,128)S(1)} collective-permute-done((f32[8,256]{1,0:T(8,128)}, f32[8,256]{1,0:T(8,128)S(1)}, u32[]{:S(2)}, u32[]{:S(2)}) %collective-permute-start) | collective-permute-done | bytes 8224 | tf_op jit(solution)/shard_map/ppermute | solution.py:1241
  9.6 0.0 copy-start.5
  9.6 0.0 copy-done.4
  9.6 0.6 copy-done.5
  10.2 12.5 %networks.1 = (f32[192,1600]{1,0:T(8,128)}, f32[1,192]{1,0:T(1,128)}, f32[32,1,1344]{2,1,0:T(1,128)}) custom-call(s32[1]{0:T(128)} %bitcast.1.base_ref, f32[2]{0:T(128)} %charges_ref.1, f32[8,256]{1,0:T(8,128)} %get-tuple-element.13.own_ref, f32[8,256]{1,0:T(8,128)} %copy-done.5, f32[8,256]{1,0:T(8,128)} %copy-done.4, s32[64,192]{1,0:T(8,128)} %bitcast.20, ...), custom_call_target="tpu_custom_call" | custom-call | tf_op jit(solution)/shard_map/networks/pallas_call | solution.py:641
  22.7 4.2 %all-to-all-start = ((f32[32,1,1344]{2,1,0:T(1,128)}), f32[32,1,1344]{2,1,0:T(1,128)S(1)}, u32[]{:S(2)}, u32[]{:S(2)}) async-start(f32[32,1,1344]{2,1,0:T(1,128)} %get-tuple-element.15), calls=%async_computation | async-start | bytes 360448 | tf_op jit(solution)/shard_map/all_to_all | solution.py:1234
  26.8 0.7 copy.27.waves_ref
  27.5 0.7 copy.26.kappa_ref
  28.2 4.3 %energies.1.short_hbm = f32[1,192]{1,0:T(1,128)} custom-call(f32[192,1600]{1,0:T(8,128)} %get-tuple-element.16.descriptor_ref, f32[240,1600]{1,0:T(8,128)} %bitcast.17, f32[2,240,240]{2,1,0:T(8,128)} %weight_hidden_ref.1, f32[1,240]{1,0:T(1,128)} %bitcast.22), custom_call_target="tpu_custom_call" | custom-call | flops 442368000 | bytes 1536000 | tf_op jit(solution)/shard_map/energies/pallas_call | solution.py:677
  32.6 2.8 %all-to-all-done.static_ref = f32[32,1,1344]{2,1,0:T(1,128)S(1)} async-done(((f32[32,1,1344]{2,1,0:T(1,128)}), f32[32,1,1344]{2,1,0:T(1,128)S(1)}, u32[]{:S(2)}, u32[]{:S(2)}) %all-to-all-start) | async-done | bytes 172064 | tf_op jit(solution)/shard_map/all_to_all | solution.py:1234
  35.4 0.0 copy-start.3
  35.4 0.7 copy-done.3
  36.0 17.8 %spread_and_solve.1 = (f32[16,4,4,8,128]{4,3,2,1,0:T(8,128)}, f32[8,256,256]{2,1,0:T(8,128)}, f32[8,8,768]{2,1,0:T(8,128)}, f32[8,256,256]{2,1,0:T(8,128)}) custom-call(f32[16,2]{1,0:T(8,128)} %copy.26.kappa_ref, s32[1]{0:T(128)} %bitcast.pair_ref, f32[32,1,1344]{2,1,0:T(1,128)} %copy-done.3, s32[16,2]{1,0:T(8,128)} %copy.27.waves_ref, ...), custom_call_target="tpu_custom_call" | custom-call | tf_op jit(solution)/shard_map/spread_and_solve/pallas_call | solution.py:952
  53.8 3.7 %all-to-all-start.1 = ((f32[16,128,128]{2,1,0:T(8,128)}), f32[16,128,128]{2,1,0:T(8,128)S(1)}, u32[]{:S(2)}, u32[]{:S(2)}) async-start(f32[16,128,128]{2,1,0:T(8,128)} %bitcast.19), calls=%async_computation.1 | async-start | bytes 2097152 | tf_op jit(solution)/shard_map/all_to_all | solution.py:1234
  57.5 13.5 %solve_and_sample.1 = f32[16,17,8,128]{3,2,1,0:T(8,128)} custom-call(f32[16,2]{1,0:T(8,128)} %copy.26.kappa_ref, s32[1]{0:T(128)} %bitcast.pair_ref, f32[8,8,768]{2,1,0:T(8,128)} %get-tuple-element.18.atoms_ref, s32[16,2]{1,0:T(8,128)} %copy.27.waves_ref, f32[1,128]{1,0:T(1,128)} %constant.64.clone.cosine_ref, f32[2,256,256]{2,1,0:T(8,128)} %constant.65.clone.tables_hbm, ...), custom_call_target="tpu_custom_call" | custom-call | flops 6442450944 | bytes 2097152 | tf_op jit(solution)/shard_map/solve_and_sample/pallas_call | solution.py:1088
  71.0 0.0 copy-start
  71.0 0.0 copy-start.1
  71.0 0.0 copy-start.2
  71.0 1.4 %all-to-all-done.1 = f32[16,128,128]{2,1,0:T(8,128)S(1)} async-done(((f32[16,128,128]{2,1,0:T(8,128)}), f32[16,128,128]{2,1,0:T(8,128)S(1)}, u32[]{:S(2)}, u32[]{:S(2)}) %all-to-all-start.1) | async-done | bytes 1048608 | tf_op jit(solution)/shard_map/all_to_all | solution.py:1234
  72.4 20.4 %all_to_all.15 = f32[16,136,128]{2,1,0:T(8,128)S(1)} all-to-all(f32[16,136,128]{2,1,0:T(8,128)} %bitcast.18), channel_id=1, replica_groups={{0,1,4,5,8,9,12,13,16,17,20,21,24,25,28,29},{2,3,6,7,10,11,14,15,18,19,..., dimensions={0} | all-to-all | bytes 2228224 | tf_op jit(solution)/shard_map/all_to_all | solution.py:1234
  92.8 0.0 copy-done
  92.8 0.0 copy-done.1
  92.8 0.0 copy-done.2
  92.8 3.6 %finish.1 = (f32[32,64,256]{2,1,0:T(8,128)}, f32[1,192]{1,0:T(1,128)}) custom-call(f32[16,4,4,8,128]{4,3,2,1,0:T(8,128)S(1)} %bitcast.15, f32[16,17,8,128]{3,2,1,0:T(8,128)S(1)} %bitcast.13, f32[16,17,8,128]{3,2,1,0:T(8,128)S(1)} %bitcast.14, f32[1,192]{1,0:T(1,128)S(1)} %copy-done.1, f32[1,192]{1,0:T(1,128)S(1)} %copy-done.2, f32[256,256]{1,0:T(8,128)S(1)} %copy-done), custom_call_target="tpu_custom_call" | custom-call | tf_op jit(solution)/shard_map/finish/pallas_call | solution.py:1160
  (4 shorter events, 0.0 us)
Async XLA Ops:
  2.0 4.9 %collective-permute-start.1 = (f32[8,256]{1,0:T(8,128)}, f32[8,256]{1,0:T(8,128)S(1)}, u32[]{:S(2)}, u32[]{:S(2)}) collective-permute-start(f32[8,256]{1,0:T(8,128)} %get-tuple-element.14), channel_id=1, source_target_pairs={{4,0},{8,4},{12,8},{16,12},{20,16},{24,20},{28,24},{0,28},{5,1},{9... | collective-permute-start | bytes 24584 | tf_op jit(solution)/shard_map/ppermute | solution.py:1242
  5.4 4.2 %collective-permute-start = (f32[8,256]{1,0:T(8,128)}, f32[8,256]{1,0:T(8,128)S(1)}, u32[]{:S(2)}, u32[]{:S(2)}) collective-permute-start(f32[8,256]{1,0:T(8,128)} %get-tuple-element.14), channel_id=1, source_target_pairs={{0,4},{4,8},{8,12},{12,16},{16,20},{20,24},{24,28},{28,0},{1,5},{5... | collective-permute-start | bytes 24584 | tf_op jit(solution)/shard_map/ppermute | solution.py:1241
  7.0 2.6 %copy-start.4 = (f32[8,256]{1,0:T(8,128)}, f32[8,256]{1,0:T(8,128)S(1)}, u32[]{:S(2)}) copy-start(f32[8,256]{1,0:T(8,128)S(1)} %collective-permute-done.1.upper_ref) | copy-start | bytes 24580
  9.6 0.6 copy-start.5
  22.7 12.7 %all-to-all-start = ((f32[32,1,1344]{2,1,0:T(1,128)}), f32[32,1,1344]{2,1,0:T(1,128)S(1)}, u32[]{:S(2)}, u32[]{:S(2)}) async-start(f32[32,1,1344]{2,1,0:T(1,128)} %get-tuple-element.15), calls=%async_computation | async-start | bytes 360448 | tf_op jit(solution)/shard_map/all_to_all | solution.py:1234
  35.4 0.7 copy-start.3
  53.8 18.6 %all-to-all-start.1 = ((f32[16,128,128]{2,1,0:T(8,128)}), f32[16,128,128]{2,1,0:T(8,128)S(1)}, u32[]{:S(2)}, u32[]{:S(2)}) async-start(f32[16,128,128]{2,1,0:T(8,128)} %bitcast.19), calls=%async_computation.1 | async-start | bytes 2097152 | tf_op jit(solution)/shard_map/all_to_all | solution.py:1234
  71.0 21.8 %copy-start = (f32[256,256]{1,0:T(8,128)S(1)}, f32[256,256]{1,0:T(8,128)}, u32[]{:S(2)}) copy-start(f32[256,256]{1,0:T(8,128)} %constant.67.clone.table_ref) | copy-start | bytes 786436
  71.0 21.8 %copy-start.1 = (f32[1,192]{1,0:T(1,128)S(1)}, f32[1,192]{1,0:T(1,128)}, u32[]{:S(2)}) copy-start(f32[1,192]{1,0:T(1,128)} %energies.1.short_hbm) | copy-start | bytes 2308
  71.0 21.8 %copy-start.2 = (f32[1,192]{1,0:T(1,128)S(1)}, f32[1,192]{1,0:T(1,128)}, u32[]{:S(2)}) copy-start(f32[1,192]{1,0:T(1,128)} %get-tuple-element.21.charge_hbm) | copy-start | bytes 2308

commit v12 on v10

--- a/solution.py
+++ b/solution.py
@@ -283,13 +283,6 @@
 
 
 def triple(left, right, dims=((1,), (0,))):
-    (left_axis,), (right_axis,) = dims
-    if left[0].shape[left_axis] % 128 == 0:
-        return multiply(
-            jnp.concatenate([left[0], left[0], left[1]], axis=left_axis),
-            jnp.concatenate([right[0], right[1], right[0]], axis=right_axis),
-            dims,
-        )
     return (
         multiply(left[0], right[0], dims)
         + multiply(left[0], right[1], dims)
@@ -509,7 +502,7 @@
         second = second + jnp.concatenate([first, first], axis=0)
         third = jnp.tanh(multiply(third_weight, stacked(second), ((1,), (0,))))
         third = third + jnp.concatenate([second, second], axis=0)
-        third_pair = split(third)
+        third_pair = jnp.concatenate(split(third), axis=0)
         for half in range(group // 4):
             columns = slice(512 * half, 512 * half + 512)
             bands = []
@@ -532,10 +525,9 @@
                 )
             environment = split(jnp.concatenate(bands, axis=0))
             both = multiply(
-                jnp.concatenate(environment, axis=0), third_pair[0][:, columns], LANES
+                jnp.concatenate(environment, axis=0), third_pair[:, columns], LANES
             )
-            sums = both[0:32] + both[32:64]
-            sums = sums + multiply(environment[0], third_pair[1][:, columns], LANES)
+            sums = both[0:32, 0:128] + both[32:64, 0:128] + both[0:32, 128:256]
             sums = sums * (1.0 / slots)
             for part in range(4):
                 moments_ref[part, pl.ds(2 * start + 8 * half, 8), :] = sums[

time: 96.3 us -> 96.6 us (level)
  no operation moved by 1% of the time
where the time goes in v12:
time: 96.6 us; the launch traced here: 96.1 us
  Pallas kernels  52.6 us (54%)
  blocking collectives  20.4 us (21%)
  starting transfers between devices  11.2 us (12%)
  waiting for transfers between devices  8.33 us (9%)
  local copies, waits for them, and re-layouts  2.63 us (3%)
    all_to_all x1, blocking collectives, exchange(): lax.all_to_all(values, axes, split_axis=0, concat_axis=0, tiled=True, axi...  20.4 us
    pallas_call x1, Pallas kernels, spread_and_solve(): pl.pallas_call(functools.partial(spread_kernel, block_x, block_y, window)...  17.2 us
    pallas_call x1, Pallas kernels, solve_and_sample(): pl.pallas_call(functools.partial(sample_kernel, block_x, block_y, window)...  13.5 us
    pallas_call x1, Pallas kernels, networks(): pl.pallas_call(functools.partial(network_kernel, ghosts), grid=(1,), out_...  12.7 us
    all_to_all x2, starting transfers between devices, exchange(): lax.all_to_all(values, axes, split_axis=0, concat_axis=0, tiled=True, axi...  7.85 us
    pallas_call x1, Pallas kernels, energies(): pl.pallas_call(energy_kernel, grid=(1,), out_shape=result, in_specs=whole...  4.33 us
    all_to_all x2, waiting for transfers between devices, exchange(): lax.all_to_all(values, axes, split_axis=0, concat_axis=0, tiled=True, axi...  4.17 us
    pallas_call x1, Pallas kernels, finish(): pl.pallas_call(functools.partial(finish_kernel, block_y), grid=(groups,),...  3.56 us
  transfers between devices with their start and end apart: 4, of which 4 were waited for; matrix products, arithmetic and copies ran while one was open for 1% of the time, Pallas kernels for 19%

profile of v12, /device:TPU:0, one launch (start us, length us, event | category | flops | bytes accessed | tf_op | source)
XLA Modules:
  0.0 96.1 jit_solution(7105938651810946282)
XLA Ops:
  0.6 1.4 %collect_atoms.1 = (f32[8,256]{1,0:T(8,128)}, f32[8,256]{1,0:T(8,128)}) custom-call(f32[3,1,192]{2,1,0:T(1,128)} %positions_ref.1, s32[1,192]{1,0:T(1,128)} %types_ref.3, s32[1,192]{1,0:T(1,128)} %count_ref.1, s32[1,192]{1,0:T(1,128)} %send_ref.1), custom_call_target="tpu_custom_call" | custom-call | tf_op jit(solution)/shard_map/collect_atoms/pallas_call | solution.py:342
  2.0 3.3 %collective-permute-start.1 = (f32[8,256]{1,0:T(8,128)}, f32[8,256]{1,0:T(8,128)S(1)}, u32[]{:S(2)}, u32[]{:S(2)}) collective-permute-start(f32[8,256]{1,0:T(8,128)} %get-tuple-element.14), channel_id=1, source_target_pairs={{4,0},{8,4},{12,8},{16,12},{20,16},{24,20},{28,24},{0,28},{5,1},{9... | collective-permute-start | bytes 24584 | tf_op jit(solution)/shard_map/ppermute | solution.py:1228
  5.4 0.0 collective-permute-start
  5.4 1.6 %collective-permute-done.1.upper_ref = f32[8,256]{1,0:T(8,128)S(1)} collective-permute-done((f32[8,256]{1,0:T(8,128)}, f32[8,256]{1,0:T(8,128)S(1)}, u32[]{:S(2)}, u32[]{:S(2)}) %collective-permute-start.1) | collective-permute-done | bytes 8224 | tf_op jit(solution)/shard_map/ppermute | solution.py:1228
  7.0 0.0 copy-start.4
  7.0 2.6 %collective-permute-done.lower_ref = f32[8,256]{1,0:T(8,128)S(1)} collective-permute-done((f32[8,256]{1,0:T(8,128)}, f32[8,256]{1,0:T(8,128)S(1)}, u32[]{:S(2)}, u32[]{:S(2)}) %collective-permute-start) | collective-permute-done | bytes 8224 | tf_op jit(solution)/shard_map/ppermute | solution.py:1227
  9.6 0.0 copy-start.5
  9.6 0.0 copy-done.4
  9.6 0.6 copy-done.5
  10.2 12.7 %networks.1 = (f32[192,1600]{1,0:T(8,128)}, f32[1,192]{1,0:T(1,128)}, f32[32,1,1344]{2,1,0:T(1,128)}) custom-call(s32[1]{0:T(128)} %bitcast.1.base_ref, f32[2]{0:T(128)} %charges_ref.1, f32[8,256]{1,0:T(8,128)} %get-tuple-element.13.own_ref, f32[8,256]{1,0:T(8,128)} %copy-done.5, f32[8,256]{1,0:T(8,128)} %copy-done.4, s32[64,192]{1,0:T(8,128)} %bitcast.20, ...), custom_call_target="tpu_custom_call" | custom-call | tf_op jit(solution)/shard_map/networks/pallas_call | solution.py:633
  22.9 4.0 %all-to-all-start = ((f32[32,1,1344]{2,1,0:T(1,128)}), f32[32,1,1344]{2,1,0:T(1,128)S(1)}, u32[]{:S(2)}, u32[]{:S(2)}) async-start(f32[32,1,1344]{2,1,0:T(1,128)} %get-tuple-element.15), calls=%async_computation | async-start | bytes 360448 | tf_op jit(solution)/shard_map/all_to_all | solution.py:1220
  26.9 0.7 copy.27.waves_ref
  27.6 0.7 copy.26.kappa_ref
  28.2 4.3 %energies.1.short_hbm = f32[1,192]{1,0:T(1,128)} custom-call(f32[192,1600]{1,0:T(8,128)} %get-tuple-element.16.descriptor_ref, f32[240,1600]{1,0:T(8,128)} %bitcast.17, f32[2,240,240]{2,1,0:T(8,128)} %weight_hidden_ref.1, f32[1,240]{1,0:T(1,128)} %bitcast.22), custom_call_target="tpu_custom_call" | custom-call | flops 442368000 | bytes 1536000 | tf_op jit(solution)/shard_map/energies/pallas_call | solution.py:669
  32.6 3.0 %all-to-all-done.static_ref = f32[32,1,1344]{2,1,0:T(1,128)S(1)} async-done(((f32[32,1,1344]{2,1,0:T(1,128)}), f32[32,1,1344]{2,1,0:T(1,128)S(1)}, u32[]{:S(2)}, u32[]{:S(2)}) %all-to-all-start) | async-done | bytes 172064 | tf_op jit(solution)/shard_map/all_to_all | solution.py:1220
  35.6 0.0 copy-start.3
  35.6 0.7 copy-done.3
  36.2 17.2 %spread_and_solve.1 = (f32[16,4,4,8,128]{4,3,2,1,0:T(8,128)}, f32[8,256,256]{2,1,0:T(8,128)}, f32[8,8,768]{2,1,0:T(8,128)}, f32[8,256,256]{2,1,0:T(8,128)}) custom-call(f32[16,2]{1,0:T(8,128)} %copy.26.kappa_ref, s32[1]{0:T(128)} %bitcast.pair_ref, f32[32,1,1344]{2,1,0:T(1,128)} %copy-done.3, s32[16,2]{1,0:T(8,128)} %copy.27.waves_ref, ...), custom_call_target="tpu_custom_call" | custom-call | tf_op jit(solution)/shard_map/spread_and_solve/pallas_call | solution.py:939
  53.4 3.9 %all-to-all-start.1 = ((f32[16,128,128]{2,1,0:T(8,128)}), f32[16,128,128]{2,1,0:T(8,128)S(1)}, u32[]{:S(2)}, u32[]{:S(2)}) async-start(f32[16,128,128]{2,1,0:T(8,128)} %bitcast.19), calls=%async_computation.1 | async-start | bytes 2097152 | tf_op jit(solution)/shard_map/all_to_all | solution.py:1220
  57.3 13.5 %solve_and_sample.1 = f32[16,17,8,128]{3,2,1,0:T(8,128)} custom-call(f32[16,2]{1,0:T(8,128)} %copy.26.kappa_ref, s32[1]{0:T(128)} %bitcast.pair_ref, f32[8,8,768]{2,1,0:T(8,128)} %get-tuple-element.18.atoms_ref, s32[16,2]{1,0:T(8,128)} %copy.27.waves_ref, f32[1,128]{1,0:T(1,128)} %constant.64.clone.cosine_ref, f32[2,256,256]{2,1,0:T(8,128)} %constant.65.clone.tables_hbm, ...), custom_call_target="tpu_custom_call" | custom-call | flops 6442450944 | bytes 2097152 | tf_op jit(solution)/shard_map/solve_and_sample/pallas_call | solution.py:1074
  70.8 0.0 copy-start
  70.8 0.0 copy-start.1
  70.8 0.0 copy-start.2
  70.8 1.2 %all-to-all-done.1 = f32[16,128,128]{2,1,0:T(8,128)S(1)} async-done(((f32[16,128,128]{2,1,0:T(8,128)}), f32[16,128,128]{2,1,0:T(8,128)S(1)}, u32[]{:S(2)}, u32[]{:S(2)}) %all-to-all-start.1) | async-done | bytes 1048608 | tf_op jit(solution)/shard_map/all_to_all | solution.py:1220
  72.0 20.4 %all_to_all.15 = f32[16,136,128]{2,1,0:T(8,128)S(1)} all-to-all(f32[16,136,128]{2,1,0:T(8,128)} %bitcast.18), channel_id=1, replica_groups={{0,1,4,5,8,9,12,13,16,17,20,21,24,25,28,29},{2,3,6,7,10,11,14,15,18,19,..., dimensions={0} | all-to-all | bytes 2228224 | tf_op jit(solution)/shard_map/all_to_all | solution.py:1220
  92.4 0.0 copy-done
  92.4 0.0 copy-done.1
  92.4 0.0 copy-done.2
  92.4 3.6 %finish.1 = (f32[32,64,256]{2,1,0:T(8,128)}, f32[1,192]{1,0:T(1,128)}) custom-call(f32[16,4,4,8,128]{4,3,2,1,0:T(8,128)S(1)} %bitcast.15, f32[16,17,8,128]{3,2,1,0:T(8,128)S(1)} %bitcast.13, f32[16,17,8,128]{3,2,1,0:T(8,128)S(1)} %bitcast.14, f32[1,192]{1,0:T(1,128)S(1)} %copy-done.1, f32[1,192]{1,0:T(1,128)S(1)} %copy-done.2, f32[256,256]{1,0:T(8,128)S(1)} %copy-done), custom_call_target="tpu_custom_call" | custom-call | tf_op jit(solution)/shard_map/finish/pallas_call | solution.py:1146
  (4 shorter events, 0.0 us)
Async XLA Ops:
  2.0 4.9 %collective-permute-start.1 = (f32[8,256]{1,0:T(8,128)}, f32[8,256]{1,0:T(8,128)S(1)}, u32[]{:S(2)}, u32[]{:S(2)}) collective-permute-start(f32[8,256]{1,0:T(8,128)} %get-tuple-element.14), channel_id=1, source_target_pairs={{4,0},{8,4},{12,8},{16,12},{20,16},{24,20},{28,24},{0,28},{5,1},{9... | collective-permute-start | bytes 24584 | tf_op jit(solution)/shard_map/ppermute | solution.py:1228
  5.4 4.2 %collective-permute-start = (f32[8,256]{1,0:T(8,128)}, f32[8,256]{1,0:T(8,128)S(1)}, u32[]{:S(2)}, u32[]{:S(2)}) collective-permute-start(f32[8,256]{1,0:T(8,128)} %get-tuple-element.14), channel_id=1, source_target_pairs={{0,4},{4,8},{8,12},{12,16},{16,20},{20,24},{24,28},{28,0},{1,5},{5... | collective-permute-start | bytes 24584 | tf_op jit(solution)/shard_map/ppermute | solution.py:1227
  7.0 2.6 %copy-start.4 = (f32[8,256]{1,0:T(8,128)}, f32[8,256]{1,0:T(8,128)S(1)}, u32[]{:S(2)}) copy-start(f32[8,256]{1,0:T(8,128)S(1)} %collective-permute-done.1.upper_ref) | copy-start | bytes 24580
  9.6 0.6 copy-start.5
  22.9 12.7 %all-to-all-start = ((f32[32,1,1344]{2,1,0:T(1,128)}), f32[32,1,1344]{2,1,0:T(1,128)S(1)}, u32[]{:S(2)}, u32[]{:S(2)}) async-start(f32[32,1,1344]{2,1,0:T(1,128)} %get-tuple-element.15), calls=%async_computation | async-start | bytes 360448 | tf_op jit(solution)/shard_map/all_to_all | solution.py:1220
  35.6 0.7 copy-start.3
  53.4 18.6 %all-to-all-start.1 = ((f32[16,128,128]{2,1,0:T(8,128)}), f32[16,128,128]{2,1,0:T(8,128)S(1)}, u32[]{:S(2)}, u32[]{:S(2)}) async-start(f32[16,128,128]{2,1,0:T(8,128)} %bitcast.19), calls=%async_computation.1 | async-start | bytes 2097152 | tf_op jit(solution)/shard_map/all_to_all | solution.py:1220
  70.8 21.6 %copy-start = (f32[256,256]{1,0:T(8,128)S(1)}, f32[256,256]{1,0:T(8,128)}, u32[]{:S(2)}) copy-start(f32[256,256]{1,0:T(8,128)} %constant.67.clone.table_ref) | copy-start | bytes 786436
  70.8 21.6 %copy-start.1 = (f32[1,192]{1,0:T(1,128)S(1)}, f32[1,192]{1,0:T(1,128)}, u32[]{:S(2)}) copy-start(f32[1,192]{1,0:T(1,128)} %energies.1.short_hbm) | copy-start | bytes 2308
  70.8 21.6 %copy-start.2 = (f32[1,192]{1,0:T(1,128)S(1)}, f32[1,192]{1,0:T(1,128)}, u32[]{:S(2)}) copy-start(f32[1,192]{1,0:T(1,128)} %get-tuple-element.21.charge_hbm) | copy-start | bytes 2308

commit v13 on v10

--- a/solution.py
+++ b/solution.py
@@ -542,14 +542,6 @@
                     8 * part : 8 * part + 8
                 ]
 
-    def body(step, carry):
-        for part in range(unroll):
-            one_group(pl.multiple_of(step * unroll * group + part * group, group))
-        return carry
-
-    unroll = rows // group
-    lax.fori_loop(0, rows // (unroll * group), body, 0)
-
     chunks = (descriptor_ref.shape[1] + 127) // 128
     last = descriptor_ref.shape[1] - 128 * (chunks - 1)
 
@@ -567,14 +559,12 @@
             else:
                 descriptor_ref[band, 128 * chunk : 128 * chunk + last] = total[:, 0:last]
 
-    bands = 8 if atoms % 64 == 0 else 1
-
-    def describe(step, carry):
-        for part in range(bands):
-            describe_band(pl.multiple_of(step * 8 * bands + 8 * part, 8))
-        return carry
-
-    lax.fori_loop(0, atoms // (8 * bands), describe, 0)
+    for start in range(0, rows + group, group):
+        if start < rows:
+            one_group(start)
+        if start > 0:
+            for band in range(2 * (start - group), 2 * start, 8):
+                describe_band(band)
 
     store = pltpu.make_async_copy(descriptor_ref, descriptor_hbm, semaphores.at[2])
     store.start()

time: 96.3 us -> 93.8 us (0.974)
  Pallas kernels: 52.3 us -> 49.9 us
    pallas_call x1, Pallas kernels: 12.5 us -> 10 us  [networks(): pl.pallas_call(functools.partial(network_kernel, ghosts), grid=(1,), out_...]
where the time goes in v13:
time: 93.8 us; the launch traced here: 93.4 us
  Pallas kernels  49.9 us (53%)
  blocking collectives  20.4 us (22%)
  starting transfers between devices  11.2 us (12%)
  waiting for transfers between devices  8.33 us (9%)
  local copies, waits for them, and re-layouts  2.63 us (3%)
    all_to_all x1, blocking collectives, exchange(): lax.all_to_all(values, axes, split_axis=0, concat_axis=0, tiled=True, axi...  20.4 us
    pallas_call x1, Pallas kernels, spread_and_solve(): pl.pallas_call(functools.partial(spread_kernel, block_x, block_y, window)...  17.1 us
    pallas_call x1, Pallas kernels, solve_and_sample(): pl.pallas_call(functools.partial(sample_kernel, block_x, block_y, window)...  13.5 us
    pallas_call x1, Pallas kernels, networks(): pl.pallas_call(functools.partial(network_kernel, ghosts), grid=(1,), out_...  10 us
    all_to_all x2, starting transfers between devices, exchange(): lax.all_to_all(values, axes, split_axis=0, concat_axis=0, tiled=True, axi...  7.86 us
    pallas_call x1, Pallas kernels, energies(): pl.pallas_call(energy_kernel, grid=(1,), out_shape=result, in_specs=whole...  4.33 us
    all_to_all x2, waiting for transfers between devices, exchange(): lax.all_to_all(values, axes, split_axis=0, concat_axis=0, tiled=True, axi...  4.17 us
    pallas_call x1, Pallas kernels, finish(): pl.pallas_call(functools.partial(finish_kernel, block_y), grid=(groups,),...  3.56 us
  transfers between devices with their start and end apart: 4, of which 4 were waited for; matrix products, arithmetic and copies ran while one was open for 1% of the time, Pallas kernels for 19%

profile of v13, /device:TPU:0, one launch (start us, length us, event | category | flops | bytes accessed | tf_op | source)
XLA Modules:
  0.0 93.4 jit_solution(8855883516079186115)
XLA Ops:
  0.6 1.4 %collect_atoms.1 = (f32[8,256]{1,0:T(8,128)}, f32[8,256]{1,0:T(8,128)}) custom-call(f32[3,1,192]{2,1,0:T(1,128)} %positions_ref.1, s32[1,192]{1,0:T(1,128)} %types_ref.3, s32[1,192]{1,0:T(1,128)} %count_ref.1, s32[1,192]{1,0:T(1,128)} %send_ref.1), custom_call_target="tpu_custom_call" | custom-call | tf_op jit(solution)/shard_map/collect_atoms/pallas_call | solution.py:349
  2.0 3.3 %collective-permute-start.1 = (f32[8,256]{1,0:T(8,128)}, f32[8,256]{1,0:T(8,128)S(1)}, u32[]{:S(2)}, u32[]{:S(2)}) collective-permute-start(f32[8,256]{1,0:T(8,128)} %get-tuple-element.14), channel_id=1, source_target_pairs={{4,0},{8,4},{12,8},{16,12},{20,16},{24,20},{28,24},{0,28},{5,1},{9... | collective-permute-start | bytes 24584 | tf_op jit(solution)/shard_map/ppermute | solution.py:1226
  5.4 0.0 collective-permute-start
  5.4 1.6 %collective-permute-done.1.upper_ref = f32[8,256]{1,0:T(8,128)S(1)} collective-permute-done((f32[8,256]{1,0:T(8,128)}, f32[8,256]{1,0:T(8,128)S(1)}, u32[]{:S(2)}, u32[]{:S(2)}) %collective-permute-start.1) | collective-permute-done | bytes 8224 | tf_op jit(solution)/shard_map/ppermute | solution.py:1226
  7.0 0.0 copy-start.4
  7.0 2.6 %collective-permute-done.lower_ref = f32[8,256]{1,0:T(8,128)S(1)} collective-permute-done((f32[8,256]{1,0:T(8,128)}, f32[8,256]{1,0:T(8,128)S(1)}, u32[]{:S(2)}, u32[]{:S(2)}) %collective-permute-start) | collective-permute-done | bytes 8224 | tf_op jit(solution)/shard_map/ppermute | solution.py:1225
  9.6 0.0 copy-start.5
  9.6 0.0 copy-done.4
  9.6 0.6 copy-done.5
  10.2 10.0 %networks.1 = (f32[192,1600]{1,0:T(8,128)}, f32[1,192]{1,0:T(1,128)}, f32[32,1,1344]{2,1,0:T(1,128)}) custom-call(s32[1]{0:T(128)} %bitcast.1.base_ref, f32[2]{0:T(128)} %charges_ref.1, f32[8,256]{1,0:T(8,128)} %get-tuple-element.13.own_ref, f32[8,256]{1,0:T(8,128)} %copy-done.5, f32[8,256]{1,0:T(8,128)} %copy-done.4, s32[64,192]{1,0:T(8,128)} %bitcast.20, ...), custom_call_target="tpu_custom_call" | custom-call | tf_op jit(solution)/shard_map/networks/pallas_call | solution.py:631
  20.2 4.0 %all-to-all-start = ((f32[32,1,1344]{2,1,0:T(1,128)}), f32[32,1,1344]{2,1,0:T(1,128)S(1)}, u32[]{:S(2)}, u32[]{:S(2)}) async-start(f32[32,1,1344]{2,1,0:T(1,128)} %get-tuple-element.15), calls=%async_computation | async-start | bytes 360448 | tf_op jit(solution)/shard_map/all_to_all | solution.py:1218
  24.2 0.7 copy.27.waves_ref
  24.9 0.7 copy.26.kappa_ref
  25.6 4.3 %energies.1.short_hbm = f32[1,192]{1,0:T(1,128)} custom-call(f32[192,1600]{1,0:T(8,128)} %get-tuple-element.16.descriptor_ref, f32[240,1600]{1,0:T(8,128)} %bitcast.17, f32[2,240,240]{2,1,0:T(8,128)} %weight_hidden_ref.1, f32[1,240]{1,0:T(1,128)} %bitcast.22), custom_call_target="tpu_custom_call" | custom-call | flops 442368000 | bytes 1536000 | tf_op jit(solution)/shard_map/energies/pallas_call | solution.py:667
  29.9 3.0 %all-to-all-done.static_ref = f32[32,1,1344]{2,1,0:T(1,128)S(1)} async-done(((f32[32,1,1344]{2,1,0:T(1,128)}), f32[32,1,1344]{2,1,0:T(1,128)S(1)}, u32[]{:S(2)}, u32[]{:S(2)}) %all-to-all-start) | async-done | bytes 172064 | tf_op jit(solution)/shard_map/all_to_all | solution.py:1218
  32.9 0.0 copy-start.3
  32.9 0.7 copy-done.3
  33.6 17.1 %spread_and_solve.1 = (f32[16,4,4,8,128]{4,3,2,1,0:T(8,128)}, f32[8,256,256]{2,1,0:T(8,128)}, f32[8,8,768]{2,1,0:T(8,128)}, f32[8,256,256]{2,1,0:T(8,128)}) custom-call(f32[16,2]{1,0:T(8,128)} %copy.26.kappa_ref, s32[1]{0:T(128)} %bitcast.pair_ref, f32[32,1,1344]{2,1,0:T(1,128)} %copy-done.3, s32[16,2]{1,0:T(8,128)} %copy.27.waves_ref, ...), custom_call_target="tpu_custom_call" | custom-call | tf_op jit(solution)/shard_map/spread_and_solve/pallas_call | solution.py:937
  50.7 3.9 %all-to-all-start.1 = ((f32[16,128,128]{2,1,0:T(8,128)}), f32[16,128,128]{2,1,0:T(8,128)S(1)}, u32[]{:S(2)}, u32[]{:S(2)}) async-start(f32[16,128,128]{2,1,0:T(8,128)} %bitcast.19), calls=%async_computation.1 | async-start | bytes 2097152 | tf_op jit(solution)/shard_map/all_to_all | solution.py:1218
  54.5 13.5 %solve_and_sample.1 = f32[16,17,8,128]{3,2,1,0:T(8,128)} custom-call(f32[16,2]{1,0:T(8,128)} %copy.26.kappa_ref, s32[1]{0:T(128)} %bitcast.pair_ref, f32[8,8,768]{2,1,0:T(8,128)} %get-tuple-element.18.atoms_ref, s32[16,2]{1,0:T(8,128)} %copy.27.waves_ref, f32[1,128]{1,0:T(1,128)} %constant.64.clone.cosine_ref, f32[2,256,256]{2,1,0:T(8,128)} %constant.65.clone.tables_hbm, ...), custom_call_target="tpu_custom_call" | custom-call | flops 6442450944 | bytes 2097152 | tf_op jit(solution)/shard_map/solve_and_sample/pallas_call | solution.py:1072
  68.0 0.0 copy-start
  68.0 0.0 copy-start.1
  68.1 0.0 copy-start.2
  68.1 1.2 %all-to-all-done.1 = f32[16,128,128]{2,1,0:T(8,128)S(1)} async-done(((f32[16,128,128]{2,1,0:T(8,128)}), f32[16,128,128]{2,1,0:T(8,128)S(1)}, u32[]{:S(2)}, u32[]{:S(2)}) %all-to-all-start.1) | async-done | bytes 1048608 | tf_op jit(solution)/shard_map/all_to_all | solution.py:1218
  69.2 20.4 %all_to_all.15 = f32[16,136,128]{2,1,0:T(8,128)S(1)} all-to-all(f32[16,136,128]{2,1,0:T(8,128)} %bitcast.18), channel_id=1, replica_groups={{0,1,4,5,8,9,12,13,16,17,20,21,24,25,28,29},{2,3,6,7,10,11,14,15,18,19,..., dimensions={0} | all-to-all | bytes 2228224 | tf_op jit(solution)/shard_map/all_to_all | solution.py:1218
  89.6 0.0 copy-done
  89.6 0.0 copy-done.1
  89.6 0.0 copy-done.2
  89.6 3.6 %finish.1 = (f32[32,64,256]{2,1,0:T(8,128)}, f32[1,192]{1,0:T(1,128)}) custom-call(f32[16,4,4,8,128]{4,3,2,1,0:T(8,128)S(1)} %bitcast.15, f32[16,17,8,128]{3,2,1,0:T(8,128)S(1)} %bitcast.13, f32[16,17,8,128]{3,2,1,0:T(8,128)S(1)} %bitcast.14, f32[1,192]{1,0:T(1,128)S(1)} %copy-done.1, f32[1,192]{1,0:T(1,128)S(1)} %copy-done.2, f32[256,256]{1,0:T(8,128)S(1)} %copy-done), custom_call_target="tpu_custom_call" | custom-call | tf_op jit(solution)/shard_map/finish/pallas_call | solution.py:1144
  (4 shorter events, 0.0 us)
Async XLA Ops:
  2.0 4.9 %collective-permute-start.1 = (f32[8,256]{1,0:T(8,128)}, f32[8,256]{1,0:T(8,128)S(1)}, u32[]{:S(2)}, u32[]{:S(2)}) collective-permute-start(f32[8,256]{1,0:T(8,128)} %get-tuple-element.14), channel_id=1, source_target_pairs={{4,0},{8,4},{12,8},{16,12},{20,16},{24,20},{28,24},{0,28},{5,1},{9... | collective-permute-start | bytes 24584 | tf_op jit(solution)/shard_map/ppermute | solution.py:1226
  5.4 4.2 %collective-permute-start = (f32[8,256]{1,0:T(8,128)}, f32[8,256]{1,0:T(8,128)S(1)}, u32[]{:S(2)}, u32[]{:S(2)}) collective-permute-start(f32[8,256]{1,0:T(8,128)} %get-tuple-element.14), channel_id=1, source_target_pairs={{0,4},{4,8},{8,12},{12,16},{16,20},{20,24},{24,28},{28,0},{1,5},{5... | collective-permute-start | bytes 24584 | tf_op jit(solution)/shard_map/ppermute | solution.py:1225
  7.0 2.6 %copy-start.4 = (f32[8,256]{1,0:T(8,128)}, f32[8,256]{1,0:T(8,128)S(1)}, u32[]{:S(2)}) copy-start(f32[8,256]{1,0:T(8,128)S(1)} %collective-permute-done.1.upper_ref) | copy-start | bytes 24580
  9.6 0.6 copy-start.5
  20.2 12.7 %all-to-all-start = ((f32[32,1,1344]{2,1,0:T(1,128)}), f32[32,1,1344]{2,1,0:T(1,128)S(1)}, u32[]{:S(2)}, u32[]{:S(2)}) async-start(f32[32,1,1344]{2,1,0:T(1,128)} %get-tuple-element.15), calls=%async_computation | async-start | bytes 360448 | tf_op jit(solution)/shard_map/all_to_all | solution.py:1218
  32.9 0.7 copy-start.3
  50.7 18.6 %all-to-all-start.1 = ((f32[16,128,128]{2,1,0:T(8,128)}), f32[16,128,128]{2,1,0:T(8,128)S(1)}, u32[]{:S(2)}, u32[]{:S(2)}) async-start(f32[16,128,128]{2,1,0:T(8,128)} %bitcast.19), calls=%async_computation.1 | async-start | bytes 2097152 | tf_op jit(solution)/shard_map/all_to_all | solution.py:1218
  68.0 21.6 %copy-start = (f32[256,256]{1,0:T(8,128)S(1)}, f32[256,256]{1,0:T(8,128)}, u32[]{:S(2)}) copy-start(f32[256,256]{1,0:T(8,128)} %constant.67.clone.table_ref) | copy-start | bytes 786436
  68.0 21.6 %copy-start.1 = (f32[1,192]{1,0:T(1,128)S(1)}, f32[1,192]{1,0:T(1,128)}, u32[]{:S(2)}) copy-start(f32[1,192]{1,0:T(1,128)} %energies.1.short_hbm) | copy-start | bytes 2308
  68.1 21.6 %copy-start.2 = (f32[1,192]{1,0:T(1,128)S(1)}, f32[1,192]{1,0:T(1,128)}, u32[]{:S(2)}) copy-start(f32[1,192]{1,0:T(1,128)} %get-tuple-element.21.charge_hbm) | copy-start | bytes 2308

commit v14 on v13

--- a/solution.py
+++ b/solution.py
@@ -872,7 +872,7 @@
                     ]
         for ref in second_refs:
             ref[...] = jnp.zeros_like(ref)
-        for brick in range(bricks):
+        def tables_of(brick):
             fields = atoms_ref[brick]
             table = first_third_split(
                 fields,
@@ -886,6 +886,13 @@
             second = second_factors(
                 fields, 0, block_y, slabs, second_refs[2 * (brick % 2)], second_refs[2 * (brick % 2) + 1]
             )
+            return table, second
+
+        coming = tables_of(0)
+        for brick in range(bricks):
+            table, second = coming
+            if brick + 1 < bricks:
+                coming = tables_of(brick + 1)
             spread = triple(table, second, LANES)
             start = block_x * brick
             extra = window - block_x

time: 93.8 us -> 93.8 us (level)
  no operation moved by 1% of the time
where the time goes in v14:
time: 93.8 us; the launch traced here: 93.4 us
  Pallas kernels  49.9 us (53%)
  blocking collectives  20.4 us (22%)
  starting transfers between devices  11.2 us (12%)
  waiting for transfers between devices  8.33 us (9%)
  local copies, waits for them, and re-layouts  2.63 us (3%)
    all_to_all x1, blocking collectives, exchange(): lax.all_to_all(values, axes, split_axis=0, concat_axis=0, tiled=True, axi...  20.4 us
    pallas_call x1, Pallas kernels, spread_and_solve(): pl.pallas_call(functools.partial(spread_kernel, block_x, block_y, window)...  17.1 us
    pallas_call x1, Pallas kernels, solve_and_sample(): pl.pallas_call(functools.partial(sample_kernel, block_x, block_y, window)...  13.5 us
    pallas_call x1, Pallas kernels, networks(): pl.pallas_call(functools.partial(network_kernel, ghosts), grid=(1,), out_...  10 us
    all_to_all x2, starting transfers between devices, exchange(): lax.all_to_all(values, axes, split_axis=0, concat_axis=0, tiled=True, axi...  7.86 us
    pallas_call x1, Pallas kernels, energies(): pl.pallas_call(energy_kernel, grid=(1,), out_shape=result, in_specs=whole...  4.33 us
    all_to_all x2, waiting for transfers between devices, exchange(): lax.all_to_all(values, axes, split_axis=0, concat_axis=0, tiled=True, axi...  4.17 us
    pallas_call x1, Pallas kernels, finish(): pl.pallas_call(functools.partial(finish_kernel, block_y), grid=(groups,),...  3.56 us
  transfers between devices with their start and end apart: 4, of which 4 were waited for; matrix products, arithmetic and copies ran while one was open for 1% of the time, Pallas kernels for 19%

profile of v14, /device:TPU:0, one launch (start us, length us, event | category | flops | bytes accessed | tf_op | source)
XLA Modules:
  0.0 93.4 jit_solution(8855883516079186115)
XLA Ops:
  0.6 1.4 %collect_atoms.1 = (f32[8,256]{1,0:T(8,128)}, f32[8,256]{1,0:T(8,128)}) custom-call(f32[3,1,192]{2,1,0:T(1,128)} %positions_ref.1, s32[1,192]{1,0:T(1,128)} %types_ref.3, s32[1,192]{1,0:T(1,128)} %count_ref.1, s32[1,192]{1,0:T(1,128)} %send_ref.1), custom_call_target="tpu_custom_call" | custom-call | tf_op jit(solution)/shard_map/collect_atoms/pallas_call | solution.py:349
  2.0 3.3 %collective-permute-start.1 = (f32[8,256]{1,0:T(8,128)}, f32[8,256]{1,0:T(8,128)S(1)}, u32[]{:S(2)}, u32[]{:S(2)}) collective-permute-start(f32[8,256]{1,0:T(8,128)} %get-tuple-element.14), channel_id=1, source_target_pairs={{4,0},{8,4},{12,8},{16,12},{20,16},{24,20},{28,24},{0,28},{5,1},{9... | collective-permute-start | bytes 24584 | tf_op jit(solution)/shard_map/ppermute | solution.py:1233
  5.4 0.0 collective-permute-start
  5.4 1.6 %collective-permute-done.1.upper_ref = f32[8,256]{1,0:T(8,128)S(1)} collective-permute-done((f32[8,256]{1,0:T(8,128)}, f32[8,256]{1,0:T(8,128)S(1)}, u32[]{:S(2)}, u32[]{:S(2)}) %collective-permute-start.1) | collective-permute-done | bytes 8224 | tf_op jit(solution)/shard_map/ppermute | solution.py:1233
  7.0 0.0 copy-start.4
  7.0 2.6 %collective-permute-done.lower_ref = f32[8,256]{1,0:T(8,128)S(1)} collective-permute-done((f32[8,256]{1,0:T(8,128)}, f32[8,256]{1,0:T(8,128)S(1)}, u32[]{:S(2)}, u32[]{:S(2)}) %collective-permute-start) | collective-permute-done | bytes 8224 | tf_op jit(solution)/shard_map/ppermute | solution.py:1232
  9.6 0.0 copy-start.5
  9.6 0.0 copy-done.4
  9.6 0.6 copy-done.5
  10.2 10.0 %networks.1 = (f32[192,1600]{1,0:T(8,128)}, f32[1,192]{1,0:T(1,128)}, f32[32,1,1344]{2,1,0:T(1,128)}) custom-call(s32[1]{0:T(128)} %bitcast.1.base_ref, f32[2]{0:T(128)} %charges_ref.1, f32[8,256]{1,0:T(8,128)} %get-tuple-element.13.own_ref, f32[8,256]{1,0:T(8,128)} %copy-done.5, f32[8,256]{1,0:T(8,128)} %copy-done.4, s32[64,192]{1,0:T(8,128)} %bitcast.20, ...), custom_call_target="tpu_custom_call" | custom-call | tf_op jit(solution)/shard_map/networks/pallas_call | solution.py:631
  20.2 4.0 %all-to-all-start = ((f32[32,1,1344]{2,1,0:T(1,128)}), f32[32,1,1344]{2,1,0:T(1,128)S(1)}, u32[]{:S(2)}, u32[]{:S(2)}) async-start(f32[32,1,1344]{2,1,0:T(1,128)} %get-tuple-element.15), calls=%async_computation | async-start | bytes 360448 | tf_op jit(solution)/shard_map/all_to_all | solution.py:1225
  24.2 0.7 copy.27.waves_ref
  24.9 0.7 copy.26.kappa_ref
  25.6 4.3 %energies.1.short_hbm = f32[1,192]{1,0:T(1,128)} custom-call(f32[192,1600]{1,0:T(8,128)} %get-tuple-element.16.descriptor_ref, f32[240,1600]{1,0:T(8,128)} %bitcast.17, f32[2,240,240]{2,1,0:T(8,128)} %weight_hidden_ref.1, f32[1,240]{1,0:T(1,128)} %bitcast.22), custom_call_target="tpu_custom_call" | custom-call | flops 442368000 | bytes 1536000 | tf_op jit(solution)/shard_map/energies/pallas_call | solution.py:667
  29.9 3.0 %all-to-all-done.static_ref = f32[32,1,1344]{2,1,0:T(1,128)S(1)} async-done(((f32[32,1,1344]{2,1,0:T(1,128)}), f32[32,1,1344]{2,1,0:T(1,128)S(1)}, u32[]{:S(2)}, u32[]{:S(2)}) %all-to-all-start) | async-done | bytes 172064 | tf_op jit(solution)/shard_map/all_to_all | solution.py:1225
  32.9 0.0 copy-start.3
  32.9 0.7 copy-done.3
  33.6 17.1 %spread_and_solve.1 = (f32[16,4,4,8,128]{4,3,2,1,0:T(8,128)}, f32[8,256,256]{2,1,0:T(8,128)}, f32[8,8,768]{2,1,0:T(8,128)}, f32[8,256,256]{2,1,0:T(8,128)}) custom-call(f32[16,2]{1,0:T(8,128)} %copy.26.kappa_ref, s32[1]{0:T(128)} %bitcast.pair_ref, f32[32,1,1344]{2,1,0:T(1,128)} %copy-done.3, s32[16,2]{1,0:T(8,128)} %copy.27.waves_ref, ...), custom_call_target="tpu_custom_call" | custom-call | tf_op jit(solution)/shard_map/spread_and_solve/pallas_call | solution.py:944
  50.7 3.9 %all-to-all-start.1 = ((f32[16,128,128]{2,1,0:T(8,128)}), f32[16,128,128]{2,1,0:T(8,128)S(1)}, u32[]{:S(2)}, u32[]{:S(2)}) async-start(f32[16,128,128]{2,1,0:T(8,128)} %bitcast.19), calls=%async_computation.1 | async-start | bytes 2097152 | tf_op jit(solution)/shard_map/all_to_all | solution.py:1225
  54.5 13.5 %solve_and_sample.1 = f32[16,17,8,128]{3,2,1,0:T(8,128)} custom-call(f32[16,2]{1,0:T(8,128)} %copy.26.kappa_ref, s32[1]{0:T(128)} %bitcast.pair_ref, f32[8,8,768]{2,1,0:T(8,128)} %get-tuple-element.18.atoms_ref, s32[16,2]{1,0:T(8,128)} %copy.27.waves_ref, f32[1,128]{1,0:T(1,128)} %constant.64.clone.cosine_ref, f32[2,256,256]{2,1,0:T(8,128)} %constant.65.clone.tables_hbm, ...), custom_call_target="tpu_custom_call" | custom-call | flops 6442450944 | bytes 2097152 | tf_op jit(solution)/shard_map/solve_and_sample/pallas_call | solution.py:1079
  68.0 0.0 copy-start
  68.0 0.0 copy-start.1
  68.1 0.0 copy-start.2
  68.1 1.2 %all-to-all-done.1 = f32[16,128,128]{2,1,0:T(8,128)S(1)} async-done(((f32[16,128,128]{2,1,0:T(8,128)}), f32[16,128,128]{2,1,0:T(8,128)S(1)}, u32[]{:S(2)}, u32[]{:S(2)}) %all-to-all-start.1) | async-done | bytes 1048608 | tf_op jit(solution)/shard_map/all_to_all | solution.py:1225
  69.2 20.4 %all_to_all.15 = f32[16,136,128]{2,1,0:T(8,128)S(1)} all-to-all(f32[16,136,128]{2,1,0:T(8,128)} %bitcast.18), channel_id=1, replica_groups={{0,1,4,5,8,9,12,13,16,17,20,21,24,25,28,29},{2,3,6,7,10,11,14,15,18,19,..., dimensions={0} | all-to-all | bytes 2228224 | tf_op jit(solution)/shard_map/all_to_all | solution.py:1225
  89.6 0.0 copy-done
  89.6 0.0 copy-done.1
  89.6 0.0 copy-done.2
  89.6 3.6 %finish.1 = (f32[32,64,256]{2,1,0:T(8,128)}, f32[1,192]{1,0:T(1,128)}) custom-call(f32[16,4,4,8,128]{4,3,2,1,0:T(8,128)S(1)} %bitcast.15, f32[16,17,8,128]{3,2,1,0:T(8,128)S(1)} %bitcast.13, f32[16,17,8,128]{3,2,1,0:T(8,128)S(1)} %bitcast.14, f32[1,192]{1,0:T(1,128)S(1)} %copy-done.1, f32[1,192]{1,0:T(1,128)S(1)} %copy-done.2, f32[256,256]{1,0:T(8,128)S(1)} %copy-done), custom_call_target="tpu_custom_call" | custom-call | tf_op jit(solution)/shard_map/finish/pallas_call | solution.py:1151
  (4 shorter events, 0.0 us)
Async XLA Ops:
  2.0 4.9 %collective-permute-start.1 = (f32[8,256]{1,0:T(8,128)}, f32[8,256]{1,0:T(8,128)S(1)}, u32[]{:S(2)}, u32[]{:S(2)}) collective-permute-start(f32[8,256]{1,0:T(8,128)} %get-tuple-element.14), channel_id=1, source_target_pairs={{4,0},{8,4},{12,8},{16,12},{20,16},{24,20},{28,24},{0,28},{5,1},{9... | collective-permute-start | bytes 24584 | tf_op jit(solution)/shard_map/ppermute | solution.py:1233
  5.4 4.2 %collective-permute-start = (f32[8,256]{1,0:T(8,128)}, f32[8,256]{1,0:T(8,128)S(1)}, u32[]{:S(2)}, u32[]{:S(2)}) collective-permute-start(f32[8,256]{1,0:T(8,128)} %get-tuple-element.14), channel_id=1, source_target_pairs={{0,4},{4,8},{8,12},{12,16},{16,20},{20,24},{24,28},{28,0},{1,5},{5... | collective-permute-start | bytes 24584 | tf_op jit(solution)/shard_map/ppermute | solution.py:1232
  7.0 2.6 %copy-start.4 = (f32[8,256]{1,0:T(8,128)}, f32[8,256]{1,0:T(8,128)S(1)}, u32[]{:S(2)}) copy-start(f32[8,256]{1,0:T(8,128)S(1)} %collective-permute-done.1.upper_ref) | copy-start | bytes 24580
  9.6 0.6 copy-start.5
  20.2 12.7 %all-to-all-start = ((f32[32,1,1344]{2,1,0:T(1,128)}), f32[32,1,1344]{2,1,0:T(1,128)S(1)}, u32[]{:S(2)}, u32[]{:S(2)}) async-start(f32[32,1,1344]{2,1,0:T(1,128)} %get-tuple-element.15), calls=%async_computation | async-start | bytes 360448 | tf_op jit(solution)/shard_map/all_to_all | solution.py:1225
  32.9 0.7 copy-start.3
  50.7 18.6 %all-to-all-start.1 = ((f32[16,128,128]{2,1,0:T(8,128)}), f32[16,128,128]{2,1,0:T(8,128)S(1)}, u32[]{:S(2)}, u32[]{:S(2)}) async-start(f32[16,128,128]{2,1,0:T(8,128)} %bitcast.19), calls=%async_computation.1 | async-start | bytes 2097152 | tf_op jit(solution)/shard_map/all_to_all | solution.py:1225
  68.0 21.6 %copy-start = (f32[256,256]{1,0:T(8,128)S(1)}, f32[256,256]{1,0:T(8,128)}, u32[]{:S(2)}) copy-start(f32[256,256]{1,0:T(8,128)} %constant.67.clone.table_ref) | copy-start | bytes 786436
  68.0 21.6 %copy-start.1 = (f32[1,192]{1,0:T(1,128)S(1)}, f32[1,192]{1,0:T(1,128)}, u32[]{:S(2)}) copy-start(f32[1,192]{1,0:T(1,128)} %energies.1.short_hbm) | copy-start | bytes 2308
  68.1 21.6 %copy-start.2 = (f32[1,192]{1,0:T(1,128)S(1)}, f32[1,192]{1,0:T(1,128)}, u32[]{:S(2)}) copy-start(f32[1,192]{1,0:T(1,128)} %get-tuple-element.21.charge_hbm) | copy-start | bytes 2308
